TPU v7x, 128 devices: a whole 4x4x4 slice. The times are simulated.
128 devices in a mesh: top: 8 (over x, core), leaf: 16 (over y, z).
Axes of the slice: x: 4, y: 4, z: 4, core: 2. Of those that a mesh axis runs over, the one named last changes fastest.
Arguments:
- points: float32 [3, 1048576], P(None, ('top', 'leaf')), may hold values from 0 to 16, as said below
- charges: float32 [16, 1048576], P(None, ('top', 'leaf')), may hold values from -6 to 6
- near_list: int32 [27, 16384], P(None, ('top', 'leaf')), may hold values from -1 to 16383, as said below
- far_list: int32 [16, 16384], P(None, ('top', 'leaf')), may hold values from 0 to 16383, as said below
- leaf_basis: float32 [64, 1048576], P(None, ('top', 'leaf')), may hold values from -0.75 to 0.75
- transfer: float32 [64, 1048576], P(None, ('top', 'leaf')), may hold values from -0.25 to 0.25
- leaf_skeleton: float32 [3, 1048576], P(None, ('top', 'leaf')), may hold values from 0 to 16, as said below
- device_far: int32 [4, 128], P(None, ('top', 'leaf')), may hold values from 0 to 127, as said below
- branch_transfer: float32 [64, 8192], P(None, ('top', 'leaf')), may hold values from -1.5 to 1.5
- device_skeleton: float32 [3, 8192], replicated, may hold values from 0 to 16, as said below
- branch_skeleton: float32 [3, 512], replicated, may hold values from 0 to 16, as said below
Outputs:
- product: float32 [16, 1048576], P(None, ('top', 'leaf'))
Inputs may be any that keep to these rules, and one draw needn't show every extreme that they name: `near_list`: leaf c (d = c // 128, m = c % 128) has the cell (4 (d // 16) + m // 32, 4 (d % 16) + m // 8 % 4, m % 8) of a grid of cubes of side 0.25; slot 0 of leaf c is c itself, the other used slots name different leaves whose cells touch c's cell (face, edge or corner), a subset of them, in no fixed order, and the unused slots after them hold -1. `far_list`: 16 different leaves whose cells do not touch c's cell, while their parents (blocks of 2 x 2 x 2 cells aligned to even cell indices) touch or equal c's parent. `device_far`: 4 different device clusters of d's branch, each with an index 2 or more away from d's. The points of each leaf lie in its cell. `leaf_skeleton`: the skeleton points of each leaf lie in its cell. `device_skeleton`: the skeleton points of device cluster d lie in the box of its leaves' cells. `branch_skeleton`: the skeleton points of branch b lie in the box of its leaves' cells.
All inputs are finite; a program needn't handle non-finite values.
Results may differ from a plain program's by a relative error of at most 0.0003.
Values sent between devices are 32-bit elements; how exact they have to be, the bound alone decides.
No kernel may reach another device: no remote copies, remote signals or barrier semaphores. Data moves between devices by JAX's collectives and lax.ppermute only.
A program may use at most 128 MiB of HBM per device.

v0:
```python
import jax
import jax.numpy as jnp
from jax import lax
from jax.sharding import PartitionSpec as P

LEAF = 64
RANK = 64
BX = 4
BY = 4
BZ = 8


EXACT = lax.Precision.HIGHEST
KERNEL_SCALE = 3.4641016151377544
SIGNAL = 0.0625
NUGGET = 0.25


def with_halo(array, sides, width):
    for axis, dim in sides:
        size, length = (lax.axis_size(axis), array.shape[dim])
        up = [(i, (i + 1) % size) for i in range(size - 1)]
        down = [(j, i) for i, j in up]
        last = lax.slice_in_dim(array, length - width, length, axis=dim)
        leading = lax.slice_in_dim(array, 0, width, axis=dim)
        before = lax.ppermute(last, axis, up)
        after = lax.ppermute(leading, axis, down)
        array = jnp.concatenate([before, array, after], axis=dim)
    return array


def kernel_tiles(targets, sources):
    differ = targets[..., :, None] - sources[..., None, :]
    distance = jnp.sqrt(jnp.sum(differ * differ, axis=0))
    scaled = KERNEL_SCALE * distance
    return SIGNAL * (1.0 + scaled) * jnp.exp(-scaled)


def window_ids(leaf_ids, width, top_index, leaf_index, group_size):
    usable = leaf_ids >= 0
    clipped = jnp.maximum(leaf_ids, 0)
    device_of = clipped // (BX * BY * BZ)
    local_id = clipped % (BX * BY * BZ)
    window_x = (device_of // group_size - top_index) * BX + local_id // (BY * BZ) + width
    window_y = (device_of % group_size - leaf_index) * BY + local_id // BZ % BY + width
    position = (window_x * (BY + 2 * width) + window_y) * BZ + local_id % BZ
    return (jnp.where(usable, position, 0), usable.astype(jnp.float32))


def near_block(target_pts, window, positions, usable):
    source = jnp.take(window, positions, axis=1)
    entries = kernel_tiles(target_pts[:, None], source[:3])
    return jnp.einsum("sbij,sb,rsbj->rbi", entries, usable, source[3:], precision=EXACT)


def far_block(target_skel, window, positions):
    source = jnp.take(window, positions, axis=1)
    entries = kernel_tiles(target_skel[:, None], source[:3])
    return jnp.einsum("fbij,rfbj->rbi", entries, source[3:], precision=EXACT)


def body(
    points,
    charges,
    near_list,
    far_list,
    leaf_basis,
    transfer,
    leaf_skeleton,
    device_far,
    branch_transfer,
    device_skeleton,
    branch_skeleton,
):
    rhs_count, point_count = charges.shape
    leaves_here = point_count // LEAF
    top_index = lax.axis_index("top")
    leaf_index = lax.axis_index("leaf")
    device = lax.axis_index(("top", "leaf"))
    group_size = lax.axis_size("leaf")
    row_count = 3 + rhs_count
    coords = points.reshape(3, leaves_here, LEAF)
    values = charges.reshape(rhs_count, leaves_here, LEAF)
    joined = jnp.concatenate([coords, values], axis=0)
    near_window = with_halo(
        joined.reshape(row_count, BX, BY, BZ * LEAF), (("top", 1), ("leaf", 2)), 1
    )
    near_window = near_window.reshape(row_count, -1, LEAF)
    basis_rows = leaf_basis.reshape(RANK, leaves_here, LEAF)
    coefficients = jnp.einsum("alk,rlk->rla", basis_rows, values, precision=EXACT)
    skeletons = leaf_skeleton.reshape(3, leaves_here, RANK)
    joined_coef = jnp.concatenate([skeletons, coefficients], axis=0)
    far_window = with_halo(
        joined_coef.reshape(row_count, BX, BY, BZ * RANK), (("top", 1), ("leaf", 2)), 3
    )
    far_window = far_window.reshape(row_count, -1, RANK)
    block_size = min(32, leaves_here)
    count_blocks = leaves_here // block_size

    def blocked(stacked):
        return jnp.moveaxis(
            stacked.reshape(stacked.shape[0], count_blocks, block_size, *stacked.shape[2:]), 1, 0
        )

    near_pos, near_use = window_ids(near_list, 1, top_index, leaf_index, group_size)

    def near_step(inputs):
        return near_block(inputs[0], near_window, inputs[1], inputs[2])

    near_out = lax.map(near_step, (blocked(coords), blocked(near_pos), blocked(near_use)))
    near_out = jnp.moveaxis(near_out, 0, 1).reshape(rhs_count, leaves_here, LEAF)
    transfers = transfer.reshape(RANK, leaves_here, RANK)
    device_coef = jnp.einsum("alb,rlb->ra", transfers, coefficients, precision=EXACT)
    projected = jnp.einsum("ab,rb->ra", branch_transfer, device_coef, precision=EXACT)
    partners = device_far[:, 0]
    every_coef, every_proj = (
        lax.all_gather(device_coef[None], ("top", "leaf"), axis=0, tiled=True),
        lax.all_gather(projected[None], ("top", "leaf"), axis=0, tiled=True),
    )
    partner_coef = jnp.take(every_coef, partners, axis=0)
    every_branch = jnp.sum(every_proj.reshape(-1, group_size, rhs_count, RANK), axis=1)
    far_pos, far_use = window_ids(far_list, 3, top_index, leaf_index, group_size)

    def far_step(inputs):
        return far_block(inputs[0], far_window, inputs[1])

    far_out = lax.map(far_step, (blocked(skeletons), blocked(far_pos)))
    far_out = jnp.moveaxis(far_out, 0, 1).reshape(rhs_count, leaves_here, RANK)
    device_skel = device_skeleton.reshape(3, -1, RANK)
    own_skel = jnp.take(device_skel, device, axis=1)
    partner_skel = jnp.take(device_skel, partners, axis=1)
    entries = kernel_tiles(own_skel[:, None], partner_skel)
    coupled = jnp.einsum("fij,frj->ri", entries, partner_coef, precision=EXACT)
    branch_skel = branch_skeleton.reshape(3, -1, RANK)
    branch_total = branch_skel.shape[1]
    own_branch = jnp.take(branch_skel, top_index, axis=1)
    couplings = kernel_tiles(own_branch[:, None], branch_skel)
    distant = (jnp.abs(jnp.arange(branch_total, dtype=jnp.int32) - top_index) >= 2).astype(
        jnp.float32
    )
    branch_field = jnp.einsum("cij,c,crj->ri", couplings, distant, every_branch, precision=EXACT)
    coupled = coupled + jnp.einsum("ab,ra->rb", branch_transfer, branch_field, precision=EXACT)
    leaf_field = far_out + jnp.einsum("alb,ra->rlb", transfers, coupled, precision=EXACT)
    far_result = jnp.einsum("alk,rla->rlk", basis_rows, leaf_field, precision=EXACT)
    summed = near_out + far_result + NUGGET * values
    return summed.reshape(rhs_count, point_count)


def solution(mesh):
    placed = (
        P(None, ("top", "leaf")),
        P(None, ("top", "leaf")),
        P(None, ("top", "leaf")),
        P(None, ("top", "leaf")),
        P(None, ("top", "leaf")),
        P(None, ("top", "leaf")),
        P(None, ("top", "leaf")),
        P(None, ("top", "leaf")),
        P(None, ("top", "leaf")),
        P(),
        P(),
    )
    return jax.shard_map(
        body, mesh=mesh, in_specs=placed, out_specs=P(None, ("top", "leaf")), check_vma=False
    )
```

profile of v0, /device:TPU:107, one launch (start us, length us, event | category | flops | bytes accessed | tf_op | source)
XLA Modules:
  0.0 855.0 jit_solution(1874836322740839436)
XLA Ops:
  16.1 11.6 %fusion.32 = f32[16,128,64]{2,0,1:T(8,128)S(1)} fusion(f32[64,128,64]{2,1,0:T(8,128)} %reshape.150, f32[16,128,64]{2,1,0:T(8,128)S(1)} %reshape.149), kind=kOutput, calls=%fused_computation.49 | convolution fusion | flops 100663296 | bytes 3145728 | tf_op jit(solution)/shard_map/alk,rlk->rla/dot_general | solution.py:90
  45.0 7.4 fusion.47
  52.5 53.0 %all-gather = f32[2048,64]{1,0:T(8,128)S(1)} all-gather(f32[16,64]{1,0:T(8,128)S(1)} %fusion.47), channel_id=2, replica_groups=mesh['top'=8,'leaf'=16] {'top','leaf'}, dimensions={0}, use_global_device_ids=true | all-gather | bytes 528384 | tf_op jit(solution)/shard_map/all_gather | solution.py:117
  106.6 57.0 %all-gather.1 = f32[2048,64]{1,0:T(8,128)S(1)} all-gather(f32[16,64]{1,0:T(8,128)S(1)} %fusion.133), channel_id=3, replica_groups=mesh['top'=8,'leaf'=16] {'top','leaf'}, dimensions={0}, use_global_device_ids=true | all-gather | bytes 528384 | tf_op jit(solution)/shard_map/all_gather | solution.py:118
  207.9 350.6 %while.22 = (s32[]{:T(128)}, f32[4,16,32,64]{3,1,2,0:T(8,128)S(1)}, s32[4,27,32]{2,0,1:T(4,128)}, f32[19,288,64]{2,0,1:T(8,128)}, f32[4,27,32]{1,2,0:T(8,128)S(1)}, /*index=5*/f32[4,3,32,64]{3,2,0,1:T(8,128)}, s32[]{:T(128)}) while((s32[]{:T(128)}, f32[4,16,32,64]{3,1,2,0:T(8,128)S(1)}, s32[4,27,32]{2,0,1:T(4,128)}, f32[19,288,64]{2,0,1:T(8,128)}, ...), condition=%wide.region_2.3_spmd, body=%wide.region_0.2_spmd.sunk | while | flops 727427712 | bytes 55915108 | solution.py:110
  209.2 7.3 gather_fusion
  223.0 32.2 %multiply_reduce_fusion.6 = f32[27,32,64,64]{3,2,1,0:T(8,128)} fusion(f32[3,27,32,64]{3,2,1,0:T(8,128)S(1)} %copy.208, f32[3,32,64]{2,1,0:T(8,128)S(1)} %dynamic-slice_bitcast_fusion.7), kind=kLoop, calls=%fused_computation.4.clone.1 | loop fusion | flops 28311552 | bytes 14843904 | tf_op jit(solution)/shard_map/while/body/eval_jaxpr/reduce_sum | solution.py:34
  255.3 40.5 %fusion.150 = f32[4,16,32,64]{3,1,2,0:T(8,128)S(1)} fusion(f32[4,16,32,64]{3,1,2,0:T(8,128)S(1)} %get-tuple-element.238, s32[]{:T(128)S(6)} %copy.218, f32[19,27,32,64]{3,0,1,2:T(8,128)S(1)} %fusion.149, f32[27,32]{0,1:T(8,128)S(1)} %dynamic-slice_bitcast_fusion.6, f32[27,32,64,64]{3,2,1,0:T(8,128)} %multiply_reduce_fusion.6), kind=kOutput, calls=%fused_computation.13.clone.1 | convolution fusion | flops 698056704 | bytes 21512196 | tf_op jit(solution)/shard_map/while/body/eval_jaxpr/sbij,sb,rsbj->rbi/dot_general | solution.py:53
  296.7 7.3 gather_fusion
  310.5 32.2 %multiply_reduce_fusion.6 = f32[27,32,64,64]{3,2,1,0:T(8,128)} fusion(f32[3,27,32,64]{3,2,1,0:T(8,128)S(1)} %copy.208, f32[3,32,64]{2,1,0:T(8,128)S(1)} %dynamic-slice_bitcast_fusion.7), kind=kLoop, calls=%fused_computation.4.clone.1 | loop fusion | flops 28311552 | bytes 14843904 | tf_op jit(solution)/shard_map/while/body/eval_jaxpr/reduce_sum | solution.py:34
  342.8 40.5 %fusion.150 = f32[4,16,32,64]{3,1,2,0:T(8,128)S(1)} fusion(f32[4,16,32,64]{3,1,2,0:T(8,128)S(1)} %get-tuple-element.238, s32[]{:T(128)S(6)} %copy.218, f32[19,27,32,64]{3,0,1,2:T(8,128)S(1)} %fusion.149, f32[27,32]{0,1:T(8,128)S(1)} %dynamic-slice_bitcast_fusion.6, f32[27,32,64,64]{3,2,1,0:T(8,128)} %multiply_reduce_fusion.6), kind=kOutput, calls=%fused_computation.13.clone.1 | convolution fusion | flops 698056704 | bytes 21512196 | tf_op jit(solution)/shard_map/while/body/eval_jaxpr/sbij,sb,rsbj->rbi/dot_general | solution.py:53
  384.2 7.3 gather_fusion
  398.0 32.2 %multiply_reduce_fusion.6 = f32[27,32,64,64]{3,2,1,0:T(8,128)} fusion(f32[3,27,32,64]{3,2,1,0:T(8,128)S(1)} %copy.208, f32[3,32,64]{2,1,0:T(8,128)S(1)} %dynamic-slice_bitcast_fusion.7), kind=kLoop, calls=%fused_computation.4.clone.1 | loop fusion | flops 28311552 | bytes 14843904 | tf_op jit(solution)/shard_map/while/body/eval_jaxpr/reduce_sum | solution.py:34
  430.3 40.5 %fusion.150 = f32[4,16,32,64]{3,1,2,0:T(8,128)S(1)} fusion(f32[4,16,32,64]{3,1,2,0:T(8,128)S(1)} %get-tuple-element.238, s32[]{:T(128)S(6)} %copy.218, f32[19,27,32,64]{3,0,1,2:T(8,128)S(1)} %fusion.149, f32[27,32]{0,1:T(8,128)S(1)} %dynamic-slice_bitcast_fusion.6, f32[27,32,64,64]{3,2,1,0:T(8,128)} %multiply_reduce_fusion.6), kind=kOutput, calls=%fused_computation.13.clone.1 | convolution fusion | flops 698056704 | bytes 21512196 | tf_op jit(solution)/shard_map/while/body/eval_jaxpr/sbij,sb,rsbj->rbi/dot_general | solution.py:53
  471.7 7.3 gather_fusion
  485.5 32.2 %multiply_reduce_fusion.6 = f32[27,32,64,64]{3,2,1,0:T(8,128)} fusion(f32[3,27,32,64]{3,2,1,0:T(8,128)S(1)} %copy.208, f32[3,32,64]{2,1,0:T(8,128)S(1)} %dynamic-slice_bitcast_fusion.7), kind=kLoop, calls=%fused_computation.4.clone.1 | loop fusion | flops 28311552 | bytes 14843904 | tf_op jit(solution)/shard_map/while/body/eval_jaxpr/reduce_sum | solution.py:34
  517.8 40.5 %fusion.150 = f32[4,16,32,64]{3,1,2,0:T(8,128)S(1)} fusion(f32[4,16,32,64]{3,1,2,0:T(8,128)S(1)} %get-tuple-element.238, s32[]{:T(128)S(6)} %copy.218, f32[19,27,32,64]{3,0,1,2:T(8,128)S(1)} %fusion.149, f32[27,32]{0,1:T(8,128)S(1)} %dynamic-slice_bitcast_fusion.6, f32[27,32,64,64]{3,2,1,0:T(8,128)} %multiply_reduce_fusion.6), kind=kOutput, calls=%fused_computation.13.clone.1 | convolution fusion | flops 698056704 | bytes 21512196 | tf_op jit(solution)/shard_map/while/body/eval_jaxpr/sbij,sb,rsbj->rbi/dot_general | solution.py:53
  567.5 8.4 reshape.151
  575.9 11.6 %copy.121 = f32[19,800,64]{2,0,1:T(8,128)} copy(f32[19,800,64]{2,1,0:T(8,128)} %reshape.151) | data formatting | bytes 7782400 | tf_op jit(solution)/shard_map/while | solution.py:127
  587.6 252.0 %while.23 = (s32[]{:T(128)}, f32[4,16,32,64]{3,1,2,0:T(8,128)S(1)}, s32[4,16,32]{2,0,1:T(4,128)}, f32[19,800,64]{2,0,1:T(8,128)}, f32[4,3,32,64]{3,2,0,1:T(8,128)}, /*index=5*/s32[]{:T(128)}) while((s32[]{:T(128)}, f32[4,16,32,64]{3,1,2,0:T(8,128)S(1)}, s32[4,16,32]{2,0,1:T(4,128)}, f32[19,800,64]{2,0,1:T(8,128)}, f32[4,3,32,64]{3,2,0,1:T(8,128)}, ...), condition=%wide.region_5.6_spmd, body=%wide.region_3.5_spmd.sunk | while | flops 430544384 | bytes 51609716 | solution.py:127
  588.6 7.5 gather_fusion.1
  604.1 20.7 %multiply_reduce_fusion.7 = f32[16,32,64,64]{3,2,1,0:T(8,128)} fusion(f32[3,16,32,64]{3,2,1,0:T(8,128)S(1)} %copy.212, f32[3,32,64]{2,1,0:T(8,128)S(1)} %dynamic-slice_bitcast_fusion.8), kind=kLoop, calls=%fused_computation.23.clone.1 | loop fusion | flops 16777216 | bytes 8806400 | tf_op jit(solution)/shard_map/while/body/eval_jaxpr/reduce_sum | solution.py:34
  624.8 25.9 %fusion.154 = f32[4,16,32,64]{3,1,2,0:T(8,128)S(1)} fusion(f32[4,16,32,64]{3,1,2,0:T(8,128)S(1)} %get-tuple-element.258, s32[]{:T(128)S(6)} %copy.225, f32[19,16,32,64]{3,0,1,2:T(8,128)} %copy-done.2, f32[16,32,64,64]{3,2,1,0:T(8,128)} %multiply_reduce_fusion.7), kind=kOutput, calls=%fused_computation.31.clone.1 | convolution fusion | flops 413138944 | bytes 21233668 | tf_op jit(solution)/shard_map/while/body/eval_jaxpr/fbij,rfbj->rbi/dot_general | solution.py:59
  651.6 7.5 gather_fusion.1
  667.1 20.7 %multiply_reduce_fusion.7 = f32[16,32,64,64]{3,2,1,0:T(8,128)} fusion(f32[3,16,32,64]{3,2,1,0:T(8,128)S(1)} %copy.212, f32[3,32,64]{2,1,0:T(8,128)S(1)} %dynamic-slice_bitcast_fusion.8), kind=kLoop, calls=%fused_computation.23.clone.1 | loop fusion | flops 16777216 | bytes 8806400 | tf_op jit(solution)/shard_map/while/body/eval_jaxpr/reduce_sum | solution.py:34
  687.8 25.9 %fusion.154 = f32[4,16,32,64]{3,1,2,0:T(8,128)S(1)} fusion(f32[4,16,32,64]{3,1,2,0:T(8,128)S(1)} %get-tuple-element.258, s32[]{:T(128)S(6)} %copy.225, f32[19,16,32,64]{3,0,1,2:T(8,128)} %copy-done.2, f32[16,32,64,64]{3,2,1,0:T(8,128)} %multiply_reduce_fusion.7), kind=kOutput, calls=%fused_computation.31.clone.1 | convolution fusion | flops 413138944 | bytes 21233668 | tf_op jit(solution)/shard_map/while/body/eval_jaxpr/fbij,rfbj->rbi/dot_general | solution.py:59
  714.6 7.5 gather_fusion.1
  730.0 20.7 %multiply_reduce_fusion.7 = f32[16,32,64,64]{3,2,1,0:T(8,128)} fusion(f32[3,16,32,64]{3,2,1,0:T(8,128)S(1)} %copy.212, f32[3,32,64]{2,1,0:T(8,128)S(1)} %dynamic-slice_bitcast_fusion.8), kind=kLoop, calls=%fused_computation.23.clone.1 | loop fusion | flops 16777216 | bytes 8806400 | tf_op jit(solution)/shard_map/while/body/eval_jaxpr/reduce_sum | solution.py:34
  750.7 25.9 %fusion.154 = f32[4,16,32,64]{3,1,2,0:T(8,128)S(1)} fusion(f32[4,16,32,64]{3,1,2,0:T(8,128)S(1)} %get-tuple-element.258, s32[]{:T(128)S(6)} %copy.225, f32[19,16,32,64]{3,0,1,2:T(8,128)} %copy-done.2, f32[16,32,64,64]{3,2,1,0:T(8,128)} %multiply_reduce_fusion.7), kind=kOutput, calls=%fused_computation.31.clone.1 | convolution fusion | flops 413138944 | bytes 21233668 | tf_op jit(solution)/shard_map/while/body/eval_jaxpr/fbij,rfbj->rbi/dot_general | solution.py:59
  777.5 7.5 gather_fusion.1
  793.0 20.7 %multiply_reduce_fusion.7 = f32[16,32,64,64]{3,2,1,0:T(8,128)} fusion(f32[3,16,32,64]{3,2,1,0:T(8,128)S(1)} %copy.212, f32[3,32,64]{2,1,0:T(8,128)S(1)} %dynamic-slice_bitcast_fusion.8), kind=kLoop, calls=%fused_computation.23.clone.1 | loop fusion | flops 16777216 | bytes 8806400 | tf_op jit(solution)/shard_map/while/body/eval_jaxpr/reduce_sum | solution.py:34
  813.7 25.9 %fusion.154 = f32[4,16,32,64]{3,1,2,0:T(8,128)S(1)} fusion(f32[4,16,32,64]{3,1,2,0:T(8,128)S(1)} %get-tuple-element.258, s32[]{:T(128)S(6)} %copy.225, f32[19,16,32,64]{3,0,1,2:T(8,128)} %copy-done.2, f32[16,32,64,64]{3,2,1,0:T(8,128)} %multiply_reduce_fusion.7), kind=kOutput, calls=%fused_computation.31.clone.1 | convolution fusion | flops 413138944 | bytes 21233668 | tf_op jit(solution)/shard_map/while/body/eval_jaxpr/fbij,rfbj->rbi/dot_general | solution.py:59
  (197 shorter events, 167.3 us)
Async XLA Ops:
  0.0 106.4 %copy-start = (f32[64,64]{1,0:T(8,128)S(1)}, f32[64,64]{1,0:T(8,128)}, u32[]{:S(2)}) copy-start(f32[64,64]{1,0:T(8,128)} %param.23) | copy-start | bytes 49156
  3.3 168.2 %collective-permute-start.1 = (f32[19,1,4,512]{3,2,1,0:T(4,128)}, f32[19,1,4,512]{3,2,1,0:T(4,128)}, u32[]{:S(2)}, u32[]{:S(2)}) collective-permute-start(f32[19,1,4,512]{3,2,1,0:T(4,128)} %get-tuple-element.161), channel_id=1, source_target_pairs={{16,0},{32,16},{48,32},{64,48},{80,64},{96,80},{112,96},{17,1},{33... | collective-permute-start | bytes 466952 | tf_op jit(solution)/shard_map/ppermute | solution.py:27
  5.9 165.6 %collective-permute-start = (f32[19,1,4,512]{3,2,1,0:T(4,128)}, f32[19,1,4,512]{3,2,1,0:T(4,128)}, u32[]{:S(2)}, u32[]{:S(2)}) collective-permute-start(f32[19,1,4,512]{3,2,1,0:T(4,128)} %get-tuple-element.160), channel_id=1, source_target_pairs={{0,16},{16,32},{32,48},{48,64},{64,80},{80,96},{96,112},{1,17},{17... | collective-permute-start | bytes 466952 | tf_op jit(solution)/shard_map/ppermute | solution.py:26
  10.3 17.4 %copy-start.4 = (f32[16,128,64]{2,1,0:T(8,128)}, f32[16,128,64]{2,1,0:T(8,128)S(1)}, u32[]{:S(2)}) copy-start(f32[16,128,64]{2,1,0:T(8,128)S(1)} %reshape.149) | copy-start | bytes 1572868
  16.1 21.5 %copy-start.14 = (s32[4,1]{0,1:T(1,128)S(1)}, s32[4,1]{0,1:T(1,128)}, u32[]{:S(2)}) copy-start(s32[4,1]{0,1:T(1,128)} %param.22) | copy-start | bytes 52
  16.1 21.6 %copy-start.8 = (s32[27,128]{1,0:T(8,128)S(1)}, s32[27,128]{1,0:T(8,128)}, u32[]{:S(2)}) copy-start(s32[27,128]{1,0:T(8,128)} %param.17) | copy-start | bytes 41476
  16.1 21.7 %copy-start.10 = (s32[16,128]{1,0:T(8,128)S(1)}, s32[16,128]{1,0:T(8,128)}, u32[]{:S(2)}) copy-start(s32[16,128]{1,0:T(8,128)} %param.18) | copy-start | bytes 24580
  30.7 162.8 %copy-start.6 = (f32[19,4,4,512]{3,2,1,0:T(4,128)}, f32[19,4,4,512]{3,2,1,0:T(4,128)S(1)}, u32[]{:S(2)}) copy-start(f32[19,4,4,512]{3,2,1,0:T(4,128)S(1)} %constant_dynamic-update-slice_fusion.2) | copy-start | bytes 1867780
  31.8 161.6 %collective-permute-start.5 = (f32[19,3,4,512]{3,2,1,0:T(4,128)}, f32[19,3,4,512]{3,2,1,0:T(4,128)}, u32[]{:S(2)}, u32[]{:S(2)}) collective-permute-start(f32[19,3,4,512]{3,2,1,0:T(4,128)} %get-tuple-element.159), channel_id=1, source_target_pairs={{16,0},{32,16},{48,32},{64,48},{80,64},{96,80},{112,96},{17,1},{33... | collective-permute-start | bytes 1400840 | tf_op jit(solution)/shard_map/ppermute | solution.py:27
  33.8 159.7 %collective-permute-start.4 = (f32[19,3,4,512]{3,2,1,0:T(4,128)}, f32[19,3,4,512]{3,2,1,0:T(4,128)}, u32[]{:S(2)}, u32[]{:S(2)}) collective-permute-start(f32[19,3,4,512]{3,2,1,0:T(4,128)} %get-tuple-element.158), channel_id=1, source_target_pairs={{0,16},{16,32},{32,48},{48,64},{64,80},{80,96},{96,112},{1,17},{17... | collective-permute-start | bytes 1400840 | tf_op jit(solution)/shard_map/ppermute | solution.py:26
  37.7 2.5 copy-start.13
  39.1 0.6 copy-start.12
  40.3 65.1 %copy-start.11 = (f32[3,512]{1,0:T(4,128)S(1)}, f32[3,512]{1,0:T(4,128)}, u32[]{:S(2)}) copy-start(f32[3,512]{1,0:T(4,128)} %param.25) | copy-start | bytes 18436
  173.0 10.8 %collective-permute-start.3 = (f32[19,6,1,512]{3,2,1,0:T(1,128)S(1)}, f32[19,6,1,512]{3,2,1,0:T(1,128)S(1)}, u32[]{:S(2)}, u32[]{:S(2)}) collective-permute-start(f32[19,6,1,512]{3,2,1,0:T(1,128)S(1)} %get-tuple-element.157), channel_id=1, source_target_pairs={{1,0},{2,1},{3,2},{4,3},{5,4},{6,5},{7,6},{8,7},{9,8},{10,9},{11,1... | collective-permute-start | bytes 700424 | tf_op jit(solution)/shard_map/ppermute | solution.py:27
  175.1 9.6 %collective-permute-start.2 = (f32[19,6,1,512]{3,2,1,0:T(1,128)S(1)}, f32[19,6,1,512]{3,2,1,0:T(1,128)S(1)}, u32[]{:S(2)}, u32[]{:S(2)}) collective-permute-start(f32[19,6,1,512]{3,2,1,0:T(1,128)S(1)} %get-tuple-element.156), channel_id=1, source_target_pairs={{0,1},{1,2},{2,3},{3,4},{4,5},{5,6},{6,7},{7,8},{8,9},{9,10},{10,1... | collective-permute-start | bytes 700424 | tf_op jit(solution)/shard_map/ppermute | solution.py:26
  197.8 360.6 %collective-permute-start.7 = (f32[19,10,3,512]{3,0,2,1:T(8,128)}, f32[19,10,3,512]{3,0,2,1:T(8,128)}, u32[]{:S(2)}, u32[]{:S(2)}) collective-permute-start(f32[19,10,3,512]{3,0,2,1:T(8,128)} %copy.117), channel_id=1, source_target_pairs={{1,0},{2,1},{3,2},{4,3},{5,4},{6,5},{7,6},{8,7},{9,8},{10,9},{11,1... | collective-permute-start | bytes 3502088 | tf_op jit(solution)/shard_map/ppermute | solution.py:27
  201.6 359.1 %collective-permute-start.6 = (f32[19,10,3,512]{3,0,2,1:T(8,128)}, f32[19,10,3,512]{3,0,2,1:T(8,128)}, u32[]{:S(2)}, u32[]{:S(2)}) collective-permute-start(f32[19,10,3,512]{3,0,2,1:T(8,128)} %copy.116), channel_id=1, source_target_pairs={{0,1},{1,2},{2,3},{3,4},{4,5},{5,6},{6,7},{7,8},{8,9},{9,10},{10,1... | collective-permute-start | bytes 3502088 | tf_op jit(solution)/shard_map/ppermute | solution.py:26
  558.4 4.5 copy-start.7
  587.5 252.1 %copy-start.9 = (f32[16,64,1]{1,0,2:T(8,128)S(1)}, f32[16,64,1]{1,0,2:T(8,128)}, u32[]{:S(2)}) copy-start(f32[16,64,1]{1,0,2:T(8,128)} %fusion.50) | copy-start | bytes 12292
  600.1 2.6 copy-start.2
  663.0 2.6 copy-start.2
  726.0 2.6 copy-start.2
  788.9 2.6 copy-start.2
  839.6 7.3 copy-start.3
  839.6 7.3 copy-start.5
  839.6 14.9 %copy-start.1 = (f32[64,64]{1,0:T(8,128)S(1)}, f32[64,64]{1,0:T(8,128)}, u32[]{:S(2)}) copy-start(f32[64,64]{1,0:T(8,128)} %param.23) | copy-start | bytes 49156
where the time goes:
time: 870 us; the launch traced here: 855 us
  matrix products  301 us (35%)
  other arithmetic  260 us (30%)
  local copies, waits for them, and re-layouts  152 us (17%)
  blocking collectives  110 us (13%)
  starting transfers between devices  26.9 us (3%)
    reduce_sum x10, other arithmetic, kernel_tiles(): distance = jnp.sqrt(jnp.sum(differ * differ, axis=0))  213 us
    dot_general x4, matrix products, near_block(): jnp.einsum('sbij,sb,rsbj->rbi', entries, usable, source[3:], precision=EX...  162 us
    dot_general x4, matrix products, far_block(): return jnp.einsum('fbij,rfbj->rbi', entries, source[3:], precision=EXACT)  104 us
    all_gather x1, blocking collectives, body(): lax.all_gather(projected[None], ('top', 'leaf'), axis=0, tiled=True)  57 us
    all_gather x1, blocking collectives, body(): lax.all_gather(device_coef[None], ('top', 'leaf'), axis=0, tiled=True)  53 us
    gather x4, local copies, waits for them, and re-layouts, far_block(): source = jnp.take(window, positions, axis=1)  29.9 us
    gather x4, local copies, waits for them, and re-layouts, near_block(): source = jnp.take(window, positions, axis=1)  29.4 us
    select_n x8, other arithmetic, near_block(): source = jnp.take(window, positions, axis=1)  20.5 us
  transfers between devices with their start and end apart: 8, of which 3 were waited for; matrix products, arithmetic and copies ran while one was open for 48% of the time, Pallas kernels for 0%

commit v1 on v0

v1 whole, which is shorter than its diff:
```python
import functools

import jax
import jax.numpy as jnp
from jax import lax
from jax.experimental import pallas as pl
from jax.experimental.pallas import tpu as pltpu
from jax.sharding import PartitionSpec as P

LEAF = 64
RHS = 16
BX = 4
BY = 4
BZ = 8
COLS = BX * BY
COL = BZ * LEAF
HERE = COLS * BZ
NEAR = 27
FAR = 16
NX = BX + 2
FX = BX + 4
NEAR_NULL = NX * NX * BZ
FAR_ALL = FX * FX * BZ
YFAR, YNEAR = 2 * BX, BX
XFAR, XNEAR = 2 * FX, NX
YCOLS = YFAR + YNEAR
XCOLS = XFAR + XNEAR
ROWS = RHS + 3
UNITS = 16

EXACT = lax.Precision.HIGHEST
KERNEL_SCALE = 3.4641016151377544
SIGNAL = 0.0625
NUGGET = 0.25
BF16 = jnp.bfloat16
F32 = jnp.float32
NT = (((1,), (1,)), ((), ()))
NN = (((1,), (0,)), ((), ()))
VMEM = pl.BlockSpec(memory_space=pltpu.VMEM)
SMEM = pl.BlockSpec(memory_space=pltpu.SMEM)
PARAMS = pltpu.CompilerParams(vmem_limit_bytes=50 * 2**20)


def dot(a, b, dims=NN):
    return lax.dot_general(a, b, dims, preferred_element_type=F32)


def halves(value):
    high = value.astype(BF16)
    return high, (value - high.astype(F32)).astype(BF16)


def low_lanes(rows):
    return lax.broadcasted_iota(jnp.int32, (rows, 128), 1) < LEAF


def column(index):
    return pl.ds(pl.multiple_of(index * COL, COL), COL)


def window_ids(ids, width, span, top, leaf, null):
    wx = ((ids >> 11) - top) * BX + ((ids >> 5) & 3) + width
    wy = (((ids >> 7) & 15) - leaf) * BY + ((ids >> 3) & 3) + width
    place = (wx * span + wy) * BZ + (ids & 7)
    place = jnp.minimum(jnp.maximum(place, 0), span * span * BZ - 1)
    return jnp.where(ids >= 0, place, null)


def first_kernel(
    points, charges, near_list, far_list, basis, transfer, skeleton, branch_transfer,
    coef, device_row, near_ids, far_ids, send_down, send_up,
):
    top, leaf = lax.axis_index("top"), lax.axis_index("leaf")
    listed = near_list[...]
    near_ids[0:NEAR] = window_ids(listed, 1, NX, top, leaf, NEAR_NULL)
    near_ids[NEAR : NEAR + 1] = jnp.full((1, HERE), NEAR_NULL, jnp.int32)
    near_ids[28:29] = jnp.sum((listed >= 0).astype(jnp.int32), axis=0, keepdims=True)
    far_ids[...] = window_ids(far_list[...], 2, FX, top, leaf, 0)

    lane = lax.broadcasted_iota(jnp.int32, (2 * RHS, 4 * LEAF), 1) // LEAF
    half = low_lanes(RHS)
    together = 4

    def coef_step(step, carry):
        places, products = [], []
        for part in range(together):
            place = pl.ds(pl.multiple_of((step * together + part) * 256, 256), 256)
            places.append(place)
            q_high, q_low = halves(charges[:, place])
            q = jnp.concatenate([q_high, q_low], axis=0)
            zero = jnp.zeros_like(q)
            rows = jnp.concatenate([jnp.where(lane == i, q, zero) for i in range(4)], axis=0)
            b_high, b_low = halves(basis[:, place])
            products.append(
                dot(rows, jnp.concatenate([b_high, b_high], axis=0), NT)
                + dot(rows, jnp.concatenate([b_low, b_low], axis=0), NT)
            )
        for place, product in zip(places, products):
            each = [product[32 * i : 32 * i + 16] + product[32 * i + 16 : 32 * i + 32] for i in range(4)]
            coef[:, place] = jnp.concatenate(
                [jnp.where(half, each[0], each[1]), jnp.where(half, each[2], each[3])], axis=1
            )
        return carry

    lax.fori_loop(0, HERE // 4 // together, coef_step, 0)

    def device_step(step, total):
        for part in range(together):
            place = pl.ds(pl.multiple_of((step * together + part) * 256, 256), 256)
            c = jnp.concatenate(halves(coef[:, place]), axis=0)
            t_high, t_low = halves(transfer[:, place])
            total = total + (dot(c, t_high, NT) + dot(c, t_low, NT))
        return total

    total = lax.fori_loop(0, HERE // 4 // together, device_step, jnp.zeros((2 * RHS, LEAF), F32))
    own = total[:RHS] + total[RHS:]
    raised = lax.dot_general(own, branch_transfer[...], NT, precision=EXACT, preferred_element_type=F32)
    device_row[...] = jnp.concatenate([own, raised], axis=1)

    def fill(target, near_y, far_y):
        for x in range(BX):
            for y in range(2):
                to, at = column(x * 2 + y), column(x * BY + far_y + y)
                target[0:RHS, to] = coef[:, at]
                target[RHS:ROWS, to] = skeleton[:, at]
            to, at = column(YFAR + x), column(x * BY + near_y)
            target[0:RHS, to] = charges[:, at]
            target[RHS:ROWS, to] = points[:, at]

    fill(send_down, 0, 0)
    fill(send_up, BY - 1, BY - 2)


def side_kernel(points, charges, skeleton, coef, from_down, from_up, send_left, send_right):
    def fill(target, near_x, far_x):
        for x in range(2):
            at_x = far_x + x
            for y in range(2):
                target[:, column(x * FX + y)] = from_down[:, column(at_x * 2 + y)]
                target[:, column(x * FX + y + BY + 2)] = from_up[:, column(at_x * 2 + y)]
            to = pl.ds((x * FX + 2) * COL, BY * COL)
            at = pl.ds(at_x * BY * COL, BY * COL)
            target[0:RHS, to] = coef[:, at]
            target[RHS:ROWS, to] = skeleton[:, at]
        target[:, column(XFAR)] = from_down[:, column(YFAR + near_x)]
        target[:, column(XFAR + BY + 1)] = from_up[:, column(YFAR + near_x)]
        to = pl.ds((XFAR + 1) * COL, BY * COL)
        at = pl.ds(near_x * BY * COL, BY * COL)
        target[0:RHS, to] = charges[:, at]
        target[RHS:ROWS, to] = points[:, at]

    fill(send_left, 0, 0)
    fill(send_right, BX - 1, BX - 2)


def build_column(coords, values, centre, col, sources, charge, targets=None, leaf=None):
    place = (coords - centre) * KERNEL_SCALE
    high = place.astype(BF16).astype(F32)
    rest = place - high
    mid = rest.astype(BF16).astype(F32)
    low = rest - mid
    norm = jnp.sum(place * place, axis=0, keepdims=True)
    norm_high = norm.astype(BF16).astype(F32)
    norm_rest = norm - norm_high
    norm_mid = norm_rest.astype(BF16).astype(F32)
    norm_low = norm_rest - norm_mid
    one = jnp.ones_like(norm)
    empty = jnp.zeros((8, COL), F32)
    rows = jnp.concatenate(
        [high, high, norm_high, norm_mid, high, mid, norm_low, one, mid, low, one, one, empty], axis=0
    )
    half = low_lanes(32)
    half_values = low_lanes(RHS)
    scaled = values * SIGNAL
    for pair in range(BZ // 2):
        lanes = slice(pair * 128, pair * 128 + 128)
        tile, tile_values = rows[:, lanes], scaled[:, lanes]
        turned, turned_values = pltpu.roll(tile, LEAF, 1), pltpu.roll(tile_values, LEAF, 1)
        at = col * BZ + 2 * pair
        sources[at] = jnp.where(half, tile, turned).astype(BF16)
        sources[at + 1] = jnp.where(half, turned, tile).astype(BF16)
        charge[at] = jnp.concatenate(halves(jnp.where(half_values, tile_values, turned_values)), axis=0)
        charge[at + 1] = jnp.concatenate(halves(jnp.where(half_values, turned_values, tile_values)), axis=0)
    if targets is not None:
        rows = jnp.concatenate(
            [
                -2.0 * high, -2.0 * mid, one, one, -2.0 * low, -2.0 * high, one, norm_high,
                -2.0 * mid, -2.0 * high, norm_mid, norm_low, empty,
            ],
            axis=0,
        )
        for pair in range(BZ // 2):
            tile = rows[:, pair * 128 : pair * 128 + 128].T.astype(BF16)
            targets[leaf + 2 * pair] = tile[:LEAF]
            targets[leaf + 2 * pair + 1] = tile[LEAF:]


def main_kernel(
    near_ids, far_ids, points, charges, skeleton, coef, from_down, from_up, from_left, from_right,
    near_out, far_out,
    near_sources, near_charge, near_targets, far_sources, far_charge, far_targets, squares, entries, sums, counts,
):
    top, leaf = lax.axis_index("top"), lax.axis_index("leaf")
    row = lax.broadcasted_iota(jnp.int32, (3, COL), 0)
    centre = jnp.where(
        row == 0, top.astype(F32) + 0.5, jnp.where(row == 1, leaf.astype(F32) + 0.5, 1.0)
    )

    def region(array, first, count, to, sources, charge):
        def step(i, carry):
            at = column(first + i)
            build_column(array[RHS:ROWS, at], array[0:RHS, at], centre, to(i), sources, charge)
            return carry

        lax.fori_loop(0, count, step, 0)

    def own(coords, values, to, sources, charge, targets):
        def step(i, carry):
            at = column(i)
            build_column(coords[:, at], values[:, at], centre, to(i), sources, charge, targets, i * BZ)
            return carry

        lax.fori_loop(0, COLS, step, 0)

    own(points, charges, lambda i: (i // BY + 1) * NX + i % BY + 1, near_sources, near_charge, near_targets)
    region(from_down, YFAR, YNEAR, lambda i: (i + 1) * NX, near_sources, near_charge)
    region(from_up, YFAR, YNEAR, lambda i: (i + 1) * NX + NX - 1, near_sources, near_charge)
    region(from_left, XFAR, XNEAR, lambda i: i, near_sources, near_charge)
    region(from_right, XFAR, XNEAR, lambda i: (NX - 1) * NX + i, near_sources, near_charge)
    near_sources[NEAR_NULL] = jnp.zeros((32, 128), BF16)
    near_charge[NEAR_NULL] = jnp.zeros((32, 128), BF16)
    own(skeleton, coef, lambda i: (i // BY + 2) * FX + i % BY + 2, far_sources, far_charge, far_targets)
    region(from_down, 0, YFAR, lambda i: (i // 2 + 2) * FX + i % 2, far_sources, far_charge)
    region(from_up, 0, YFAR, lambda i: (i // 2 + 2) * FX + i % 2 + BY + 2, far_sources, far_charge)
    region(from_left, 0, XFAR, lambda i: i, far_sources, far_charge)
    region(from_right, 0, XFAR, lambda i: (BX + 2) * FX + i, far_sources, far_charge)

    half = low_lanes(32)
    half_sums = low_lanes(RHS)

    def gathered(array, ids, slot, target):
        four = [array[ids[slot + k, target]] for k in range(4)]
        return jnp.concatenate([jnp.where(half, four[0], four[1]), jnp.where(half, four[2], four[3])], axis=1)

    def entries_of(unit):
        square = jnp.maximum(squares[unit], 1e-20)
        scaled = square * lax.rsqrt(square)
        high, low = halves((1.0 + scaled) * jnp.exp(-scaled))
        entries[unit, 0:LEAF] = high
        entries[unit, LEAF : 2 * LEAF] = low

    def clear():
        for unit in range(UNITS):
            squares[unit] = jnp.full((LEAF, 4 * LEAF), 1e6, F32)
            entries[unit] = jnp.zeros((2 * LEAF, 4 * LEAF), BF16)

    def near_leaf(group, unit):
        inner = unit * BZ + group + 1
        outer = ((group - 6) * (COLS // 2) + unit // 2) * BZ + (unit % 2) * (BZ - 1)
        return jnp.where(group < 6, inner, outer)

    for group in range(8):
        most = near_ids[28, near_leaf(group, 0)]
        for unit in range(1, UNITS):
            most = jnp.maximum(most, near_ids[28, near_leaf(group, unit)])
        counts[group] = jnp.minimum((most + 3) // 4, 7)

    def zero(i, carry):
        sums[i] = jnp.zeros((RHS, 128), F32)
        return carry

    lax.fori_loop(0, HERE, zero, 0)
    clear()
    steps = counts[0]
    for group in range(1, 8):
        steps = steps + counts[group]

    def near_step(step, state):
        (group, part), later, last = state
        for unit in range(UNITS):
            target = near_leaf(last[0], unit)
            product = dot(gathered(near_charge, near_ids, last[1] * 4, target), entries[unit], NT)
            sums[target] = sums[target] + (product[:RHS] + product[RHS:])
            entries_of(unit)
            target = near_leaf(group, unit)
            squares[unit] = dot(near_targets[target], gathered(near_sources, near_ids, part * 4, target))
        over = part + 1 >= counts[group]
        following = (
            jnp.where(over, jnp.minimum(group + 1, 7), group),
            jnp.where(over, 0, part + 1),
        )
        return following, (group, part), later

    start = (jnp.int32(0), jnp.int32(0))
    lax.fori_loop(0, steps + 2, near_step, (start, start, start))

    def near_store(i, carry):
        place = pl.ds(pl.multiple_of(i * 128, 128), 128)
        first, second = sums[2 * i], sums[2 * i + 1]
        first = first + pltpu.roll(first, LEAF, 1)
        second = second + pltpu.roll(second, LEAF, 1)
        near_out[:, place] = jnp.where(half_sums, first, second) + NUGGET * charges[:, place]
        return carry

    lax.fori_loop(0, HERE // 2, near_store, 0)

    clear()

    def far_step(step, carry):
        after = jnp.minimum(step, HERE // 4 - 1) * 4
        before = jnp.maximum(step - 2, 0) * 4
        for i in range(4):
            total = jnp.zeros((2 * RHS, 128), F32)
            for part in range(4):
                unit = i * 4 + part
                total = total + dot(gathered(far_charge, far_ids, part * 4, before + i), entries[unit], NT)
                entries_of(unit)
                squares[unit] = dot(
                    far_targets[after + i], gathered(far_sources, far_ids, part * 4, after + i)
                )
            sums[before + i] = total[:RHS] + total[RHS:]
        return carry

    lax.fori_loop(0, HERE // 4 + 2, far_step, 0)

    def far_store(i, carry):
        place = pl.ds(pl.multiple_of(i * 128, 128), 128)
        first, second = sums[2 * i], sums[2 * i + 1]
        first = first + pltpu.roll(first, LEAF, 1)
        second = second + pltpu.roll(second, LEAF, 1)
        far_out[:, place] = jnp.where(half_sums, first, second)
        return carry

    lax.fori_loop(0, HERE // 2, far_store, 0)


def last_kernel(
    device_far, rows, device_skeleton, branch_skeleton, branch_transfer, transfer, basis, near, far, out
):
    top, leaf = lax.axis_index("top"), lax.axis_index("leaf")
    same = lax.broadcasted_iota(jnp.int32, (LEAF, LEAF), 0) == lax.broadcasted_iota(
        jnp.int32, (LEAF, LEAF), 1
    )

    def upright(coords):
        return [
            jnp.sum(jnp.where(same, coords[i : i + 1], 0.0), axis=1, keepdims=True) for i in range(3)
        ]

    def block(own, other):
        total = 0.0
        for i in range(3):
            differ = own[i] - other[i : i + 1]
            total = total + differ * differ
        scaled = KERNEL_SCALE * jnp.sqrt(total)
        return SIGNAL * (1.0 + scaled) * jnp.exp(-scaled)

    def exact(a, b, dims):
        return lax.dot_general(a, b, dims, precision=EXACT, preferred_element_type=F32)

    own = upright(device_skeleton[top * 16 + leaf])
    coupled = jnp.zeros((RHS, LEAF), F32)
    for k in range(4):
        partner = jnp.minimum(jnp.maximum(device_far[k, 0], 0), 127)
        coupled = coupled + exact(rows[partner][:, :LEAF], block(own, device_skeleton[partner]), NT)
    own = upright(branch_skeleton[top])
    field = jnp.zeros((RHS, LEAF), F32)
    for e in range(8):
        total = rows[16 * e]
        for d in range(1, 16):
            total = total + rows[16 * e + d]
        weight = jnp.where(jnp.abs(e - top) >= 2, 1.0, 0.0)
        field = field + exact(total[:, LEAF:] * weight, block(own, branch_skeleton[e]), NT)
    coupled = coupled + exact(field, branch_transfer[...], NN)
    lifted = jnp.concatenate(halves(coupled), axis=0)
    half = low_lanes(RHS)
    together = 4

    def step(index, carry):
        places, fields = [], []
        for part in range(together):
            place = pl.ds(pl.multiple_of((index * together + part) * 256, 256), 256)
            t_high, t_low = halves(transfer[:, place])
            up = dot(lifted, t_high) + dot(lifted, t_low)
            places.append(place)
            fields.append(far[:, place] + (up[:RHS] + up[RHS:]))
        products = []
        for place, value in zip(places, fields):
            pieces = []
            for i in range(4):
                tile = value[:, (i // 2) * 128 : (i // 2) * 128 + 128]
                tile = jnp.where(half, tile, 0.0) if i % 2 == 0 else jnp.where(half, 0.0, tile)
                pieces.extend(halves(tile))
            lines = jnp.concatenate(pieces, axis=0)
            b_high, b_low = halves(basis[:, place])
            products.append(
                dot(lines, jnp.concatenate([b_high, b_high], axis=0))
                + dot(lines, jnp.concatenate([b_low, b_low], axis=0))
            )
        for place, product in zip(places, products):
            each = [product[32 * i : 32 * i + 16] + product[32 * i + 16 : 32 * i + 32] for i in range(4)]
            result = jnp.concatenate(
                [
                    jnp.where(half, each[0][:, :128], each[1][:, :128]),
                    jnp.where(half, each[2][:, 128:], each[3][:, 128:]),
                ],
                axis=1,
            )
            out[:, place] = near[:, place] + result
        return carry

    lax.fori_loop(0, HERE // 4 // together, step, 0)


def shape(*dims, dtype=F32):
    return jax.ShapeDtypeStruct(dims, dtype)


def body(
    points,
    charges,
    near_list,
    far_list,
    leaf_basis,
    transfer,
    leaf_skeleton,
    device_far,
    branch_transfer,
    device_skeleton,
    branch_skeleton,
):
    here = charges.shape[1]

    def moved(array, axis, up):
        size = lax.axis_size(axis)
        pairs = [(i, i + 1) for i in range(size - 1)]
        return lax.ppermute(array, axis, pairs if up else [(j, i) for i, j in pairs])

    coef, device_row, near_ids, far_ids, send_down, send_up = pl.pallas_call(
        first_kernel,
        in_specs=[VMEM] * 8,
        out_specs=[VMEM] * 6,
        out_shape=[
            shape(RHS, here), shape(RHS, 128), shape(32, HERE, dtype=jnp.int32), shape(FAR, HERE, dtype=jnp.int32),
            shape(ROWS, YCOLS * COL), shape(ROWS, YCOLS * COL),
        ],
        compiler_params=PARAMS,
        name="coefficients",
    )(points, charges, near_list, far_list, leaf_basis, transfer, leaf_skeleton, branch_transfer)
    every_row = lax.all_gather(device_row, ("top", "leaf"), axis=0)
    from_down = moved(send_up, "leaf", True)
    from_up = moved(send_down, "leaf", False)
    send_left, send_right = pl.pallas_call(
        side_kernel,
        in_specs=[VMEM] * 6,
        out_specs=[VMEM] * 2,
        out_shape=[shape(ROWS, XCOLS * COL), shape(ROWS, XCOLS * COL)],
        compiler_params=PARAMS,
        name="sides",
    )(points, charges, leaf_skeleton, coef, from_down, from_up)
    from_left = moved(send_right, "top", True)
    from_right = moved(send_left, "top", False)
    near, far = pl.pallas_call(
        main_kernel,
        in_specs=[SMEM] * 2 + [VMEM] * 8,
        out_specs=[VMEM] * 2,
        out_shape=[shape(RHS, here), shape(RHS, here)],
        scratch_shapes=[
            pltpu.VMEM((NEAR_NULL + 1, 32, 128), BF16),
            pltpu.VMEM((NEAR_NULL + 1, 32, 128), BF16),
            pltpu.VMEM((HERE, LEAF, 32), BF16),
            pltpu.VMEM((FAR_ALL, 32, 128), BF16),
            pltpu.VMEM((FAR_ALL, 32, 128), BF16),
            pltpu.VMEM((HERE, LEAF, 32), BF16),
            pltpu.VMEM((UNITS, LEAF, 4 * LEAF), F32),
            pltpu.VMEM((UNITS, 2 * LEAF, 4 * LEAF), BF16),
            pltpu.VMEM((HERE, RHS, 128), F32),
            pltpu.SMEM((8,), jnp.int32),
        ],
        compiler_params=PARAMS,
        cost_estimate=pl.CostEstimate(flops=10**11, bytes_accessed=10**7, transcendentals=4 * 10**7),
        name="lists",
    )(near_ids, far_ids, points, charges, leaf_skeleton, coef, from_down, from_up, from_left, from_right)
    return pl.pallas_call(
        last_kernel,
        in_specs=[SMEM] + [VMEM] * 8,
        out_specs=VMEM,
        out_shape=shape(RHS, here),
        compiler_params=PARAMS,
        name="fields",
    )(
        device_far,
        every_row,
        device_skeleton.reshape(3, -1, LEAF).transpose(1, 0, 2),
        branch_skeleton.reshape(3, -1, LEAF).transpose(1, 0, 2),
        branch_transfer,
        transfer,
        leaf_basis,
        near,
        far,
    )


def solution(mesh):
    split = P(None, ("top", "leaf"))
    return jax.shard_map(
        body, mesh=mesh, in_specs=(split,) * 9 + (P(), P()), out_specs=split, check_vma=False
    )
```

time: 870 us -> 160 us (0.18); the launches traced: 855 us -> 157 us
  matrix products: 301 us -> 0 us
  other arithmetic: 260 us -> 0 us
  local copies, waits for them, and re-layouts: 152 us -> 8.64 us
  blocking collectives: 110 us -> 0 us
  Pallas kernels: 0 us -> 93.5 us
  waiting for transfers between devices: 2.37 us -> 29.3 us
  starting transfers between devices: 26.9 us -> 12 us
  between operations: 0.94 us -> 13.5 us
    dot_general x16 -> x0, matrix products: 301 us -> none  [the longest x4 162 us: near_block(): jnp.einsum('sbij,sb,rsbj->rbi', entries, usable, source[3:], precision=EX...]
    reduce_sum x11 -> x0, other arithmetic: 213 us -> none  [the longest x10 213 us: kernel_tiles(): distance = jnp.sqrt(jnp.sum(differ * differ, axis=0))]
    all_gather x2 -> x0, blocking collectives: 110 us -> none  [the longest x1 57 us: body(): lax.all_gather(projected[None], ('top', 'leaf'), axis=0, tiled=True)]
    pallas_call x0 -> x4, Pallas kernels: none -> 93.5 us  [the longest x1 76.5 us: body(): pl.pallas_call(main_kernel, in_specs=[SMEM] * 2 + [VMEM] * 8, out_specs=[...]
    gather x10 -> x0, local copies, waits for them, and re-layouts: 60.5 us -> none  [the longest x4 29.9 us: far_block(): source = jnp.take(window, positions, axis=1)]
    select_n x22 -> x0, other arithmetic: 36 us -> none  [the longest x8 20.5 us: near_block(): source = jnp.take(window, positions, axis=1)]
    ppermute x8 -> x4, waiting for transfers between devices: 2.37 us -> 29.3 us  [moved(): lax.ppermute(array, axis, pairs if up else [(j, i) for i, j in pairs])]
    while x10 -> x0, local copies, waits for them, and re-layouts: 25.5 us -> none  [the longest x1 11.6 us: body(): far_out = lax.map(far_step, (blocked(skeletons), blocked(far_pos)))]
  transfers between devices with their start and end apart: 8 -> 5, of which waited for: 3 -> 4; matrix products, arithmetic and copies ran while one was open for 48% -> 0% of each run, Pallas kernels for 0% -> 49%
where the time goes in v1:
time: 160 us; the launch traced here: 157 us
  Pallas kernels  93.5 us (58%)
  waiting for transfers between devices  29.3 us (18%)
  between operations  13.5 us (8%)
  starting transfers between devices  12 us (8%)
  local copies, waits for them, and re-layouts  8.64 us (5%)
    pallas_call x1, Pallas kernels, body(): pl.pallas_call(main_kernel, in_specs=[SMEM] * 2 + [VMEM] * 8, out_specs=[...  76.5 us
    ppermute x4, waiting for transfers between devices, moved(): lax.ppermute(array, axis, pairs if up else [(j, i) for i, j in pairs])  29.3 us
    ppermute x4, starting transfers between devices, moved(): lax.ppermute(array, axis, pairs if up else [(j, i) for i, j in pairs])  12 us
    unnamed x33, local copies, waits for them, and re-layouts  8.26 us
    pallas_call x1, Pallas kernels, body(): pl.pallas_call(last_kernel, in_specs=[SMEM] + [VMEM] * 8, out_specs=VMEM,...  7.94 us
    pallas_call x1, Pallas kernels, body(): pl.pallas_call(first_kernel, in_specs=[VMEM] * 8, out_specs=[VMEM] * 6, o...  7.52 us
  transfers between devices with their start and end apart: 5, of which 4 were waited for; matrix products, arithmetic and copies ran while one was open for 0% of the time, Pallas kernels for 49%

profile of v1, /device:TPU:107, one launch (start us, length us, event | category | flops | bytes accessed | tf_op | source)
XLA Modules:
  0.0 156.9 jit_solution(4951396965290694255)
XLA Ops:
  6.5 0.0 all-gather.3.cloned.1.call-start
  6.5 1.0 copy-done
  7.6 0.9 copy-done.3
  8.5 0.9 copy-done.5
  9.4 0.8 copy-done.9
  10.1 0.7 copy-done.11
  10.9 0.7 copy-done.12
  11.6 7.5 %coefficients.1 = (f32[16,8192]{1,0:T(8,128)S(1)}, f32[16,128]{1,0:T(8,128)}, s32[32,128]{1,0:T(8,128)S(1)}, s32[16,128]{1,0:T(8,128)S(1)}, f32[19,6144]{1,0:T(8,128)S(1)}, /*index=5*/f32[19,6144]{1,0:T(8,128)S(1)}) custom-call(f32[3,8192]{1,0:T(4,128)S(1)} %copy-done.3, f32[16,8192]{1,0:T(8,128)S(1)} %copy-done, s32[27,128]{1,0:T(8,128)S(1)} %copy-done.11, ...), custom_call_target="tpu_custom_call" | custom-call | tf_op jit(solution)/shard_map/coefficients/pallas_call | solution.py:439
  19.1 1.9 %collective-permute-start = (f32[19,6144]{1,0:T(8,128)S(1)}, f32[19,6144]{1,0:T(8,128)S(1)}, u32[]{:S(2)}, u32[]{:S(2)}) collective-permute-start(f32[19,6144]{1,0:T(8,128)S(1)} %get-tuple-element.19), channel_id=1, source_target_pairs={{0,1},{1,2},{2,3},{3,4},{4,5},{5,6},{6,7},{7,8},{8,9},{9,10},{10,1... | collective-permute-start | bytes 1400840 | tf_op jit(solution)/shard_map/ppermute | solution.py:437
  21.0 3.4 %collective-permute-start.1 = (f32[19,6144]{1,0:T(8,128)S(1)}, f32[19,6144]{1,0:T(8,128)S(1)}, u32[]{:S(2)}, u32[]{:S(2)}) collective-permute-start(f32[19,6144]{1,0:T(8,128)S(1)} %get-tuple-element.20), channel_id=1, source_target_pairs={{1,0},{2,1},{3,2},{4,3},{5,4},{6,5},{7,6},{8,7},{9,8},{10,9},{11,1... | collective-permute-start | bytes 1400840 | tf_op jit(solution)/shard_map/ppermute | solution.py:437
  24.4 10.8 %collective-permute-done.from_down = f32[19,6144]{1,0:T(8,128)S(1)} collective-permute-done((f32[19,6144]{1,0:T(8,128)S(1)}, f32[19,6144]{1,0:T(8,128)S(1)}, u32[]{:S(2)}, u32[]{:S(2)}) %collective-permute-start) | collective-permute-done | bytes 466976 | tf_op jit(solution)/shard_map/ppermute | solution.py:437
  35.2 3.8 %collective-permute-done.1.from_up = f32[19,6144]{1,0:T(8,128)S(1)} collective-permute-done((f32[19,6144]{1,0:T(8,128)S(1)}, f32[19,6144]{1,0:T(8,128)S(1)}, u32[]{:S(2)}, u32[]{:S(2)}) %collective-permute-start.1) | collective-permute-done | bytes 466976 | tf_op jit(solution)/shard_map/ppermute | solution.py:437
  39.0 0.0 copy-start.4
  39.0 0.0 copy-start.6
  39.0 1.5 sides.1
  40.5 4.8 %collective-permute-start.2 = (f32[19,11264]{1,0:T(8,128)}, f32[19,11264]{1,0:T(8,128)}, u32[]{:S(2)}, u32[]{:S(2)}) collective-permute-start(f32[19,11264]{1,0:T(8,128)} %get-tuple-element.21), channel_id=1, source_target_pairs={{0,16},{16,32},{32,48},{48,64},{64,80},{80,96},{96,112},{1,17},{17... | collective-permute-start | bytes 2568200 | tf_op jit(solution)/shard_map/ppermute | solution.py:437
  45.3 1.9 %collective-permute-start.3 = (f32[19,11264]{1,0:T(8,128)}, f32[19,11264]{1,0:T(8,128)}, u32[]{:S(2)}, u32[]{:S(2)}) collective-permute-start(f32[19,11264]{1,0:T(8,128)} %get-tuple-element.22), channel_id=1, source_target_pairs={{16,0},{32,16},{48,32},{64,48},{80,64},{96,80},{112,96},{17,1},{33... | collective-permute-start | bytes 2568200 | tf_op jit(solution)/shard_map/ppermute | solution.py:437
  47.2 0.0 all-gather.3.cloned.1.call-update
  47.2 0.0 copy-done.13
  47.2 0.2 reshape.6
  47.4 0.1 copy.18
  47.5 0.1 reshape.7
  47.6 0.1 copy.15.device_far
  47.7 9.9 %collective-permute-done.2.from_left = f32[19,11264]{1,0:T(8,128)} collective-permute-done((f32[19,11264]{1,0:T(8,128)}, f32[19,11264]{1,0:T(8,128)}, u32[]{:S(2)}, u32[]{:S(2)}) %collective-permute-start.2) | collective-permute-done | bytes 856096 | tf_op jit(solution)/shard_map/ppermute | solution.py:437
  57.7 4.7 %collective-permute-done.3.from_right = f32[19,11264]{1,0:T(8,128)} collective-permute-done((f32[19,11264]{1,0:T(8,128)}, f32[19,11264]{1,0:T(8,128)}, u32[]{:S(2)}, u32[]{:S(2)}) %collective-permute-start.3) | collective-permute-done | bytes 856096 | tf_op jit(solution)/shard_map/ppermute | solution.py:437
  62.4 0.0 copy-start.10
  62.4 76.5 %lists.1 = (f32[16,8192]{1,0:T(8,128)S(1)}, f32[16,8192]{1,0:T(8,128)S(1)}) custom-call(s32[32,128]{1,0:T(8,128)S(1)} %get-tuple-element.16.near_ids, s32[16,128]{1,0:T(8,128)S(1)} %get-tuple-element.17.far_ids, f32[3,8192]{1,0:T(4,128)S(1)} %copy-done.4, f32[16,8192]{1,0:T(8,128)S(1)} %copy-done.1, f32[3,8192]{1,0:T(4,128)S(1)} %copy-done.6, ...), custom_call_target="tpu_custom_call" | custom-call | flops 99999997952 | bytes 10000000 | tf_op jit(solution)/shard_map/lists/pallas_call | solution.py:463
  139.0 0.0 copy-start.7
  139.0 0.8 copy-done.7
  139.8 1.2 copy-done.2
  141.1 1.0 copy-done.8
  142.1 7.9 %fields.1 = f32[16,8192]{1,0:T(8,128)} custom-call(s32[4,1]{1,0:T(4,128)S(1)} %copy.15.device_far, f32[128,16,128]{2,1,0:T(8,128)S(1)} %bitcast.7, f32[128,3,64]{2,1,0:T(4,128)S(1)} %bitcast.8, f32[8,3,64]{2,1,0:T(4,128)S(1)} %bitcast.9, f32[64,64]{1,0:T(8,128)S(1)} %copy-done.10, f32[64,8192]{1,0:T(8,128)} %transfer.3, f32[64,8192]{1,0:T(8,128)} %basis.3, ...), custom_call_target="tpu_custom_call" | custom-call | tf_op jit(solution)/shard_map/fields/pallas_call | solution.py:484
  (20 shorter events, 0.0 us)
Async XLA Ops:
  6.5 133.3 %all-gather.3.cloned.1.call-start = ((), (), s32[]{:S(2)}) async-start(), calls=%async_computation | async-start | bytes 1056768 | tf_op jit(solution)/shard_map/all_gather | solution.py:450
  6.5 1.0 copy-start
  7.6 0.9 copy-start.3
  8.5 0.9 copy-start.5
  9.4 0.8 copy-start.9
  10.1 0.7 copy-start.11
  10.9 0.7 copy-start.12
  19.1 16.1 %collective-permute-start = (f32[19,6144]{1,0:T(8,128)S(1)}, f32[19,6144]{1,0:T(8,128)S(1)}, u32[]{:S(2)}, u32[]{:S(2)}) collective-permute-start(f32[19,6144]{1,0:T(8,128)S(1)} %get-tuple-element.19), channel_id=1, source_target_pairs={{0,1},{1,2},{2,3},{3,4},{4,5},{5,6},{6,7},{7,8},{8,9},{9,10},{10,1... | collective-permute-start | bytes 1400840 | tf_op jit(solution)/shard_map/ppermute | solution.py:437
  21.0 18.0 %collective-permute-start.1 = (f32[19,6144]{1,0:T(8,128)S(1)}, f32[19,6144]{1,0:T(8,128)S(1)}, u32[]{:S(2)}, u32[]{:S(2)}) collective-permute-start(f32[19,6144]{1,0:T(8,128)S(1)} %get-tuple-element.20), channel_id=1, source_target_pairs={{1,0},{2,1},{3,2},{4,3},{5,4},{6,5},{7,6},{8,7},{9,8},{10,9},{11,1... | collective-permute-start | bytes 1400840 | tf_op jit(solution)/shard_map/ppermute | solution.py:437
  39.0 8.3 %copy-start.13 = (f32[3,8192]{1,0:T(4,128)S(1)}, f32[3,8192]{1,0:T(4,128)}, u32[]{:S(2)}) copy-start(f32[3,8192]{1,0:T(4,128)} %param.20) | copy-start | bytes 294916
  39.0 8.6 %copy-start.14 = (f32[3,512]{1,0:T(4,128)S(1)}, f32[3,512]{1,0:T(4,128)}, u32[]{:S(2)}) copy-start(f32[3,512]{1,0:T(4,128)} %param.21) | copy-start | bytes 18436
  39.0 8.7 %copy-start.15 = (s32[4,1]{0,1:T(1,128)S(1)}, s32[4,1]{0,1:T(1,128)}, u32[]{:S(2)}) copy-start(s32[4,1]{0,1:T(1,128)} %param.18) | copy-start | bytes 52
  39.0 23.4 %copy-start.1 = (f32[16,8192]{1,0:T(8,128)S(1)}, f32[16,8192]{1,0:T(8,128)}, u32[]{:S(2)}) copy-start(f32[16,8192]{1,0:T(8,128)} %charges.5) | copy-start | bytes 1572868
  39.0 23.4 %copy-start.4 = (f32[3,8192]{1,0:T(4,128)S(1)}, f32[3,8192]{1,0:T(4,128)}, u32[]{:S(2)}) copy-start(f32[3,8192]{1,0:T(4,128)} %points.5) | copy-start | bytes 294916
  39.0 23.4 %copy-start.6 = (f32[3,8192]{1,0:T(4,128)S(1)}, f32[3,8192]{1,0:T(4,128)}, u32[]{:S(2)}) copy-start(f32[3,8192]{1,0:T(4,128)} %skeleton.5) | copy-start | bytes 294916
  40.5 17.2 %collective-permute-start.2 = (f32[19,11264]{1,0:T(8,128)}, f32[19,11264]{1,0:T(8,128)}, u32[]{:S(2)}, u32[]{:S(2)}) collective-permute-start(f32[19,11264]{1,0:T(8,128)} %get-tuple-element.21), channel_id=1, source_target_pairs={{0,16},{16,32},{32,48},{48,64},{64,80},{80,96},{96,112},{1,17},{17... | collective-permute-start | bytes 2568200 | tf_op jit(solution)/shard_map/ppermute | solution.py:437
  45.3 17.1 %collective-permute-start.3 = (f32[19,11264]{1,0:T(8,128)}, f32[19,11264]{1,0:T(8,128)}, u32[]{:S(2)}, u32[]{:S(2)}) collective-permute-start(f32[19,11264]{1,0:T(8,128)} %get-tuple-element.22), channel_id=1, source_target_pairs={{16,0},{32,16},{48,32},{64,48},{80,64},{96,80},{112,96},{17,1},{33... | collective-permute-start | bytes 2568200 | tf_op jit(solution)/shard_map/ppermute | solution.py:437
  62.4 77.4 %copy-start.10 = (f32[64,64]{1,0:T(8,128)S(1)}, f32[64,64]{1,0:T(8,128)}, u32[]{:S(2)}) copy-start(f32[64,64]{1,0:T(8,128)} %branch_transfer.3) | copy-start | bytes 49156
  139.0 0.9 copy-start.7
  139.8 1.2 copy-start.2
  141.0 1.0 copy-start.8
Sparse Core Ops, SparseCore 0:
  47.4 61.6 all-gather.2

commit v2 on v1

--- a/solution.py
+++ b/solution.py
@@ -1,5 +1,3 @@
-import functools
-
 import jax
 import jax.numpy as jnp
 from jax import lax
@@ -26,7 +24,10 @@
 YCOLS = YFAR + YNEAR
 XCOLS = XFAR + XNEAR
 ROWS = RHS + 3
-UNITS = 16
+UNITS = 32
+INNER = ((1, 1), (1, 2), (2, 1), (2, 2))
+STRIP = ((1, 0), (1, 3), (2, 0), (2, 3))
+RIM = tuple((x, y) for x in (0, 3) for y in range(4))
 
 EXACT = lax.Precision.HIGHEST
 KERNEL_SCALE = 3.4641016151377544
@@ -38,7 +39,7 @@
 NN = (((1,), (0,)), ((), ()))
 VMEM = pl.BlockSpec(memory_space=pltpu.VMEM)
 SMEM = pl.BlockSpec(memory_space=pltpu.SMEM)
-PARAMS = pltpu.CompilerParams(vmem_limit_bytes=50 * 2**20)
+PARAMS = pltpu.CompilerParams(vmem_limit_bytes=60 * 2**20)
 
 
 def dot(a, b, dims=NN):
@@ -66,15 +67,36 @@
     return jnp.where(ids >= 0, place, null)
 
 
+def work_lists(used, work):
+    lane = lax.broadcasted_iota(jnp.int32, (1, HERE), 1)
+    inner_x = (((lane >> 5) + 1) & 2) != 0
+    inner_y = ((((lane >> 3) & 3) + 1) & 2) != 0
+    member = jnp.where(inner_x, jnp.where(inner_y, 0, 1), 2)
+    parts = (used + 3) >> 2
+    first = lax.broadcasted_iota(jnp.int32, (HERE, HERE), 0)
+    second = lax.broadcasted_iota(jnp.int32, (HERE, HERE), 1)
+    place = lax.broadcasted_iota(jnp.int32, (HERE, 512), 1)
+    for phase in range(3):
+        kept = jnp.where(member == phase, parts, 0)
+        end = jnp.sum(jnp.where(second <= first, kept, 0), axis=1, keepdims=True)
+        count = jnp.sum(jnp.where(second == first, kept, 0), axis=1, keepdims=True)
+        passed = end <= place
+        leaf = jnp.sum(jnp.where(passed, 1, 0), axis=0, keepdims=True)
+        start = jnp.sum(jnp.where(passed, count, 0), axis=0, keepdims=True)
+        code = leaf * 8 + (place[:1] - start)
+        work[phase : phase + 1] = jnp.where(leaf < HERE, code, 7)
+        work[4 + phase : 5 + phase] = jnp.zeros((1, 512), jnp.int32) + jnp.sum(kept, axis=1, keepdims=True)
+
+
 def first_kernel(
     points, charges, near_list, far_list, basis, transfer, skeleton, branch_transfer,
-    coef, device_row, near_ids, far_ids, send_down, send_up,
+    coef, device_row, near_ids, far_ids, work, send_down, send_up,
 ):
     top, leaf = lax.axis_index("top"), lax.axis_index("leaf")
     listed = near_list[...]
     near_ids[0:NEAR] = window_ids(listed, 1, NX, top, leaf, NEAR_NULL)
-    near_ids[NEAR : NEAR + 1] = jnp.full((1, HERE), NEAR_NULL, jnp.int32)
-    near_ids[28:29] = jnp.sum((listed >= 0).astype(jnp.int32), axis=0, keepdims=True)
+    near_ids[NEAR:32] = jnp.full((5, HERE), NEAR_NULL, jnp.int32)
+    work_lists(jnp.sum((listed >= 0).astype(jnp.int32), axis=0, keepdims=True), work)
     far_ids[...] = window_ids(far_list[...], 2, FX, top, leaf, 0)
 
     lane = lax.broadcasted_iota(jnp.int32, (2 * RHS, 4 * LEAF), 1) // LEAF
@@ -153,18 +175,21 @@
     fill(send_right, BX - 1, BX - 2)
 
 
-def build_column(coords, values, centre, col, sources, charge, targets=None, leaf=None):
+def pieces_of(coords, centre):
     place = (coords - centre) * KERNEL_SCALE
     high = place.astype(BF16).astype(F32)
     rest = place - high
     mid = rest.astype(BF16).astype(F32)
-    low = rest - mid
     norm = jnp.sum(place * place, axis=0, keepdims=True)
     norm_high = norm.astype(BF16).astype(F32)
     norm_rest = norm - norm_high
     norm_mid = norm_rest.astype(BF16).astype(F32)
-    norm_low = norm_rest - norm_mid
-    one = jnp.ones_like(norm)
+    return high, mid, rest - mid, norm_high, norm_mid, norm_rest - norm_mid
+
+
+def build_column(coords, values, centre, col, sources, charge):
+    high, mid, low, norm_high, norm_mid, norm_low = pieces_of(coords, centre)
+    one = jnp.ones_like(norm_high)
     empty = jnp.zeros((8, COL), F32)
     rows = jnp.concatenate(
         [high, high, norm_high, norm_mid, high, mid, norm_low, one, mid, low, one, one, empty], axis=0
@@ -181,154 +206,190 @@
         sources[at + 1] = jnp.where(half, turned, tile).astype(BF16)
         charge[at] = jnp.concatenate(halves(jnp.where(half_values, tile_values, turned_values)), axis=0)
         charge[at + 1] = jnp.concatenate(halves(jnp.where(half_values, turned_values, tile_values)), axis=0)
-    if targets is not None:
-        rows = jnp.concatenate(
-            [
-                -2.0 * high, -2.0 * mid, one, one, -2.0 * low, -2.0 * high, one, norm_high,
-                -2.0 * mid, -2.0 * high, norm_mid, norm_low, empty,
-            ],
-            axis=0,
-        )
-        for pair in range(BZ // 2):
-            tile = rows[:, pair * 128 : pair * 128 + 128].T.astype(BF16)
-            targets[leaf + 2 * pair] = tile[:LEAF]
-            targets[leaf + 2 * pair + 1] = tile[LEAF:]
-
-
-def main_kernel(
-    near_ids, far_ids, points, charges, skeleton, coef, from_down, from_up, from_left, from_right,
-    near_out, far_out,
-    near_sources, near_charge, near_targets, far_sources, far_charge, far_targets, squares, entries, sums, counts,
-):
+
+
+def build_targets(coords, centre, targets, leaf):
+    high, mid, low, norm_high, norm_mid, norm_low = pieces_of(coords, centre)
+    one = jnp.ones_like(norm_high)
+    rows = jnp.concatenate(
+        [
+            -2.0 * high, -2.0 * mid, one, one, -2.0 * low, -2.0 * high, one, norm_high,
+            -2.0 * mid, -2.0 * high, norm_mid, norm_low, jnp.zeros((8, COL), F32),
+        ],
+        axis=0,
+    )
+    for pair in range(BZ // 2):
+        tile = rows[:, pair * 128 : pair * 128 + 128].T.astype(BF16)
+        targets[leaf + 2 * pair] = tile[:LEAF]
+        targets[leaf + 2 * pair + 1] = tile[LEAF:]
+
+
+def centre_of():
     top, leaf = lax.axis_index("top"), lax.axis_index("leaf")
     row = lax.broadcasted_iota(jnp.int32, (3, COL), 0)
-    centre = jnp.where(
-        row == 0, top.astype(F32) + 0.5, jnp.where(row == 1, leaf.astype(F32) + 0.5, 1.0)
-    )
-
-    def region(array, first, count, to, sources, charge):
-        def step(i, carry):
-            at = column(first + i)
-            build_column(array[RHS:ROWS, at], array[0:RHS, at], centre, to(i), sources, charge)
+    return jnp.where(row == 0, top.astype(F32) + 0.5, jnp.where(row == 1, leaf.astype(F32) + 0.5, 1.0))
+
+
+def region(array, first, count, to, centre, sources, charge):
+    def step(i, carry):
+        at = column(first + i)
+        build_column(array[RHS:ROWS, at], array[0:RHS, at], centre, to(i), sources, charge)
+        return carry
+
+    lax.fori_loop(0, count, step, 0)
+
+
+def own_columns(coords, values, to, centre, sources, charge):
+    def step(i, carry):
+        at = column(i)
+        build_column(coords[:, at], values[:, at], centre, to(i), sources, charge)
+        return carry
+
+    lax.fori_loop(0, COLS, step, 0)
+
+
+def gathered(array, ids, slot, target):
+    half = low_lanes(32)
+    four = [array[ids[slot + k, target]] for k in range(4)]
+    return jnp.concatenate([jnp.where(half, four[0], four[1]), jnp.where(half, four[2], four[3])], axis=1)
+
+
+def entries_of(square):
+    square = jnp.maximum(square, 1e-20)
+    scaled = square * lax.rsqrt(square)
+    decay = jnp.exp(-scaled)
+    return jnp.concatenate(halves(decay + scaled * decay), axis=0)
+
+
+def list_steps(steps, choose, ids, sources, charge, targets, squares, add):
+    def distances(step, unit):
+        target, slot = choose(step, unit)
+        squares[unit] = dot(targets[target], gathered(sources, ids, slot, target))
+
+    for unit in range(UNITS):
+        distances(0, unit)
+
+    def run(step, carry):
+        waiting = None
+        for unit in range(UNITS + 1):
+            if unit < UNITS:
+                entries = entries_of(squares[unit])
+                distances(jnp.minimum(step + 1, steps - 1), unit)
+            if waiting is not None:
+                target, slot = choose(step, unit - 1)
+                product = dot(gathered(charge, ids, slot, target), waiting, NT)
+                add(step, unit - 1, target, product[:RHS] + product[RHS:])
+            waiting = entries
+        return carry
+
+    lax.fori_loop(0, steps, run, 0)
+
+
+def near_pass(phase, cells, near_ids, work, points, centre, sources, charge, targets, squares, sums):
+    for x, y in cells:
+        col = x * BY + y
+        build_targets(points[:, col * COL : col * COL + COL], centre, targets, col * BZ)
+
+        def zero(i, carry, first=col * BZ):
+            sums[first + i] = jnp.zeros((RHS, 128), F32)
             return carry
 
-        lax.fori_loop(0, count, step, 0)
-
-    def own(coords, values, to, sources, charge, targets):
-        def step(i, carry):
-            at = column(i)
-            build_column(coords[:, at], values[:, at], centre, to(i), sources, charge, targets, i * BZ)
-            return carry
-
-        lax.fori_loop(0, COLS, step, 0)
-
-    own(points, charges, lambda i: (i // BY + 1) * NX + i % BY + 1, near_sources, near_charge, near_targets)
-    region(from_down, YFAR, YNEAR, lambda i: (i + 1) * NX, near_sources, near_charge)
-    region(from_up, YFAR, YNEAR, lambda i: (i + 1) * NX + NX - 1, near_sources, near_charge)
-    region(from_left, XFAR, XNEAR, lambda i: i, near_sources, near_charge)
-    region(from_right, XFAR, XNEAR, lambda i: (NX - 1) * NX + i, near_sources, near_charge)
-    near_sources[NEAR_NULL] = jnp.zeros((32, 128), BF16)
-    near_charge[NEAR_NULL] = jnp.zeros((32, 128), BF16)
-    own(skeleton, coef, lambda i: (i // BY + 2) * FX + i % BY + 2, far_sources, far_charge, far_targets)
-    region(from_down, 0, YFAR, lambda i: (i // 2 + 2) * FX + i % 2, far_sources, far_charge)
-    region(from_up, 0, YFAR, lambda i: (i // 2 + 2) * FX + i % 2 + BY + 2, far_sources, far_charge)
-    region(from_left, 0, XFAR, lambda i: i, far_sources, far_charge)
-    region(from_right, 0, XFAR, lambda i: (BX + 2) * FX + i, far_sources, far_charge)
-
-    half = low_lanes(32)
-    half_sums = low_lanes(RHS)
-
-    def gathered(array, ids, slot, target):
-        four = [array[ids[slot + k, target]] for k in range(4)]
-        return jnp.concatenate([jnp.where(half, four[0], four[1]), jnp.where(half, four[2], four[3])], axis=1)
-
-    def entries_of(unit):
-        square = jnp.maximum(squares[unit], 1e-20)
-        scaled = square * lax.rsqrt(square)
-        high, low = halves((1.0 + scaled) * jnp.exp(-scaled))
-        entries[unit, 0:LEAF] = high
-        entries[unit, LEAF : 2 * LEAF] = low
-
-    def clear():
-        for unit in range(UNITS):
-            squares[unit] = jnp.full((LEAF, 4 * LEAF), 1e6, F32)
-            entries[unit] = jnp.zeros((2 * LEAF, 4 * LEAF), BF16)
-
-    def near_leaf(group, unit):
-        inner = unit * BZ + group + 1
-        outer = ((group - 6) * (COLS // 2) + unit // 2) * BZ + (unit % 2) * (BZ - 1)
-        return jnp.where(group < 6, inner, outer)
-
-    for group in range(8):
-        most = near_ids[28, near_leaf(group, 0)]
-        for unit in range(1, UNITS):
-            most = jnp.maximum(most, near_ids[28, near_leaf(group, unit)])
-        counts[group] = jnp.minimum((most + 3) // 4, 7)
-
-    def zero(i, carry):
-        sums[i] = jnp.zeros((RHS, 128), F32)
-        return carry
-
-    lax.fori_loop(0, HERE, zero, 0)
-    clear()
-    steps = counts[0]
-    for group in range(1, 8):
-        steps = steps + counts[group]
-
-    def near_step(step, state):
-        (group, part), later, last = state
-        for unit in range(UNITS):
-            target = near_leaf(last[0], unit)
-            product = dot(gathered(near_charge, near_ids, last[1] * 4, target), entries[unit], NT)
-            sums[target] = sums[target] + (product[:RHS] + product[RHS:])
-            entries_of(unit)
-            target = near_leaf(group, unit)
-            squares[unit] = dot(near_targets[target], gathered(near_sources, near_ids, part * 4, target))
-        over = part + 1 >= counts[group]
-        following = (
-            jnp.where(over, jnp.minimum(group + 1, 7), group),
-            jnp.where(over, 0, part + 1),
-        )
-        return following, (group, part), later
-
-    start = (jnp.int32(0), jnp.int32(0))
-    lax.fori_loop(0, steps + 2, near_step, (start, start, start))
-
-    def near_store(i, carry):
-        place = pl.ds(pl.multiple_of(i * 128, 128), 128)
-        first, second = sums[2 * i], sums[2 * i + 1]
-        first = first + pltpu.roll(first, LEAF, 1)
-        second = second + pltpu.roll(second, LEAF, 1)
-        near_out[:, place] = jnp.where(half_sums, first, second) + NUGGET * charges[:, place]
-        return carry
-
-    lax.fori_loop(0, HERE // 2, near_store, 0)
-
-    clear()
-
-    def far_step(step, carry):
-        after = jnp.minimum(step, HERE // 4 - 1) * 4
-        before = jnp.maximum(step - 2, 0) * 4
-        for i in range(4):
-            total = jnp.zeros((2 * RHS, 128), F32)
-            for part in range(4):
-                unit = i * 4 + part
-                total = total + dot(gathered(far_charge, far_ids, part * 4, before + i), entries[unit], NT)
-                entries_of(unit)
-                squares[unit] = dot(
-                    far_targets[after + i], gathered(far_sources, far_ids, part * 4, after + i)
-                )
-            sums[before + i] = total[:RHS] + total[RHS:]
-        return carry
-
-    lax.fori_loop(0, HERE // 4 + 2, far_step, 0)
+        lax.fori_loop(0, BZ, zero, 0)
+    sources[NEAR_NULL] = jnp.zeros((32, 128), BF16)
+    charge[NEAR_NULL] = jnp.zeros((32, 128), BF16)
+
+    def choose(step, unit):
+        code = work[phase, step * UNITS + unit]
+        return code >> 3, (code & 7) * 4
+
+    def add(step, unit, target, value):
+        sums[target] = sums[target] + value
+
+    steps = jnp.maximum((work[4 + phase, 0] + UNITS - 1) // UNITS, 1)
+    list_steps(steps, choose, near_ids, sources, charge, targets, squares, add)
+
+
+def folded(sums, pair):
+    first, second = sums[2 * pair], sums[2 * pair + 1]
+    first = first + pltpu.roll(first, LEAF, 1)
+    second = second + pltpu.roll(second, LEAF, 1)
+    return jnp.where(low_lanes(RHS), first, second)
+
+
+def near_store(cells, out, places, sums, charges):
+    for (x, y), to in zip(cells, places):
+        for pair in range(BZ // 2):
+            at = (x * BY + y) * COL + pair * 128
+            value = folded(sums, (x * BY + y) * (BZ // 2) + pair)
+            out[:, to * COL + pair * 128 : to * COL + pair * 128 + 128] = value + NUGGET * charges[:, at : at + 128]
+
+
+def near_own(points, charges, centre, sources, charge):
+    own_columns(points, charges, lambda i: (i // BY + 1) * NX + i % BY + 1, centre, sources, charge)
+
+
+def near_sides(from_down, from_up, centre, sources, charge):
+    region(from_down, YFAR, YNEAR, lambda i: (i + 1) * NX, centre, sources, charge)
+    region(from_up, YFAR, YNEAR, lambda i: (i + 1) * NX + NX - 1, centre, sources, charge)
+
+
+def inner_kernel(near_ids, work, points, charges, out, sources, charge, targets, squares, sums):
+    centre = centre_of()
+    near_own(points, charges, centre, sources, charge)
+    near_pass(0, INNER, near_ids, work, points, centre, sources, charge, targets, squares, sums)
+    near_store(INNER, out, range(4), sums, charges)
+
+
+def strip_kernel(
+    near_ids, work, points, charges, from_down, from_up, out, sources, charge, targets, squares, sums
+):
+    centre = centre_of()
+    near_own(points, charges, centre, sources, charge)
+    near_sides(from_down, from_up, centre, sources, charge)
+    near_pass(1, STRIP, near_ids, work, points, centre, sources, charge, targets, squares, sums)
+    near_store(STRIP, out, range(4), sums, charges)
+
+
+def rest_kernel(
+    near_ids, work, far_ids, points, charges, skeleton, coef, from_down, from_up, from_left, from_right,
+    inner, strip, near_out, far_out,
+    sources, charge, targets, far_sources, far_charge, far_targets, squares, sums,
+):
+    centre = centre_of()
+    near_own(points, charges, centre, sources, charge)
+    near_sides(from_down, from_up, centre, sources, charge)
+    region(from_left, XFAR, XNEAR, lambda i: i, centre, sources, charge)
+    region(from_right, XFAR, XNEAR, lambda i: (NX - 1) * NX + i, centre, sources, charge)
+    near_pass(2, RIM, near_ids, work, points, centre, sources, charge, targets, squares, sums)
+    near_store(RIM, near_out, [x * BY + y for x, y in RIM], sums, charges)
+    for cells, done in ((INNER, inner), (STRIP, strip)):
+        for i, (x, y) in enumerate(cells):
+            near_out[:, column(x * BY + y)] = done[:, i * COL : i * COL + COL]
+
+    own_columns(
+        skeleton, coef, lambda i: (i // BY + 2) * FX + i % BY + 2, centre, far_sources, far_charge
+    )
+
+    def target_step(i, carry):
+        build_targets(skeleton[:, column(i)], centre, far_targets, i * BZ)
+        return carry
+
+    lax.fori_loop(0, COLS, target_step, 0)
+    region(from_down, 0, YFAR, lambda i: (i // 2 + 2) * FX + i % 2, centre, far_sources, far_charge)
+    region(from_up, 0, YFAR, lambda i: (i // 2 + 2) * FX + i % 2 + BY + 2, centre, far_sources, far_charge)
+    region(from_left, 0, XFAR, lambda i: i, centre, far_sources, far_charge)
+    region(from_right, 0, XFAR, lambda i: (BX + 2) * FX + i, centre, far_sources, far_charge)
+
+    def choose(step, unit):
+        return step * (UNITS // 4) + unit // 4, unit % 4 * 4
+
+    def add(step, unit, target, value):
+        sums[target] = value if unit % 4 == 0 else sums[target] + value
+
+    list_steps(HERE * 4 // UNITS, choose, far_ids, far_sources, far_charge, far_targets, squares, add)
 
     def far_store(i, carry):
-        place = pl.ds(pl.multiple_of(i * 128, 128), 128)
-        first, second = sums[2 * i], sums[2 * i + 1]
-        first = first + pltpu.roll(first, LEAF, 1)
-        second = second + pltpu.roll(second, LEAF, 1)
-        far_out[:, place] = jnp.where(half_sums, first, second)
+        far_out[:, pl.ds(pl.multiple_of(i * 128, 128), 128)] = folded(sums, i)
         return carry
 
     lax.fori_loop(0, HERE // 2, far_store, 0)
@@ -436,13 +497,13 @@
         pairs = [(i, i + 1) for i in range(size - 1)]
         return lax.ppermute(array, axis, pairs if up else [(j, i) for i, j in pairs])
 
-    coef, device_row, near_ids, far_ids, send_down, send_up = pl.pallas_call(
+    coef, device_row, near_ids, far_ids, work, send_down, send_up = pl.pallas_call(
         first_kernel,
         in_specs=[VMEM] * 8,
-        out_specs=[VMEM] * 6,
+        out_specs=[VMEM] * 7,
         out_shape=[
             shape(RHS, here), shape(RHS, 128), shape(32, HERE, dtype=jnp.int32), shape(FAR, HERE, dtype=jnp.int32),
-            shape(ROWS, YCOLS * COL), shape(ROWS, YCOLS * COL),
+            shape(8, 512, dtype=jnp.int32), shape(ROWS, YCOLS * COL), shape(ROWS, YCOLS * COL),
         ],
         compiler_params=PARAMS,
         name="coefficients",
@@ -450,6 +511,29 @@
     every_row = lax.all_gather(device_row, ("top", "leaf"), axis=0)
     from_down = moved(send_up, "leaf", True)
     from_up = moved(send_down, "leaf", False)
+
+    def scratch(leaves):
+        return [
+            pltpu.VMEM((leaves, 32, 128), BF16),
+            pltpu.VMEM((leaves, 32, 128), BF16),
+            pltpu.VMEM((HERE, LEAF, 32), BF16),
+        ]
+
+    common = [pltpu.VMEM((UNITS, LEAF, 4 * LEAF), F32), pltpu.VMEM((HERE, RHS, 128), F32)]
+
+    def cost(us):
+        return pl.CostEstimate(flops=us * 10**9, bytes_accessed=10**6, transcendentals=0)
+
+    inner = pl.pallas_call(
+        inner_kernel,
+        in_specs=[SMEM] * 2 + [VMEM] * 2,
+        out_specs=VMEM,
+        out_shape=shape(RHS, 4 * COL),
+        scratch_shapes=scratch(NEAR_NULL + 1) + common,
+        compiler_params=PARAMS,
+        cost_estimate=cost(13),
+        name="inner",
+    )(near_ids, work, points, charges)
     send_left, send_right = pl.pallas_call(
         side_kernel,
         in_specs=[VMEM] * 6,
@@ -460,27 +544,29 @@
     )(points, charges, leaf_skeleton, coef, from_down, from_up)
     from_left = moved(send_right, "top", True)
     from_right = moved(send_left, "top", False)
+    strip = pl.pallas_call(
+        strip_kernel,
+        in_specs=[SMEM] * 2 + [VMEM] * 4,
+        out_specs=VMEM,
+        out_shape=shape(RHS, 4 * COL),
+        scratch_shapes=scratch(NEAR_NULL + 1) + common,
+        compiler_params=PARAMS,
+        cost_estimate=cost(13),
+        name="strip",
+    )(near_ids, work, points, charges, from_down, from_up)
     near, far = pl.pallas_call(
-        main_kernel,
-        in_specs=[SMEM] * 2 + [VMEM] * 8,
+        rest_kernel,
+        in_specs=[SMEM] * 3 + [VMEM] * 10,
         out_specs=[VMEM] * 2,
         out_shape=[shape(RHS, here), shape(RHS, here)],
-        scratch_shapes=[
-            pltpu.VMEM((NEAR_NULL + 1, 32, 128), BF16),
-            pltpu.VMEM((NEAR_NULL + 1, 32, 128), BF16),
-            pltpu.VMEM((HERE, LEAF, 32), BF16),
-            pltpu.VMEM((FAR_ALL, 32, 128), BF16),
-            pltpu.VMEM((FAR_ALL, 32, 128), BF16),
-            pltpu.VMEM((HERE, LEAF, 32), BF16),
-            pltpu.VMEM((UNITS, LEAF, 4 * LEAF), F32),
-            pltpu.VMEM((UNITS, 2 * LEAF, 4 * LEAF), BF16),
-            pltpu.VMEM((HERE, RHS, 128), F32),
-            pltpu.SMEM((8,), jnp.int32),
-        ],
+        scratch_shapes=scratch(NEAR_NULL + 1) + scratch(FAR_ALL) + common,
         compiler_params=PARAMS,
-        cost_estimate=pl.CostEstimate(flops=10**11, bytes_accessed=10**7, transcendentals=4 * 10**7),
-        name="lists",
-    )(near_ids, far_ids, points, charges, leaf_skeleton, coef, from_down, from_up, from_left, from_right)
+        cost_estimate=cost(55),
+        name="rest",
+    )(
+        near_ids, work, far_ids, points, charges, leaf_skeleton, coef, from_down, from_up, from_left, from_right,
+        inner, strip,
+    )
     return pl.pallas_call(
         last_kernel,
         in_specs=[SMEM] + [VMEM] * 8,

time: 160 us -> 131 us (0.82); the launches traced: 157 us -> 130 us
  waiting for transfers between devices: 29.3 us -> 5.32 us
  local copies, waits for them, and re-layouts: 8.64 us -> 4.18 us
    ppermute x4, waiting for transfers between devices: 29.3 us -> 5.3 us  [moved(): lax.ppermute(array, axis, pairs if up else [(j, i) for i, j in pairs])]
    unnamed x33 -> x15, local copies, waits for them, and re-layouts: 8.26 us -> 2.48 us
    pallas_call x2 -> x4, Pallas kernels: 84.1 us -> 83.3 us  [the longest x1 52.3 us: body(): pl.pallas_call(rest_kernel, in_specs=[SMEM] * 3 + [VMEM] * 10, out_specs=...]
  transfers between devices with their start and end apart: 5 -> 5, of which waited for: 4 -> 2; matrix products, arithmetic and copies ran while one was open for 0% -> 2% of each run, Pallas kernels for 49% -> 60%
where the time goes in v2:
time: 131 us; the launch traced here: 130 us
  Pallas kernels  94.9 us (72%)
  between operations  13.5 us (10%)
  starting transfers between devices  12 us (9%)
  waiting for transfers between devices  5.32 us (4%)
  local copies, waits for them, and re-layouts  4.18 us (3%)
    pallas_call x1, Pallas kernels, body(): pl.pallas_call(rest_kernel, in_specs=[SMEM] * 3 + [VMEM] * 10, out_specs=...  52.3 us
    pallas_call x1, Pallas kernels, body(): pl.pallas_call(strip_kernel, in_specs=[SMEM] * 2 + [VMEM] * 4, out_specs=...  12.2 us
    ppermute x4, starting transfers between devices, moved(): lax.ppermute(array, axis, pairs if up else [(j, i) for i, j in pairs])  12 us
    pallas_call x1, Pallas kernels, body(): pl.pallas_call(inner_kernel, in_specs=[SMEM] * 2 + [VMEM] * 2, out_specs=...  10.2 us
    pallas_call x1, Pallas kernels, body(): pl.pallas_call(last_kernel, in_specs=[SMEM] + [VMEM] * 8, out_specs=VMEM,...  8.59 us
    pallas_call x1, Pallas kernels, body(): pl.pallas_call(first_kernel, in_specs=[VMEM] * 8, out_specs=[VMEM] * 7, o...  8.51 us
    ppermute x4, waiting for transfers between devices, moved(): lax.ppermute(array, axis, pairs if up else [(j, i) for i, j in pairs])  5.3 us
    pallas_call x1, Pallas kernels, body(): pl.pallas_call(side_kernel, in_specs=[VMEM] * 6, out_specs=[VMEM] * 2, ou...  3.07 us
  transfers between devices with their start and end apart: 5, of which 2 were waited for; matrix products, arithmetic and copies ran while one was open for 2% of the time, Pallas kernels for 60%

profile of v2, /device:TPU:107, one launch (start us, length us, event | category | flops | bytes accessed | tf_op | source)
XLA Modules:
  0.0 129.9 jit_solution(1913136516220255146)
XLA Ops:
  6.5 0.0 all-gather.3.cloned.1.call-start
  6.5 8.5 %coefficients.1 = (f32[16,8192]{1,0:T(8,128)}, f32[16,128]{1,0:T(8,128)}, s32[32,128]{1,0:T(8,128)}, s32[16,128]{1,0:T(8,128)}, s32[8,512]{1,0:T(8,128)}, /*index=5*/f32[19,6144]{1,0:T(8,128)}, f32[19,6144]{1,0:T(8,128)}) custom-call(f32[3,8192]{1,0:T(4,128)} %points.9, f32[16,8192]{1,0:T(8,128)} %charges.9, s32[27,128]{1,0:T(8,128)} %near_list.1, ...), custom_call_target="tpu_custom_call" | custom-call | tf_op jit(solution)/shard_map/coefficients/pallas_call | solution.py:500
  15.0 1.9 %collective-permute-start = (f32[19,6144]{1,0:T(8,128)}, f32[19,6144]{1,0:T(8,128)S(1)}, u32[]{:S(2)}, u32[]{:S(2)}) collective-permute-start(f32[19,6144]{1,0:T(8,128)} %get-tuple-element.21), channel_id=1, source_target_pairs={{0,1},{1,2},{2,3},{3,4},{4,5},{5,6},{6,7},{7,8},{8,9},{9,10},{10,1... | collective-permute-start | bytes 1400840 | tf_op jit(solution)/shard_map/ppermute | solution.py:498
  17.0 3.4 %collective-permute-start.1 = (f32[19,6144]{1,0:T(8,128)}, f32[19,6144]{1,0:T(8,128)S(1)}, u32[]{:S(2)}, u32[]{:S(2)}) collective-permute-start(f32[19,6144]{1,0:T(8,128)} %get-tuple-element.22), channel_id=1, source_target_pairs={{1,0},{2,1},{3,2},{4,3},{5,4},{6,5},{7,6},{8,7},{9,8},{10,9},{11,1... | collective-permute-start | bytes 1400840 | tf_op jit(solution)/shard_map/ppermute | solution.py:498
  20.3 0.0 all-gather.3.cloned.1.call-update
  20.4 0.0 copy-start.2
  20.4 0.0 copy-start.3
  20.4 0.0 copy-start.4
  20.4 10.2 %inner.1 = f32[16,2048]{1,0:T(8,128)} custom-call(s32[32,128]{1,0:T(8,128)} %get-tuple-element.17.near_ids, s32[8,512]{1,0:T(8,128)} %get-tuple-element.18.work, f32[3,8192]{1,0:T(4,128)} %points.9, f32[16,8192]{1,0:T(8,128)} %charges.9), custom_call_target="tpu_custom_call" | custom-call | flops 12999999488 | bytes 1000000 | tf_op jit(solution)/shard_map/inner/pallas_call | solution.py:527
  30.6 0.0 copy-done.2
  30.6 0.2 reshape.6
  30.8 0.9 copy.18
  31.7 0.0 copy-done.3
  31.7 0.1 reshape.7
  31.7 0.6 copy.19
  32.3 0.0 copy-done.4
  32.3 0.7 copy.15.device_far
  33.0 0.0 collective-permute-done.from_down
  33.0 0.0 copy-start
  33.0 2.1 %collective-permute-done.1.from_up = f32[19,6144]{1,0:T(8,128)S(1)} collective-permute-done((f32[19,6144]{1,0:T(8,128)}, f32[19,6144]{1,0:T(8,128)S(1)}, u32[]{:S(2)}, u32[]{:S(2)}) %collective-permute-start.1) | collective-permute-done | bytes 466976 | tf_op jit(solution)/shard_map/ppermute | solution.py:498
  35.1 0.0 copy-done
  35.1 0.8 copy-done.1
  35.9 3.1 %sides.1 = (f32[19,11264]{1,0:T(8,128)}, f32[19,11264]{1,0:T(8,128)}) custom-call(f32[3,8192]{1,0:T(4,128)} %points.9, f32[16,8192]{1,0:T(8,128)} %charges.9, f32[3,8192]{1,0:T(4,128)} %skeleton.5, f32[16,8192]{1,0:T(8,128)} %get-tuple-element.20.coef, f32[19,6144]{1,0:T(8,128)} %copy-done, f32[19,6144]{1,0:T(8,128)} %copy-done.1), custom_call_target="tpu_custom_call" | custom-call | tf_op jit(solution)/shard_map/sides/pallas_call | solution.py:537
  39.0 4.8 %collective-permute-start.2 = (f32[19,11264]{1,0:T(8,128)}, f32[19,11264]{1,0:T(8,128)S(1)}, u32[]{:S(2)}, u32[]{:S(2)}) collective-permute-start(f32[19,11264]{1,0:T(8,128)} %get-tuple-element.23), channel_id=1, source_target_pairs={{0,16},{16,32},{32,48},{48,64},{64,80},{80,96},{96,112},{1,17},{17... | collective-permute-start | bytes 2568200 | tf_op jit(solution)/shard_map/ppermute | solution.py:498
  43.8 1.9 %collective-permute-start.3 = (f32[19,11264]{1,0:T(8,128)}, f32[19,11264]{1,0:T(8,128)S(1)}, u32[]{:S(2)}, u32[]{:S(2)}) collective-permute-start(f32[19,11264]{1,0:T(8,128)} %get-tuple-element.24), channel_id=1, source_target_pairs={{16,0},{32,16},{48,32},{64,48},{80,64},{96,80},{112,96},{17,1},{33... | collective-permute-start | bytes 2568200 | tf_op jit(solution)/shard_map/ppermute | solution.py:498
  45.7 12.2 %strip.1 = f32[16,2048]{1,0:T(8,128)} custom-call(s32[32,128]{1,0:T(8,128)} %get-tuple-element.17.near_ids, s32[8,512]{1,0:T(8,128)} %get-tuple-element.18.work, f32[3,8192]{1,0:T(4,128)} %points.9, f32[16,8192]{1,0:T(8,128)} %charges.9, f32[19,6144]{1,0:T(8,128)} %copy-done, f32[19,6144]{1,0:T(8,128)} %copy-done.1), custom_call_target="tpu_custom_call" | custom-call | flops 12999999488 | bytes 1000000 | tf_op jit(solution)/shard_map/strip/pallas_call | solution.py:547
  57.9 0.0 collective-permute-done.2.from_left
  58.0 3.2 %collective-permute-done.3.from_right = f32[19,11264]{1,0:T(8,128)S(1)} collective-permute-done((f32[19,11264]{1,0:T(8,128)}, f32[19,11264]{1,0:T(8,128)S(1)}, u32[]{:S(2)}, u32[]{:S(2)}) %collective-permute-start.3) | collective-permute-done | bytes 856096 | tf_op jit(solution)/shard_map/ppermute | solution.py:498
  61.1 0.0 copy-done.5
  61.1 1.0 copy-done.6
  62.1 52.3 %rest.1 = (f32[16,8192]{1,0:T(8,128)}, f32[16,8192]{1,0:T(8,128)}) custom-call(s32[32,128]{1,0:T(8,128)} %get-tuple-element.17.near_ids, s32[8,512]{1,0:T(8,128)} %get-tuple-element.18.work, s32[16,128]{1,0:T(8,128)} %get-tuple-element.19.far_ids, f32[3,8192]{1,0:T(4,128)} %points.9, f32[16,8192]{1,0:T(8,128)} %charges.9, f32[3,8192]{1,0:T(4,128)} %skeleton.5, ...), custom_call_target="tpu_custom_call" | custom-call | flops 54999998464 | bytes 1000000 | tf_op jit(solution)/shard_map/rest/pallas_call | solution.py:557
  114.4 8.6 %fields.1 = f32[16,8192]{1,0:T(8,128)} custom-call(s32[4,1]{1,0:T(4,128)} %copy.15.device_far, f32[128,16,128]{2,1,0:T(8,128)} %bitcast.7, f32[128,3,64]{2,1,0:T(4,128)} %bitcast.8, f32[8,3,64]{2,1,0:T(4,128)} %bitcast.9, f32[64,64]{1,0:T(8,128)} %branch_transfer.3, f32[64,8192]{1,0:T(8,128)} %transfer.3, f32[64,8192]{1,0:T(8,128)} %basis.3, ...), custom_call_target="tpu_custom_call" | custom-call | tf_op jit(solution)/shard_map/fields/pallas_call | solution.py:570
  (4 shorter events, 0.0 us)
Async XLA Ops:
  6.5 107.9 %all-gather.3.cloned.1.call-start = ((), (), s32[]{:S(2)}) async-start(), calls=%async_computation | async-start | bytes 1056768 | tf_op jit(solution)/shard_map/all_gather | solution.py:511
  15.0 18.0 %collective-permute-start = (f32[19,6144]{1,0:T(8,128)}, f32[19,6144]{1,0:T(8,128)S(1)}, u32[]{:S(2)}, u32[]{:S(2)}) collective-permute-start(f32[19,6144]{1,0:T(8,128)} %get-tuple-element.21), channel_id=1, source_target_pairs={{0,1},{1,2},{2,3},{3,4},{4,5},{5,6},{6,7},{7,8},{8,9},{9,10},{10,1... | collective-permute-start | bytes 1400840 | tf_op jit(solution)/shard_map/ppermute | solution.py:498
  17.0 18.2 %collective-permute-start.1 = (f32[19,6144]{1,0:T(8,128)}, f32[19,6144]{1,0:T(8,128)S(1)}, u32[]{:S(2)}, u32[]{:S(2)}) collective-permute-start(f32[19,6144]{1,0:T(8,128)} %get-tuple-element.22), channel_id=1, source_target_pairs={{1,0},{2,1},{3,2},{4,3},{5,4},{6,5},{7,6},{8,7},{9,8},{10,9},{11,1... | collective-permute-start | bytes 1400840 | tf_op jit(solution)/shard_map/ppermute | solution.py:498
  20.4 10.3 %copy-start.2 = (f32[3,8192]{1,0:T(4,128)S(1)}, f32[3,8192]{1,0:T(4,128)}, u32[]{:S(2)}) copy-start(f32[3,8192]{1,0:T(4,128)} %param.20) | copy-start | bytes 294916
  20.4 11.3 %copy-start.3 = (f32[3,512]{1,0:T(4,128)S(1)}, f32[3,512]{1,0:T(4,128)}, u32[]{:S(2)}) copy-start(f32[3,512]{1,0:T(4,128)} %param.21) | copy-start | bytes 18436
  20.4 12.0 %copy-start.4 = (s32[4,1]{0,1:T(1,128)S(1)}, s32[4,1]{0,1:T(1,128)}, u32[]{:S(2)}) copy-start(s32[4,1]{0,1:T(1,128)} %param.18) | copy-start | bytes 52
  33.0 2.1 %copy-start = (f32[19,6144]{1,0:T(8,128)}, f32[19,6144]{1,0:T(8,128)S(1)}, u32[]{:S(2)}) copy-start(f32[19,6144]{1,0:T(8,128)S(1)} %collective-permute-done.from_down) | copy-start | bytes 1400836
  35.1 0.8 copy-start.1
  39.0 18.9 %collective-permute-start.2 = (f32[19,11264]{1,0:T(8,128)}, f32[19,11264]{1,0:T(8,128)S(1)}, u32[]{:S(2)}, u32[]{:S(2)}) collective-permute-start(f32[19,11264]{1,0:T(8,128)} %get-tuple-element.23), channel_id=1, source_target_pairs={{0,16},{16,32},{32,48},{48,64},{64,80},{80,96},{96,112},{1,17},{17... | collective-permute-start | bytes 2568200 | tf_op jit(solution)/shard_map/ppermute | solution.py:498
  43.8 17.3 %collective-permute-start.3 = (f32[19,11264]{1,0:T(8,128)}, f32[19,11264]{1,0:T(8,128)S(1)}, u32[]{:S(2)}, u32[]{:S(2)}) collective-permute-start(f32[19,11264]{1,0:T(8,128)} %get-tuple-element.24), channel_id=1, source_target_pairs={{16,0},{32,16},{48,32},{64,48},{80,64},{96,80},{112,96},{17,1},{33... | collective-permute-start | bytes 2568200 | tf_op jit(solution)/shard_map/ppermute | solution.py:498
  58.0 3.2 %copy-start.5 = (f32[19,11264]{1,0:T(8,128)}, f32[19,11264]{1,0:T(8,128)S(1)}, u32[]{:S(2)}) copy-start(f32[19,11264]{1,0:T(8,128)S(1)} %collective-permute-done.2.from_left) | copy-start | bytes 2568196
  61.1 1.0 copy-start.6
Sparse Core Ops, SparseCore 0:
  20.5 62.2 all-gather.2

commit v3 on v2

v3 whole, which is shorter than its diff:
```python
import jax
import jax.numpy as jnp
from jax import lax
from jax.experimental import pallas as pl
from jax.experimental.pallas import tpu as pltpu
from jax.sharding import PartitionSpec as P

LEAF = 64
RANK = 64
RHS = 16
BX = 4
BY = 4
BZ = 8
COLS = BX * BY
COL = BZ * LEAF
HERE = COLS * BZ
NEAR = 27
FAR = 16
NX = BX + 2
FX = BX + 4
NEAR_NULL = NX * NX * BZ
FAR_ALL = FX * FX * BZ
YFAR, YNEAR = 2 * BX, BX
XFAR, XNEAR = 2 * FX, NX
YCOLS = YFAR + YNEAR
XCOLS = XFAR + XNEAR
YLANES = (YCOLS + (YCOLS + 3) // 4) * COL
XLANES = (XCOLS + (XCOLS + 3) // 4) * COL
UNITS = 32
BLOCK = 1024
INNER = ((1, 1), (1, 2), (2, 1), (2, 2))
STRIP = ((1, 0), (1, 3), (2, 0), (2, 3))
RIM = tuple((x, y) for x in (0, 3) for y in range(4))

EXACT = lax.Precision.HIGHEST
KERNEL_SCALE = 3.4641016151377544
LOG2E = 1.4426950408889634
SIGNAL = 0.0625
NUGGET = 0.25
BF16 = jnp.bfloat16
F32 = jnp.float32
NT = (((1,), (1,)), ((), ()))
NN = (((1,), (0,)), ((), ()))
VMEM = pl.BlockSpec(memory_space=pltpu.VMEM)
SMEM = pl.BlockSpec(memory_space=pltpu.SMEM)


def room(mib):
    return pltpu.CompilerParams(vmem_limit_bytes=mib * 2**20)


def dot(a, b, dims=NN):
    return lax.dot_general(a, b, dims, preferred_element_type=F32)


def halves(value):
    high = value.astype(BF16)
    return high, (value - high.astype(F32)).astype(BF16)


def low_lanes(rows):
    return lax.broadcasted_iota(jnp.int32, (rows, 128), 1) < LEAF


def column(index):
    return pl.ds(pl.multiple_of(index * COL, COL), COL)


def coords_at(array, columns, index, odd):
    row = pl.ds(pl.multiple_of(index // 2 % 2 * 8, 8), 8)
    return array[row, column(columns + index // 4)][3 * odd : 3 * odd + 3]


def set_coords(array, columns, index, value):
    row = index // 2 % 2 * 8 + index % 2 * 3
    array[row : row + 3, column(columns + index // 4)] = value


def window_ids(ids, width, span, top, leaf, null):
    wx = ((ids >> 11) - top) * BX + ((ids >> 5) & 3) + width
    wy = (((ids >> 7) & 15) - leaf) * BY + ((ids >> 3) & 3) + width
    place = (wx * span + wy) * BZ + (ids & 7)
    place = jnp.minimum(jnp.maximum(place, 0), span * span * BZ - 1)
    return jnp.where(ids >= 0, place, null)


def work_lists(used, work):
    lane = lax.broadcasted_iota(jnp.int32, (1, HERE), 1)
    inner_x = (((lane >> 5) + 1) & 2) != 0
    inner_y = ((((lane >> 3) & 3) + 1) & 2) != 0
    member = jnp.where(inner_x, jnp.where(inner_y, 0, 1), 2)
    parts = (used + 3) >> 2
    first = lax.broadcasted_iota(jnp.int32, (HERE, HERE), 0)
    second = lax.broadcasted_iota(jnp.int32, (HERE, HERE), 1)
    place = lax.broadcasted_iota(jnp.int32, (HERE, 512), 1)
    for phase in range(3):
        kept = jnp.where(member == phase, parts, 0)
        end = jnp.sum(jnp.where(second <= first, kept, 0), axis=1, keepdims=True)
        count = jnp.sum(jnp.where(second == first, kept, 0), axis=1, keepdims=True)
        passed = end <= place
        leaf = jnp.sum(jnp.where(passed, 1, 0), axis=0, keepdims=True)
        start = jnp.sum(jnp.where(passed, count, 0), axis=0, keepdims=True)
        code = leaf * 8 + (place[:1] - start)
        work[phase : phase + 1] = jnp.where(leaf < HERE, code, 7)
        work[4 + phase : 5 + phase] = jnp.zeros((1, 512), jnp.int32) + jnp.sum(kept, axis=1, keepdims=True)


def first_kernel(
    points, charges, near_list, far_list, basis, transfer, skeleton, branch_transfer,
    coef, device_row, near_ids, far_ids, work, send_down, send_up, total,
):
    lane = lax.broadcasted_iota(jnp.int32, (2 * RHS, 4 * LEAF), 1) // LEAF
    half = low_lanes(RHS)
    together = BLOCK // 256
    index = pl.program_id(0)

    places, products = [], []
    for part in range(together):
        place = pl.ds(pl.multiple_of(index * BLOCK + part * 256, 256), 256)
        here = slice(part * 256, part * 256 + 256)
        places.append((place, here))
        q_high, q_low = halves(charges[:, place])
        q = jnp.concatenate([q_high, q_low], axis=0)
        zero = jnp.zeros_like(q)
        rows = jnp.concatenate([jnp.where(lane == i, q, zero) for i in range(4)], axis=0)
        b_high, b_low = halves(basis[:, here])
        products.append(
            dot(rows, jnp.concatenate([b_high, b_high], axis=0), NT)
            + dot(rows, jnp.concatenate([b_low, b_low], axis=0), NT)
        )
    sums = []
    for (place, here), product in zip(places, products):
        each = [product[32 * i : 32 * i + 16] + product[32 * i + 16 : 32 * i + 32] for i in range(4)]
        value = jnp.concatenate(
            [jnp.where(half, each[0], each[1]), jnp.where(half, each[2], each[3])], axis=1
        )
        coef[:, place] = value
        c = jnp.concatenate(halves(value), axis=0)
        t_high, t_low = halves(transfer[:, here])
        sums.append(dot(c, t_high, NT) + dot(c, t_low, NT))

    @pl.when(index == 0)
    def start():
        total[...] = jnp.zeros((2 * RHS, LEAF), F32)

    total[...] = total[...] + sum(sums[1:], sums[0])

    @pl.when(index == HERE * LEAF // BLOCK - 1)
    def finish():
        top, leaf = lax.axis_index("top"), lax.axis_index("leaf")
        listed = near_list[...]
        near_ids[0:NEAR] = window_ids(listed, 1, NX, top, leaf, NEAR_NULL)
        near_ids[NEAR:32] = jnp.full((5, HERE), NEAR_NULL, jnp.int32)
        work_lists(jnp.sum((listed >= 0).astype(jnp.int32), axis=0, keepdims=True), work)
        far_ids[...] = window_ids(far_list[...], 2, FX, top, leaf, 0)

        own = total[0:RHS] + total[RHS : 2 * RHS]
        raised = lax.dot_general(own, branch_transfer[...], NT, precision=EXACT, preferred_element_type=F32)
        device_row[...] = jnp.concatenate([own, raised], axis=1)

        def fill(target, near_y, far_y):
            for x in range(BX):
                for y in range(2):
                    at = column(x * BY + far_y + y)
                    target[:, column(x * 2 + y)] = coef[:, at]
                    set_coords(target, YCOLS, x * 2 + y, skeleton[:, at])
                at = column(x * BY + near_y)
                target[:, column(YFAR + x)] = charges[:, at]
                set_coords(target, YCOLS, YFAR + x, points[:, at])

        blank = jnp.zeros((RHS, YLANES - YCOLS * COL), F32)
        send_down[:, YCOLS * COL : YLANES] = blank
        send_up[:, YCOLS * COL : YLANES] = blank
        fill(send_down, 0, 0)
        fill(send_up, BY - 1, BY - 2)


def side_kernel(points, charges, skeleton, coef, from_down, from_up, send_left, send_right):
    def fill(target, near_x, far_x):
        def put(index, values, coords):
            target[:, column(index)] = values
            set_coords(target, XCOLS, index, coords)

        def side(index, array, at):
            put(index, array[:, column(at)], coords_at(array, YCOLS, at, at % 2))

        for x in range(2):
            at_x = far_x + x
            for y in range(2):
                side(x * FX + y, from_down, at_x * 2 + y)
                side(x * FX + y + BY + 2, from_up, at_x * 2 + y)
            for y in range(BY):
                at = column(at_x * BY + y)
                put(x * FX + 2 + y, coef[:, at], skeleton[:, at])
        side(XFAR, from_down, YFAR + near_x)
        side(XFAR + BY + 1, from_up, YFAR + near_x)
        for y in range(BY):
            at = column(near_x * BY + y)
            put(XFAR + 1 + y, charges[:, at], points[:, at])

    blank = jnp.zeros((RHS, XLANES - XCOLS * COL), F32)
    send_left[:, XCOLS * COL : XLANES] = blank
    send_right[:, XCOLS * COL : XLANES] = blank
    fill(send_left, 0, 0)
    fill(send_right, BX - 1, BX - 2)


def pieces_of(coords, centre):
    place = (coords - centre) * KERNEL_SCALE
    high = place.astype(BF16).astype(F32)
    rest = place - high
    mid = rest.astype(BF16).astype(F32)
    norm = jnp.sum(place * place, axis=0, keepdims=True)
    norm_high = norm.astype(BF16).astype(F32)
    norm_rest = norm - norm_high
    norm_mid = norm_rest.astype(BF16).astype(F32)
    return high, mid, rest - mid, norm_high, norm_mid, norm_rest - norm_mid


def build_column(coords, values, centre, col, sources, charge):
    high, mid, low, norm_high, norm_mid, norm_low = pieces_of(coords, centre)
    one = jnp.ones_like(norm_high)
    empty = jnp.zeros((8, 128), BF16)
    rows = jnp.concatenate([high, high, norm_high, norm_mid, high, mid, norm_low, one, mid, low, one, one], axis=0)
    half = low_lanes(24)
    half_values = low_lanes(RHS)
    scaled = values * SIGNAL
    for pair in range(BZ // 2):
        lanes = slice(pair * 128, pair * 128 + 128)
        tile, tile_values = rows[:, lanes], scaled[:, lanes]
        turned, turned_values = pltpu.roll(tile, LEAF, 1), pltpu.roll(tile_values, LEAF, 1)
        at = col * BZ + 2 * pair
        sources[at] = jnp.concatenate([jnp.where(half, tile, turned).astype(BF16), empty], axis=0)
        sources[at + 1] = jnp.concatenate([jnp.where(half, turned, tile).astype(BF16), empty], axis=0)
        charge[at] = jnp.concatenate(halves(jnp.where(half_values, tile_values, turned_values)), axis=0)
        charge[at + 1] = jnp.concatenate(halves(jnp.where(half_values, turned_values, tile_values)), axis=0)


def build_targets(coords, centre, targets, leaf):
    high, mid, low, norm_high, norm_mid, norm_low = pieces_of(coords, centre)
    one = jnp.ones_like(norm_high)
    rows = jnp.concatenate(
        [
            -2.0 * high, -2.0 * mid, one, one, -2.0 * low, -2.0 * high, one, norm_high,
            -2.0 * mid, -2.0 * high, norm_mid, norm_low, jnp.zeros((8, COL), F32),
        ],
        axis=0,
    )
    for pair in range(BZ // 2):
        tile = rows[:, pair * 128 : pair * 128 + 128].T.astype(BF16)
        targets[leaf + 2 * pair] = tile[:LEAF]
        targets[leaf + 2 * pair + 1] = tile[LEAF:]


def centre_of():
    top, leaf = lax.axis_index("top"), lax.axis_index("leaf")
    row = lax.broadcasted_iota(jnp.int32, (3, COL), 0)
    return jnp.where(row == 0, top.astype(F32) + 0.5, jnp.where(row == 1, leaf.astype(F32) + 0.5, 1.0))


def region(array, columns, first, count, to, centre, sources, charge):
    def step(half, carry):
        for odd in range(2):
            i = 2 * half + odd
            coords = coords_at(array, columns, first + i, odd)
            build_column(coords, array[:, column(first + i)], centre, to(i), sources, charge)
        return carry

    lax.fori_loop(0, count // 2, step, 0)


def own_columns(coords, values, to, centre, sources, charge):
    def step(half, carry):
        for i in (2 * half, 2 * half + 1):
            at = column(i)
            build_column(coords[:, at], values[:, at], centre, to(i), sources, charge)
        return carry

    lax.fori_loop(0, COLS // 2, step, 0)


def gathered(array, ids, slot, target):
    half = low_lanes(32)
    four = [array[ids[slot + k, target]] for k in range(4)]
    return jnp.concatenate([jnp.where(half, four[0], four[1]), jnp.where(half, four[2], four[3])], axis=1)


def entries_of(square):
    square = jnp.maximum(square, 1e-20)
    scaled = square * lax.rsqrt(square)
    decay = jnp.exp2(scaled * -LOG2E)
    return jnp.concatenate(halves(decay + scaled * decay), axis=0)


def list_steps(steps, choose, ids, sources, charge, targets, squares, add):
    def distances(step, unit):
        target, slot = choose(step, unit)
        squares[unit] = dot(targets[target], gathered(sources, ids, slot, target))

    for unit in range(UNITS):
        distances(0, unit)

    def run(step, carry):
        waiting = None
        for unit in range(UNITS + 1):
            if unit < UNITS:
                entries = entries_of(squares[unit])
                distances(jnp.minimum(step + 1, steps - 1), unit)
            if waiting is not None:
                target, slot = choose(step, unit - 1)
                product = dot(gathered(charge, ids, slot, target), waiting, NT)
                add(step, unit - 1, target, product[:RHS] + product[RHS:])
            waiting = entries
        return carry

    lax.fori_loop(0, steps, run, 0)


def near_pass(phase, cells, near_ids, work, points, centre, sources, charge, targets, squares, sums):
    for x, y in cells:
        col = x * BY + y
        build_targets(points[:, col * COL : col * COL + COL], centre, targets, col * BZ)

        def zero(i, carry, first=col * BZ):
            sums[first + i] = jnp.zeros((RHS, 128), F32)
            return carry

        lax.fori_loop(0, BZ, zero, 0)
    sources[NEAR_NULL] = jnp.zeros((32, 128), BF16)
    charge[NEAR_NULL] = jnp.zeros((32, 128), BF16)

    def choose(step, unit):
        code = work[phase, step * UNITS + unit]
        return code >> 3, (code & 7) * 4

    def add(step, unit, target, value):
        sums[target] = sums[target] + value

    steps = jnp.maximum((work[4 + phase, 0] + UNITS - 1) // UNITS, 1)
    list_steps(steps, choose, near_ids, sources, charge, targets, squares, add)


def folded(sums, pair):
    first, second = sums[2 * pair], sums[2 * pair + 1]
    first = first + pltpu.roll(first, LEAF, 1)
    second = second + pltpu.roll(second, LEAF, 1)
    return jnp.where(low_lanes(RHS), first, second)


def near_store(cells, out, places, sums, charges):
    for (x, y), to in zip(cells, places):
        for pair in range(BZ // 2):
            at = (x * BY + y) * COL + pair * 128
            value = folded(sums, (x * BY + y) * (BZ // 2) + pair)
            out[:, to * COL + pair * 128 : to * COL + pair * 128 + 128] = value + NUGGET * charges[:, at : at + 128]


def near_own(points, charges, centre, sources, charge):
    own_columns(points, charges, lambda i: (i // BY + 1) * NX + i % BY + 1, centre, sources, charge)


def near_sides(from_down, from_up, centre, sources, charge):
    region(from_down, YCOLS, YFAR, YNEAR, lambda i: (i + 1) * NX, centre, sources, charge)
    region(from_up, YCOLS, YFAR, YNEAR, lambda i: (i + 1) * NX + NX - 1, centre, sources, charge)


def inner_kernel(near_ids, work, points, charges, out, sources, charge, targets, squares, sums):
    centre = centre_of()
    near_own(points, charges, centre, sources, charge)
    near_pass(0, INNER, near_ids, work, points, centre, sources, charge, targets, squares, sums)
    near_store(INNER, out, range(4), sums, charges)


def strip_kernel(
    near_ids, work, points, charges, from_down, from_up, out, sources, charge, targets, squares, sums
):
    centre = centre_of()
    near_own(points, charges, centre, sources, charge)
    near_sides(from_down, from_up, centre, sources, charge)
    near_pass(1, STRIP, near_ids, work, points, centre, sources, charge, targets, squares, sums)
    near_store(STRIP, out, range(4), sums, charges)


def rest_kernel(
    near_ids, work, far_ids, points, charges, skeleton, coef, from_down, from_up, from_left, from_right,
    inner, strip, near_out, far_out,
    sources, charge, targets, far_sources, far_charge, far_targets, squares, sums,
):
    centre = centre_of()
    near_own(points, charges, centre, sources, charge)
    near_sides(from_down, from_up, centre, sources, charge)
    region(from_left, XCOLS, XFAR, XNEAR, lambda i: i, centre, sources, charge)
    region(from_right, XCOLS, XFAR, XNEAR, lambda i: (NX - 1) * NX + i, centre, sources, charge)
    near_pass(2, RIM, near_ids, work, points, centre, sources, charge, targets, squares, sums)
    near_store(RIM, near_out, [x * BY + y for x, y in RIM], sums, charges)
    for cells, done in ((INNER, inner), (STRIP, strip)):
        for i, (x, y) in enumerate(cells):
            near_out[:, column(x * BY + y)] = done[:, i * COL : i * COL + COL]

    own_columns(
        skeleton, coef, lambda i: (i // BY + 2) * FX + i % BY + 2, centre, far_sources, far_charge
    )

    def target_step(i, carry):
        build_targets(skeleton[:, column(i)], centre, far_targets, i * BZ)
        return carry

    lax.fori_loop(0, COLS, target_step, 0)
    region(from_down, YCOLS, 0, YFAR, lambda i: (i // 2 + 2) * FX + i % 2, centre, far_sources, far_charge)
    region(from_up, YCOLS, 0, YFAR, lambda i: (i // 2 + 2) * FX + i % 2 + BY + 2, centre, far_sources, far_charge)
    region(from_left, XCOLS, 0, XFAR, lambda i: i, centre, far_sources, far_charge)
    region(from_right, XCOLS, 0, XFAR, lambda i: (BX + 2) * FX + i, centre, far_sources, far_charge)

    def choose(step, unit):
        return step * (UNITS // 4) + unit // 4, unit % 4 * 4

    def add(step, unit, target, value):
        sums[target] = value if unit % 4 == 0 else sums[target] + value

    list_steps(HERE * 4 // UNITS, choose, far_ids, far_sources, far_charge, far_targets, squares, add)

    def far_store(i, carry):
        far_out[:, pl.ds(pl.multiple_of(i * 128, 128), 128)] = folded(sums, i)
        return carry

    lax.fori_loop(0, HERE // 2, far_store, 0)


def last_kernel(
    device_far, rows, device_skeleton, branch_skeleton, branch_transfer, transfer, basis, near, far, out, coupling
):
    @pl.when(pl.program_id(0) == 0)
    def start():
        top, leaf = lax.axis_index("top"), lax.axis_index("leaf")
        same = lax.broadcasted_iota(jnp.int32, (LEAF, LEAF), 0) == lax.broadcasted_iota(
            jnp.int32, (LEAF, LEAF), 1
        )

        def upright(coords):
            return [
                jnp.sum(jnp.where(same, coords[i : i + 1], 0.0), axis=1, keepdims=True) for i in range(3)
            ]

        def kernel_block(own, other):
            total = 0.0
            for i in range(3):
                differ = own[i] - other[i : i + 1]
                total = total + differ * differ
            scaled = KERNEL_SCALE * jnp.sqrt(total)
            return SIGNAL * (1.0 + scaled) * jnp.exp(-scaled)

        def exact(a, b, dims):
            return lax.dot_general(a, b, dims, precision=EXACT, preferred_element_type=F32)

        def cluster(skeletons, index):
            tile = skeletons[:, pl.ds(pl.multiple_of(index // 2 * 128, 128), 128)]
            return jnp.where(index % 2 == 0, tile, pltpu.roll(tile, LEAF, 1))[:, :LEAF]

        own = upright(cluster(device_skeleton, top * 16 + leaf))
        coupled = jnp.zeros((RHS, LEAF), F32)
        for k in range(4):
            partner = jnp.minimum(jnp.maximum(device_far[k, 0], 0), 127)
            coupled = coupled + exact(rows[partner][:, :LEAF], kernel_block(own, cluster(device_skeleton, partner)), NT)
        own = upright(cluster(branch_skeleton, top))
        field = jnp.zeros((RHS, LEAF), F32)
        for e in range(8):
            total = rows[16 * e]
            for d in range(1, 16):
                total = total + rows[16 * e + d]
            weight = jnp.where(jnp.abs(e - top) >= 2, 1.0, 0.0)
            field = field + exact(total[:, LEAF:] * weight, kernel_block(own, cluster(branch_skeleton, e)), NT)
        coupled = coupled + exact(field, branch_transfer[...], NN)
        coupling[...] = coupled

    lifted = jnp.concatenate(halves(coupling[...]), axis=0)
    half = low_lanes(RHS)
    together = BLOCK // 256

    places, fields = [], []
    for part in range(together):
        place = slice(part * 256, part * 256 + 256)
        t_high, t_low = halves(transfer[:, place])
        up = dot(lifted, t_high) + dot(lifted, t_low)
        places.append(place)
        fields.append(far[:, place] + (up[:RHS] + up[RHS:]))
    products = []
    for place, value in zip(places, fields):
        pieces = []
        for i in range(4):
            tile = value[:, (i // 2) * 128 : (i // 2) * 128 + 128]
            tile = jnp.where(half, tile, 0.0) if i % 2 == 0 else jnp.where(half, 0.0, tile)
            pieces.extend(halves(tile))
        lines = jnp.concatenate(pieces, axis=0)
        b_high, b_low = halves(basis[:, place])
        products.append(
            dot(lines, jnp.concatenate([b_high, b_high], axis=0))
            + dot(lines, jnp.concatenate([b_low, b_low], axis=0))
        )
    for place, product in zip(places, products):
        each = [product[32 * i : 32 * i + 16] + product[32 * i + 16 : 32 * i + 32] for i in range(4)]
        result = jnp.concatenate(
            [
                jnp.where(half, each[0][:, :128], each[1][:, :128]),
                jnp.where(half, each[2][:, 128:], each[3][:, 128:]),
            ],
            axis=1,
        )
        out[:, place] = near[:, place] + result


def block(rows):
    return pl.BlockSpec((rows, BLOCK), lambda i: (0, i))


def shape(*dims, dtype=F32):
    return jax.ShapeDtypeStruct(dims, dtype)


def body(
    points,
    charges,
    near_list,
    far_list,
    leaf_basis,
    transfer,
    leaf_skeleton,
    device_far,
    branch_transfer,
    device_skeleton,
    branch_skeleton,
):
    here = charges.shape[1]

    def moved(array, axis, up):
        size = lax.axis_size(axis)
        pairs = [(i, i + 1) for i in range(size - 1)]
        return lax.ppermute(array, axis, pairs if up else [(j, i) for i, j in pairs])

    coef, device_row, near_ids, far_ids, work, send_down, send_up = pl.pallas_call(
        first_kernel,
        grid=(here // BLOCK,),
        in_specs=[VMEM] * 4 + [block(RANK)] * 2 + [VMEM] * 2,
        out_specs=[VMEM] * 7,
        scratch_shapes=[pltpu.VMEM((2 * RHS, LEAF), F32)],
        out_shape=[
            shape(RHS, here), shape(RHS, 128), shape(32, HERE, dtype=jnp.int32), shape(FAR, HERE, dtype=jnp.int32),
            shape(8, 512, dtype=jnp.int32), shape(RHS, YLANES), shape(RHS, YLANES),
        ],
        compiler_params=room(60),
        name="coefficients",
    )(points, charges, near_list, far_list, leaf_basis, transfer, leaf_skeleton, branch_transfer)
    every_row = lax.all_gather(device_row, ("top", "leaf"), axis=0)
    from_down = moved(send_up, "leaf", True)
    from_up = moved(send_down, "leaf", False)

    def scratch(leaves):
        return [
            pltpu.VMEM((leaves, 32, 128), BF16),
            pltpu.VMEM((leaves, 32, 128), BF16),
            pltpu.VMEM((HERE, LEAF, 32), BF16),
        ]

    common = [pltpu.VMEM((UNITS, LEAF, 4 * LEAF), F32), pltpu.VMEM((HERE, RHS, 128), F32)]

    def cost(us):
        return pl.CostEstimate(flops=us * 10**9, bytes_accessed=10**6, transcendentals=0)

    inner = pl.pallas_call(
        inner_kernel,
        in_specs=[SMEM] * 2 + [VMEM] * 2,
        out_specs=VMEM,
        out_shape=shape(RHS, 4 * COL),
        scratch_shapes=scratch(NEAR_NULL + 1) + common,
        compiler_params=room(16),
        cost_estimate=cost(13),
        name="inner",
    )(near_ids, work, points, charges)
    send_left, send_right = pl.pallas_call(
        side_kernel,
        in_specs=[VMEM] * 6,
        out_specs=[VMEM] * 2,
        out_shape=[shape(RHS, XLANES), shape(RHS, XLANES)],
        compiler_params=room(12),
        name="sides",
    )(points, charges, leaf_skeleton, coef, from_down, from_up)
    from_left = moved(send_right, "top", True)
    from_right = moved(send_left, "top", False)
    strip = pl.pallas_call(
        strip_kernel,
        in_specs=[SMEM] * 2 + [VMEM] * 4,
        out_specs=VMEM,
        out_shape=shape(RHS, 4 * COL),
        scratch_shapes=scratch(NEAR_NULL + 1) + common,
        compiler_params=room(16),
        cost_estimate=cost(13),
        name="strip",
    )(near_ids, work, points, charges, from_down, from_up)
    near, far = pl.pallas_call(
        rest_kernel,
        in_specs=[SMEM] * 3 + [VMEM] * 10,
        out_specs=[VMEM] * 2,
        out_shape=[shape(RHS, here), shape(RHS, here)],
        scratch_shapes=scratch(NEAR_NULL + 1) + scratch(FAR_ALL) + common,
        compiler_params=room(30),
        cost_estimate=cost(55),
        name="rest",
    )(
        near_ids, work, far_ids, points, charges, leaf_skeleton, coef, from_down, from_up, from_left, from_right,
        inner, strip,
    )
    return pl.pallas_call(
        last_kernel,
        grid=(here // BLOCK,),
        in_specs=[SMEM] + [VMEM] * 4 + [block(RANK)] * 2 + [block(RHS)] * 2,
        out_specs=block(RHS),
        scratch_shapes=[pltpu.VMEM((RHS, LEAF), F32)],
        out_shape=shape(RHS, here),
        compiler_params=room(60),
        name="fields",
    )(
        device_far,
        every_row,
        device_skeleton,
        branch_skeleton,
        branch_transfer,
        transfer,
        leaf_basis,
        near,
        far,
    )


def solution(mesh):
    split = P(None, ("top", "leaf"))
    return jax.shard_map(
        body, mesh=mesh, in_specs=(split,) * 9 + (P(), P()), out_specs=split, check_vma=False
    )
```

time: 131 us -> 117 us (0.89)
  Pallas kernels: 94.9 us -> 82.3 us
    pallas_call x1, Pallas kernels: 52.3 us -> 45 us  [body(): pl.pallas_call(rest_kernel, in_specs=[SMEM] * 3 + [VMEM] * 10, out_specs=...]
    pallas_call x1, Pallas kernels: 3.07 us -> 0.17 us  [body(): pl.pallas_call(side_kernel, in_specs=[VMEM] * 6, out_specs=[VMEM] * 2, ou...]
    pallas_call x1, Pallas kernels: 12.2 us -> 9.85 us  [body(): pl.pallas_call(strip_kernel, in_specs=[SMEM] * 2 + [VMEM] * 4, out_specs=...]
    reshape x4 -> x0, local copies, waits for them, and re-layouts: 1.7 us -> none  [the longest x2 1.02 us: body(): device_skeleton.reshape(3, -1, LEAF).transpose(1, 0, 2)]
    unnamed x15 -> x25, local copies, waits for them, and re-layouts: 2.48 us -> 3.78 us
  transfers between devices with their start and end apart: 5 -> 5, of which waited for: 2 -> 2; matrix products, arithmetic and copies ran while one was open for 2% -> 1% of each run, Pallas kernels for 60% -> 55%
where the time goes in v3:
time: 117 us; the launch traced here: 116 us
  Pallas kernels  82.3 us (70%)
  between operations  13.5 us (12%)
  starting transfers between devices  12 us (10%)
  waiting for transfers between devices  4.53 us (4%)
  local copies, waits for them, and re-layouts  3.78 us (3%)
    pallas_call x1, Pallas kernels, body(): pl.pallas_call(rest_kernel, in_specs=[SMEM] * 3 + [VMEM] * 10, out_specs=...  45 us
    ppermute x4, starting transfers between devices, moved(): lax.ppermute(array, axis, pairs if up else [(j, i) for i, j in pairs])  12 us
    pallas_call x1, Pallas kernels, body(): pl.pallas_call(strip_kernel, in_specs=[SMEM] * 2 + [VMEM] * 4, out_specs=...  9.85 us
    pallas_call x1, Pallas kernels, body(): pl.pallas_call(inner_kernel, in_specs=[SMEM] * 2 + [VMEM] * 2, out_specs=...  9.32 us
    pallas_call x1, Pallas kernels, body(): pl.pallas_call(last_kernel, grid=(here // BLOCK,), in_specs=[SMEM] + [VME...  9.3 us
    pallas_call x1, Pallas kernels, body(): pl.pallas_call(first_kernel, grid=(here // BLOCK,), in_specs=[VMEM] * 4 +...  8.68 us
    ppermute x4, waiting for transfers between devices, moved(): lax.ppermute(array, axis, pairs if up else [(j, i) for i, j in pairs])  4.51 us
    unnamed x25, local copies, waits for them, and re-layouts  3.78 us
  transfers between devices with their start and end apart: 5, of which 2 were waited for; matrix products, arithmetic and copies ran while one was open for 1% of the time, Pallas kernels for 55%

profile of v3, /device:TPU:107, one launch (start us, length us, event | category | flops | bytes accessed | tf_op | source)
XLA Modules:
  0.0 116.1 jit_solution(1900633051155437579)
XLA Ops:
  6.5 0.0 all-gather.3.cloned.1.call-start
  6.5 8.7 %coefficients.1 = (f32[16,8192]{1,0:T(8,128)}, f32[16,128]{1,0:T(8,128)}, s32[32,128]{1,0:T(8,128)}, s32[16,128]{1,0:T(8,128)}, s32[8,512]{1,0:T(8,128)}, /*index=5*/f32[16,7680]{1,0:T(8,128)}, f32[16,7680]{1,0:T(8,128)}) custom-call(f32[3,8192]{1,0:T(4,128)} %points.9, f32[16,8192]{1,0:T(8,128)} %charges.9, s32[27,128]{1,0:T(8,128)} %near_list.1, ...), custom_call_target="tpu_custom_call" | custom-call | tf_op jit(solution)/shard_map/coefficients/pallas_call | solution.py:539
  15.2 1.9 %collective-permute-start = (f32[16,7680]{1,0:T(8,128)}, f32[16,7680]{1,0:T(8,128)S(1)}, u32[]{:S(2)}, u32[]{:S(2)}) collective-permute-start(f32[16,7680]{1,0:T(8,128)} %get-tuple-element.21), channel_id=1, source_target_pairs={{0,1},{1,2},{2,3},{3,4},{4,5},{5,6},{6,7},{7,8},{8,9},{9,10},{10,1... | collective-permute-start | bytes 1474568 | tf_op jit(solution)/shard_map/ppermute | solution.py:537
  17.1 3.4 %collective-permute-start.1 = (f32[16,7680]{1,0:T(8,128)}, f32[16,7680]{1,0:T(8,128)S(1)}, u32[]{:S(2)}, u32[]{:S(2)}) collective-permute-start(f32[16,7680]{1,0:T(8,128)} %get-tuple-element.22), channel_id=1, source_target_pairs={{1,0},{2,1},{3,2},{4,3},{5,4},{6,5},{7,6},{8,7},{9,8},{10,9},{11,1... | collective-permute-start | bytes 1474568 | tf_op jit(solution)/shard_map/ppermute | solution.py:537
  20.5 0.0 all-gather.3.cloned.1.call-update
  20.5 0.0 copy-done.3
  20.5 0.0 copy-done
  20.6 0.0 copy-start.6
  20.6 0.7 copy-done.6
  21.3 0.7 copy-done.8
  22.0 9.3 %inner.1 = f32[16,2048]{1,0:T(8,128)S(1)} custom-call(s32[32,128]{1,0:T(8,128)S(1)} %copy-done.6, s32[8,512]{1,0:T(8,128)S(1)} %copy-done.8, f32[3,8192]{1,0:T(4,128)S(1)} %copy-done.3, f32[16,8192]{1,0:T(8,128)S(1)} %copy-done), custom_call_target="tpu_custom_call" | custom-call | flops 12999999488 | bytes 1000000 | tf_op jit(solution)/shard_map/inner/pallas_call | solution.py:568
  31.3 0.0 copy-done.11
  31.3 0.0 copy-start.7
  31.3 0.0 copy-start.9
  31.4 0.7 copy.12.device_far
  32.0 0.0 collective-permute-done.from_down
  32.0 1.2 %collective-permute-done.1.from_up = f32[16,7680]{1,0:T(8,128)S(1)} collective-permute-done((f32[16,7680]{1,0:T(8,128)}, f32[16,7680]{1,0:T(8,128)S(1)}, u32[]{:S(2)}, u32[]{:S(2)}) %collective-permute-start.1) | collective-permute-done | bytes 491552 | tf_op jit(solution)/shard_map/ppermute | solution.py:537
  33.2 0.0 copy-done.4
  33.2 0.2 sides.1
  33.4 4.8 %collective-permute-start.2 = (f32[16,14336]{1,0:T(8,128)S(1)}, f32[16,14336]{1,0:T(8,128)S(1)}, u32[]{:S(2)}, u32[]{:S(2)}) collective-permute-start(f32[16,14336]{1,0:T(8,128)S(1)} %get-tuple-element.23), channel_id=1, source_target_pairs={{0,16},{16,32},{32,48},{48,64},{64,80},{80,96},{96,112},{1,17},{17... | collective-permute-start | bytes 2752520 | tf_op jit(solution)/shard_map/ppermute | solution.py:537
  38.2 0.0 copy-start.10
  38.2 1.9 %collective-permute-start.3 = (f32[16,14336]{1,0:T(8,128)S(1)}, f32[16,14336]{1,0:T(8,128)S(1)}, u32[]{:S(2)}, u32[]{:S(2)}) collective-permute-start(f32[16,14336]{1,0:T(8,128)S(1)} %get-tuple-element.24), channel_id=1, source_target_pairs={{16,0},{32,16},{48,32},{64,48},{80,64},{96,80},{112,96},{17,1},{33... | collective-permute-start | bytes 2752520 | tf_op jit(solution)/shard_map/ppermute | solution.py:537
  40.1 0.0 copy-done.7
  40.1 0.0 copy-done.9
  40.1 9.9 %strip.1 = f32[16,2048]{1,0:T(8,128)S(1)} custom-call(s32[32,128]{1,0:T(8,128)S(1)} %copy-done.7, s32[8,512]{1,0:T(8,128)S(1)} %copy-done.9, f32[3,8192]{1,0:T(4,128)S(1)} %copy-done.3, f32[16,8192]{1,0:T(8,128)S(1)} %copy-done, f32[16,7680]{1,0:T(8,128)S(1)} %collective-permute-done.from_down, f32[16,7680]{1,0:T(8,128)S(1)} %collective-permute-done.1.from_up), custom_call_target="tpu_custom_call" | custom-call | flops 12999999488 | bytes 1000000 | tf_op jit(solution)/shard_map/strip/pallas_call | solution.py:588
  50.0 0.0 collective-permute-done.2.from_left
  50.0 3.3 %collective-permute-done.3.from_right = f32[16,14336]{1,0:T(8,128)S(1)} collective-permute-done((f32[16,14336]{1,0:T(8,128)S(1)}, f32[16,14336]{1,0:T(8,128)S(1)}, u32[]{:S(2)}, u32[]{:S(2)}) %collective-permute-start.3) | collective-permute-done | bytes 917536 | tf_op jit(solution)/shard_map/ppermute | solution.py:537
  53.3 45.0 %rest.1 = (f32[16,8192]{1,0:T(8,128)S(1)}, f32[16,8192]{1,0:T(8,128)S(1)}) custom-call(s32[32,128]{1,0:T(8,128)S(1)} %copy-done.7, s32[8,512]{1,0:T(8,128)S(1)} %copy-done.9, s32[16,128]{1,0:T(8,128)S(1)} %copy-done.10, f32[3,8192]{1,0:T(4,128)S(1)} %copy-done.3, f32[16,8192]{1,0:T(8,128)S(1)} %copy-done, f32[3,8192]{1,0:T(4,128)S(1)} %copy-done.4, ...), custom_call_target="tpu_custom_call" | custom-call | flops 54999998464 | bytes 1000000 | tf_op jit(solution)/shard_map/rest/pallas_call | solution.py:598
  98.3 0.0 copy-start.1
  98.3 0.9 copy-done.1
  99.2 0.8 copy-done.2
  100.0 9.3 %fields.1 = f32[16,8192]{1,0:T(8,128)} custom-call(s32[4,1]{1,0:T(4,128)} %copy.12.device_far, f32[128,16,128]{2,1,0:T(8,128)} %bitcast.1, f32[3,8192]{1,0:T(4,128)} %device_skeleton.1, f32[3,512]{1,0:T(4,128)} %branch_skeleton.1, f32[64,64]{1,0:T(8,128)} %branch_transfer.3, f32[64,8192]{1,0:T(8,128)} %transfer.3, f32[64,8192]{1,0:T(8,128)} %basis.3, ...), custom_call_target="tpu_custom_call" | custom-call | tf_op jit(solution)/shard_map/fields/pallas_call | solution.py:611
  (10 shorter events, 0.0 us)
Async XLA Ops:
  6.5 14.0 %copy-start.3 = (f32[3,8192]{1,0:T(4,128)S(1)}, f32[3,8192]{1,0:T(4,128)}, u32[]{:S(2)}) copy-start(f32[3,8192]{1,0:T(4,128)} %points.9) | copy-start | bytes 294916
  6.5 14.0 %copy-start = (f32[16,8192]{1,0:T(8,128)S(1)}, f32[16,8192]{1,0:T(8,128)}, u32[]{:S(2)}) copy-start(f32[16,8192]{1,0:T(8,128)} %charges.9) | copy-start | bytes 1572868
  6.5 93.5 %all-gather.3.cloned.1.call-start = ((), (), s32[]{:S(2)}) async-start(), calls=%async_computation | async-start | bytes 1056768 | tf_op jit(solution)/shard_map/all_gather | solution.py:552
  15.2 16.8 %collective-permute-start = (f32[16,7680]{1,0:T(8,128)}, f32[16,7680]{1,0:T(8,128)S(1)}, u32[]{:S(2)}, u32[]{:S(2)}) collective-permute-start(f32[16,7680]{1,0:T(8,128)} %get-tuple-element.21), channel_id=1, source_target_pairs={{0,1},{1,2},{2,3},{3,4},{4,5},{5,6},{6,7},{7,8},{8,9},{9,10},{10,1... | collective-permute-start | bytes 1474568 | tf_op jit(solution)/shard_map/ppermute | solution.py:537
  17.1 16.1 %collective-permute-start.1 = (f32[16,7680]{1,0:T(8,128)}, f32[16,7680]{1,0:T(8,128)S(1)}, u32[]{:S(2)}, u32[]{:S(2)}) collective-permute-start(f32[16,7680]{1,0:T(8,128)} %get-tuple-element.22), channel_id=1, source_target_pairs={{1,0},{2,1},{3,2},{4,3},{5,4},{6,5},{7,6},{8,7},{9,8},{10,9},{11,1... | collective-permute-start | bytes 1474568 | tf_op jit(solution)/shard_map/ppermute | solution.py:537
  20.6 0.7 copy-start.6
  21.3 0.7 copy-start.8
  22.0 9.3 %copy-start.11 = (s32[4,1]{0,1:T(1,128)S(1)}, s32[4,1]{0,1:T(1,128)}, u32[]{:S(2)}) copy-start(s32[4,1]{0,1:T(1,128)} %param.18) | copy-start | bytes 52
  22.0 11.2 %copy-start.4 = (f32[3,8192]{1,0:T(4,128)S(1)}, f32[3,8192]{1,0:T(4,128)}, u32[]{:S(2)}) copy-start(f32[3,8192]{1,0:T(4,128)} %skeleton.5) | copy-start | bytes 294916
  22.0 11.2 %copy-start.5 = (f32[16,8192]{1,0:T(8,128)S(1)}, f32[16,8192]{1,0:T(8,128)}, u32[]{:S(2)}) copy-start(f32[16,8192]{1,0:T(8,128)} %get-tuple-element.20.coef) | copy-start | bytes 1572868
  31.3 8.8 %copy-start.7 = (s32[32,128]{1,0:T(8,128)S(1)}, s32[32,128]{1,0:T(8,128)}, u32[]{:S(2)}) copy-start(s32[32,128]{1,0:T(8,128)} %get-tuple-element.17.near_ids) | copy-start | bytes 49156
  31.3 8.8 %copy-start.9 = (s32[8,512]{1,0:T(8,128)S(1)}, s32[8,512]{1,0:T(8,128)}, u32[]{:S(2)}) copy-start(s32[8,512]{1,0:T(8,128)} %get-tuple-element.18.work) | copy-start | bytes 49156
  33.4 16.6 %collective-permute-start.2 = (f32[16,14336]{1,0:T(8,128)S(1)}, f32[16,14336]{1,0:T(8,128)S(1)}, u32[]{:S(2)}, u32[]{:S(2)}) collective-permute-start(f32[16,14336]{1,0:T(8,128)S(1)} %get-tuple-element.23), channel_id=1, source_target_pairs={{0,16},{16,32},{32,48},{48,64},{64,80},{80,96},{96,112},{1,17},{17... | collective-permute-start | bytes 2752520 | tf_op jit(solution)/shard_map/ppermute | solution.py:537
  38.2 15.1 %copy-start.10 = (s32[16,128]{1,0:T(8,128)S(1)}, s32[16,128]{1,0:T(8,128)}, u32[]{:S(2)}) copy-start(s32[16,128]{1,0:T(8,128)} %get-tuple-element.19.far_ids) | copy-start | bytes 24580
  38.2 15.1 %collective-permute-start.3 = (f32[16,14336]{1,0:T(8,128)S(1)}, f32[16,14336]{1,0:T(8,128)S(1)}, u32[]{:S(2)}, u32[]{:S(2)}) collective-permute-start(f32[16,14336]{1,0:T(8,128)S(1)} %get-tuple-element.24), channel_id=1, source_target_pairs={{16,0},{32,16},{48,32},{64,48},{80,64},{96,80},{112,96},{17,1},{33... | collective-permute-start | bytes 2752520 | tf_op jit(solution)/shard_map/ppermute | solution.py:537
  98.3 0.9 copy-start.1
  99.2 0.8 copy-start.2
Sparse Core Ops, SparseCore 0:
  20.7 62.1 all-gather.2

commit v4 on v3

--- a/solution.py
+++ b/solution.py
@@ -27,7 +27,7 @@
 YLANES = (YCOLS + (YCOLS + 3) // 4) * COL
 XLANES = (XCOLS + (XCOLS + 3) // 4) * COL
 UNITS = 32
-BLOCK = 1024
+BLOCK = 2048
 INNER = ((1, 1), (1, 2), (2, 1), (2, 2))
 STRIP = ((1, 0), (1, 3), (2, 0), (2, 3))
 RIM = tuple((x, y) for x in (0, 3) for y in range(4))
@@ -259,24 +259,27 @@
 
 
 def region(array, columns, first, count, to, centre, sources, charge):
-    def step(half, carry):
-        for odd in range(2):
-            i = 2 * half + odd
-            coords = coords_at(array, columns, first + i, odd)
+    together = 4 if count % 4 == 0 else 2
+
+    def step(index, carry):
+        for part in range(together):
+            i = together * index + part
+            coords = coords_at(array, columns, first + i, part % 2)
             build_column(coords, array[:, column(first + i)], centre, to(i), sources, charge)
         return carry
 
-    lax.fori_loop(0, count // 2, step, 0)
+    lax.fori_loop(0, count // together, step, 0)
 
 
 def own_columns(coords, values, to, centre, sources, charge):
-    def step(half, carry):
-        for i in (2 * half, 2 * half + 1):
+    def step(index, carry):
+        for part in range(4):
+            i = 4 * index + part
             at = column(i)
             build_column(coords[:, at], values[:, at], centre, to(i), sources, charge)
         return carry
 
-    lax.fori_loop(0, COLS // 2, step, 0)
+    lax.fori_loop(0, COLS // 4, step, 0)
 
 
 def gathered(array, ids, slot, target):
@@ -292,18 +295,18 @@
     return jnp.concatenate(halves(decay + scaled * decay), axis=0)
 
 
-def list_steps(steps, choose, ids, sources, charge, targets, squares, add):
+def list_steps(steps, units, choose, ids, sources, charge, targets, squares, add):
     def distances(step, unit):
         target, slot = choose(step, unit)
         squares[unit] = dot(targets[target], gathered(sources, ids, slot, target))
 
-    for unit in range(UNITS):
+    for unit in range(units):
         distances(0, unit)
 
     def run(step, carry):
         waiting = None
-        for unit in range(UNITS + 1):
-            if unit < UNITS:
+        for unit in range(units + 1):
+            if unit < units:
                 entries = entries_of(squares[unit])
                 distances(jnp.minimum(step + 1, steps - 1), unit)
             if waiting is not None:
@@ -337,7 +340,7 @@
         sums[target] = sums[target] + value
 
     steps = jnp.maximum((work[4 + phase, 0] + UNITS - 1) // UNITS, 1)
-    list_steps(steps, choose, near_ids, sources, charge, targets, squares, add)
+    list_steps(steps, UNITS, choose, near_ids, sources, charge, targets, squares, add)
 
 
 def folded(sums, pair):
@@ -372,19 +375,32 @@
 
 
 def strip_kernel(
-    near_ids, work, points, charges, from_down, from_up, out, sources, charge, targets, squares, sums
+    near_ids, work, points, charges, skeleton, coef, from_down, from_up,
+    out, far_sources, far_charge, far_targets,
+    sources, charge, targets, squares, sums,
 ):
     centre = centre_of()
     near_own(points, charges, centre, sources, charge)
     near_sides(from_down, from_up, centre, sources, charge)
     near_pass(1, STRIP, near_ids, work, points, centre, sources, charge, targets, squares, sums)
     near_store(STRIP, out, range(4), sums, charges)
+    own_columns(skeleton, coef, lambda i: i, centre, far_sources, far_charge)
+    region(from_down, YCOLS, 0, YFAR, lambda i: COLS + i, centre, far_sources, far_charge)
+    region(from_up, YCOLS, 0, YFAR, lambda i: COLS + YFAR + i, centre, far_sources, far_charge)
+
+    def target_step(i, carry):
+        for part in range(2):
+            col = 2 * i + part
+            build_targets(skeleton[:, column(col)], centre, far_targets, col * BZ)
+        return carry
+
+    lax.fori_loop(0, COLS // 2, target_step, 0)
 
 
 def rest_kernel(
-    near_ids, work, far_ids, points, charges, skeleton, coef, from_down, from_up, from_left, from_right,
-    inner, strip, near_out, far_out,
-    sources, charge, targets, far_sources, far_charge, far_targets, squares, sums,
+    near_ids, work, far_ids, points, charges, from_down, from_up, from_left, from_right,
+    inner, strip, early_sources, early_charge, far_targets, near_out, far_out,
+    sources, charge, targets, far_sources, far_charge, squares, sums,
 ):
     centre = centre_of()
     near_own(points, charges, centre, sources, charge)
@@ -397,27 +413,29 @@
         for i, (x, y) in enumerate(cells):
             near_out[:, column(x * BY + y)] = done[:, i * COL : i * COL + COL]
 
-    own_columns(
-        skeleton, coef, lambda i: (i // BY + 2) * FX + i % BY + 2, centre, far_sources, far_charge
-    )
-
-    def target_step(i, carry):
-        build_targets(skeleton[:, column(i)], centre, far_targets, i * BZ)
-        return carry
-
-    lax.fori_loop(0, COLS, target_step, 0)
-    region(from_down, YCOLS, 0, YFAR, lambda i: (i // 2 + 2) * FX + i % 2, centre, far_sources, far_charge)
-    region(from_up, YCOLS, 0, YFAR, lambda i: (i // 2 + 2) * FX + i % 2 + BY + 2, centre, far_sources, far_charge)
+    def place(first, count, to):
+        def step(i, carry):
+            for leaf in range(BZ):
+                at, source = to(i) * BZ + leaf, (first + i) * BZ + leaf
+                far_sources[at] = early_sources[source]
+                far_charge[at] = early_charge[source]
+            return carry
+
+        lax.fori_loop(0, count, step, 0)
+
+    place(0, COLS, lambda i: (i // BY + 2) * FX + i % BY + 2)
+    place(COLS, YFAR, lambda i: (i // 2 + 2) * FX + i % 2)
+    place(COLS + YFAR, YFAR, lambda i: (i // 2 + 2) * FX + i % 2 + BY + 2)
     region(from_left, XCOLS, 0, XFAR, lambda i: i, centre, far_sources, far_charge)
     region(from_right, XCOLS, 0, XFAR, lambda i: (BX + 2) * FX + i, centre, far_sources, far_charge)
 
     def choose(step, unit):
-        return step * (UNITS // 4) + unit // 4, unit % 4 * 4
+        return step * 16 + unit // 4, unit % 4 * 4
 
     def add(step, unit, target, value):
         sums[target] = value if unit % 4 == 0 else sums[target] + value
 
-    list_steps(HERE * 4 // UNITS, choose, far_ids, far_sources, far_charge, far_targets, squares, add)
+    list_steps(HERE * 4 // 64, 64, choose, far_ids, far_sources, far_charge, far_targets, squares, add)
 
     def far_store(i, carry):
         far_out[:, pl.ds(pl.multiple_of(i * 128, 128), 128)] = folded(sums, i)
@@ -560,7 +578,7 @@
             pltpu.VMEM((HERE, LEAF, 32), BF16),
         ]
 
-    common = [pltpu.VMEM((UNITS, LEAF, 4 * LEAF), F32), pltpu.VMEM((HERE, RHS, 128), F32)]
+    common = [pltpu.VMEM((64, LEAF, 4 * LEAF), F32), pltpu.VMEM((HERE, RHS, 128), F32)]
 
     def cost(us):
         return pl.CostEstimate(flops=us * 10**9, bytes_accessed=10**6, transcendentals=0)
@@ -585,28 +603,32 @@
     )(points, charges, leaf_skeleton, coef, from_down, from_up)
     from_left = moved(send_right, "top", True)
     from_right = moved(send_left, "top", False)
-    strip = pl.pallas_call(
+    early = (COLS + 2 * YFAR) * BZ
+    strip, early_sources, early_charge, far_targets = pl.pallas_call(
         strip_kernel,
-        in_specs=[SMEM] * 2 + [VMEM] * 4,
-        out_specs=VMEM,
-        out_shape=shape(RHS, 4 * COL),
+        in_specs=[SMEM] * 2 + [VMEM] * 6,
+        out_specs=[VMEM] * 4,
+        out_shape=[
+            shape(RHS, 4 * COL), shape(early, 32, 128, dtype=BF16), shape(early, 32, 128, dtype=BF16),
+            shape(HERE, LEAF, 32, dtype=BF16),
+        ],
         scratch_shapes=scratch(NEAR_NULL + 1) + common,
-        compiler_params=room(16),
-        cost_estimate=cost(13),
+        compiler_params=room(26),
+        cost_estimate=cost(15),
         name="strip",
-    )(near_ids, work, points, charges, from_down, from_up)
+    )(near_ids, work, points, charges, leaf_skeleton, coef, from_down, from_up)
     near, far = pl.pallas_call(
         rest_kernel,
-        in_specs=[SMEM] * 3 + [VMEM] * 10,
+        in_specs=[SMEM] * 3 + [VMEM] * 11,
         out_specs=[VMEM] * 2,
         out_shape=[shape(RHS, here), shape(RHS, here)],
-        scratch_shapes=scratch(NEAR_NULL + 1) + scratch(FAR_ALL) + common,
-        compiler_params=room(30),
+        scratch_shapes=scratch(NEAR_NULL + 1) + scratch(FAR_ALL)[:2] + common,
+        compiler_params=room(34),
         cost_estimate=cost(55),
         name="rest",
     )(
-        near_ids, work, far_ids, points, charges, leaf_skeleton, coef, from_down, from_up, from_left, from_right,
-        inner, strip,
+        near_ids, work, far_ids, points, charges, from_down, from_up, from_left, from_right,
+        inner, strip, early_sources, early_charge, far_targets,
     )
     return pl.pallas_call(
         last_kernel,

time: 117 us -> 107 us (0.915)
  Pallas kernels: 82.3 us -> 73.8 us
    pallas_call x2, Pallas kernels: 54.8 us -> 51.7 us  [the longest x1 39.6 us: body(): pl.pallas_call(rest_kernel, in_specs=[SMEM] * 3 + [VMEM] * 11, out_specs=...]
    pallas_call x1, Pallas kernels: 9.3 us -> 7.2 us  [body(): pl.pallas_call(last_kernel, grid=(here // BLOCK,), in_specs=[SMEM] + [VME...]
    pallas_call x1, Pallas kernels: 8.68 us -> 6.63 us  [body(): pl.pallas_call(first_kernel, grid=(here // BLOCK,), in_specs=[VMEM] * 4 +...]
    pallas_call x1, Pallas kernels: 9.32 us -> 8.07 us  [body(): pl.pallas_call(inner_kernel, in_specs=[SMEM] * 2 + [VMEM] * 2, out_specs=...]
  transfers between devices with their start and end apart: 5 -> 5, of which waited for: 2 -> 2; matrix products, arithmetic and copies ran while one was open for 1% -> 1% of each run, Pallas kernels for 55% -> 56%
where the time goes in v4:
time: 107 us
  Pallas kernels  73.8 us (69%)
  between operations  13.5 us (13%)
  starting transfers between devices  12.2 us (11%)
  local copies, waits for them, and re-layouts  3.78 us (4%)
  waiting for transfers between devices  3.39 us (3%)
    pallas_call x1, Pallas kernels, body(): pl.pallas_call(rest_kernel, in_specs=[SMEM] * 3 + [VMEM] * 11, out_specs=...  39.6 us
    ppermute x4, starting transfers between devices, moved(): lax.ppermute(array, axis, pairs if up else [(j, i) for i, j in pairs])  12.2 us
    pallas_call x1, Pallas kernels, body(): pl.pallas_call(strip_kernel, in_specs=[SMEM] * 2 + [VMEM] * 6, out_specs=...  12 us
    pallas_call x1, Pallas kernels, body(): pl.pallas_call(inner_kernel, in_specs=[SMEM] * 2 + [VMEM] * 2, out_specs=...  8.07 us
    pallas_call x1, Pallas kernels, body(): pl.pallas_call(last_kernel, grid=(here // BLOCK,), in_specs=[SMEM] + [VME...  7.2 us
    pallas_call x1, Pallas kernels, body(): pl.pallas_call(first_kernel, grid=(here // BLOCK,), in_specs=[VMEM] * 4 +...  6.63 us
    unnamed x25, local copies, waits for them, and re-layouts  3.78 us
    ppermute x4, waiting for transfers between devices, moved(): lax.ppermute(array, axis, pairs if up else [(j, i) for i, j in pairs])  3.37 us
  transfers between devices with their start and end apart: 5, of which 2 were waited for; matrix products, arithmetic and copies ran while one was open for 1% of the time, Pallas kernels for 56%

profile of v4, /device:TPU:107, one launch (start us, length us, event | category | flops | bytes accessed | tf_op | source)
XLA Modules:
  0.0 106.6 jit_solution(2310789303921911517)
XLA Ops:
  6.5 0.0 all-gather.3.cloned.1.call-start
  6.5 6.6 %coefficients.1 = (f32[16,8192]{1,0:T(8,128)}, f32[16,128]{1,0:T(8,128)}, s32[32,128]{1,0:T(8,128)}, s32[16,128]{1,0:T(8,128)}, s32[8,512]{1,0:T(8,128)}, /*index=5*/f32[16,7680]{1,0:T(8,128)}, f32[16,7680]{1,0:T(8,128)}) custom-call(f32[3,8192]{1,0:T(4,128)} %points.9, f32[16,8192]{1,0:T(8,128)} %charges.9, s32[27,128]{1,0:T(8,128)} %near_list.1, ...), custom_call_target="tpu_custom_call" | custom-call | tf_op jit(solution)/shard_map/coefficients/pallas_call | solution.py:557
  13.2 1.9 %collective-permute-start = (f32[16,7680]{1,0:T(8,128)}, f32[16,7680]{1,0:T(8,128)S(1)}, u32[]{:S(2)}, u32[]{:S(2)}) collective-permute-start(f32[16,7680]{1,0:T(8,128)} %get-tuple-element.24), channel_id=1, source_target_pairs={{0,1},{1,2},{2,3},{3,4},{4,5},{5,6},{6,7},{7,8},{8,9},{9,10},{10,1... | collective-permute-start | bytes 1474568 | tf_op jit(solution)/shard_map/ppermute | solution.py:555
  15.1 3.4 %collective-permute-start.1 = (f32[16,7680]{1,0:T(8,128)}, f32[16,7680]{1,0:T(8,128)S(1)}, u32[]{:S(2)}, u32[]{:S(2)}) collective-permute-start(f32[16,7680]{1,0:T(8,128)} %get-tuple-element.25), channel_id=1, source_target_pairs={{1,0},{2,1},{3,2},{4,3},{5,4},{6,5},{7,6},{8,7},{9,8},{10,9},{11,1... | collective-permute-start | bytes 1474568 | tf_op jit(solution)/shard_map/ppermute | solution.py:555
  18.5 0.0 all-gather.3.cloned.1.call-update
  18.5 0.0 copy-done.4
  18.5 0.0 copy-done
  18.5 0.0 copy-start.6
  18.5 0.7 copy-done.6
  19.2 0.7 copy-done.8
  19.9 8.1 %inner.1 = f32[16,2048]{1,0:T(8,128)S(1)} custom-call(s32[32,128]{1,0:T(8,128)S(1)} %copy-done.6, s32[8,512]{1,0:T(8,128)S(1)} %copy-done.8, f32[3,8192]{1,0:T(4,128)S(1)} %copy-done.4, f32[16,8192]{1,0:T(8,128)S(1)} %copy-done), custom_call_target="tpu_custom_call" | custom-call | flops 12999999488 | bytes 1000000 | tf_op jit(solution)/shard_map/inner/pallas_call | solution.py:586
  28.0 0.0 copy-done.11
  28.0 0.0 copy-start.7
  28.0 0.0 copy-start.9
  28.1 0.7 copy.12.device_far
  28.7 0.0 collective-permute-done.from_down
  28.7 2.4 %collective-permute-done.1.from_up = f32[16,7680]{1,0:T(8,128)S(1)} collective-permute-done((f32[16,7680]{1,0:T(8,128)}, f32[16,7680]{1,0:T(8,128)S(1)}, u32[]{:S(2)}, u32[]{:S(2)}) %collective-permute-start.1) | collective-permute-done | bytes 491552 | tf_op jit(solution)/shard_map/ppermute | solution.py:555
  31.2 0.0 copy-done.3
  31.2 0.0 copy-done.5
  31.2 0.2 sides.1
  31.3 4.8 %collective-permute-start.2 = (f32[16,14336]{1,0:T(8,128)S(1)}, f32[16,14336]{1,0:T(8,128)S(1)}, u32[]{:S(2)}, u32[]{:S(2)}) collective-permute-start(f32[16,14336]{1,0:T(8,128)S(1)} %get-tuple-element.27), channel_id=1, source_target_pairs={{0,16},{16,32},{32,48},{48,64},{64,80},{80,96},{96,112},{1,17},{17... | collective-permute-start | bytes 2752520 | tf_op jit(solution)/shard_map/ppermute | solution.py:555
  36.1 2.1 %collective-permute-start.3 = (f32[16,14336]{1,0:T(8,128)S(1)}, f32[16,14336]{1,0:T(8,128)S(1)}, u32[]{:S(2)}, u32[]{:S(2)}) collective-permute-start(f32[16,14336]{1,0:T(8,128)S(1)} %get-tuple-element.28), channel_id=1, source_target_pairs={{16,0},{32,16},{48,32},{64,48},{80,64},{96,80},{112,96},{17,1},{33... | collective-permute-start | bytes 2752520 | tf_op jit(solution)/shard_map/ppermute | solution.py:555
  38.3 0.0 copy-done.7
  38.3 0.0 copy-done.9
  38.3 12.0 %strip.1 = (f32[16,2048]{1,0:T(8,128)S(1)}, bf16[256,32,128]{2,1,0:T(8,128)(2,1)S(1)}, bf16[256,32,128]{2,1,0:T(8,128)(2,1)S(1)}, bf16[128,64,32]{2,1,0:T(8,128)(2,1)S(1)}) custom-call(s32[32,128]{1,0:T(8,128)S(1)} %copy-done.7, s32[8,512]{1,0:T(8,128)S(1)} %copy-done.9, f32[3,8192]{1,0:T(4,128)S(1)} %copy-done.4, f32[16,8192]{1,0:T(8,128)S(1)} %copy-done, ...), custom_call_target="tpu_custom_call" | custom-call | flops 15000000512 | bytes 1000000 | tf_op jit(solution)/shard_map/strip/pallas_call | solution.py:607
  50.3 0.0 collective-permute-done.2.from_left
  50.3 0.9 collective-permute-done.3.from_right
  51.3 0.0 copy-done.10
  51.3 39.6 %rest.1 = (f32[16,8192]{1,0:T(8,128)S(1)}, f32[16,8192]{1,0:T(8,128)S(1)}) custom-call(s32[32,128]{1,0:T(8,128)S(1)} %copy-done.7, s32[8,512]{1,0:T(8,128)S(1)} %copy-done.9, s32[16,128]{1,0:T(8,128)S(1)} %copy-done.10, f32[3,8192]{1,0:T(4,128)S(1)} %copy-done.4, f32[16,8192]{1,0:T(8,128)S(1)} %copy-done, f32[16,7680]{1,0:T(8,128)S(1)} %collective-permute-done.from_down, ...), custom_call_target="tpu_custom_call" | custom-call | flops 54999998464 | bytes 1000000 | tf_op jit(solution)/shard_map/rest/pallas_call | solution.py:620
  90.9 0.8 copy-done.1
  91.8 0.8 copy-done.2
  92.6 7.2 %fields.1 = f32[16,8192]{1,0:T(8,128)} custom-call(s32[4,1]{1,0:T(4,128)} %copy.12.device_far, f32[128,16,128]{2,1,0:T(8,128)} %bitcast.1, f32[3,8192]{1,0:T(4,128)} %device_skeleton.1, f32[3,512]{1,0:T(4,128)} %branch_skeleton.1, f32[64,64]{1,0:T(8,128)} %branch_transfer.3, f32[64,8192]{1,0:T(8,128)} %transfer.3, f32[64,8192]{1,0:T(8,128)} %basis.3, ...), custom_call_target="tpu_custom_call" | custom-call | tf_op jit(solution)/shard_map/fields/pallas_call | solution.py:633
  (10 shorter events, 0.0 us)
Async XLA Ops:
  6.5 12.0 %copy-start.4 = (f32[3,8192]{1,0:T(4,128)S(1)}, f32[3,8192]{1,0:T(4,128)}, u32[]{:S(2)}) copy-start(f32[3,8192]{1,0:T(4,128)} %points.9) | copy-start | bytes 294916
  6.5 12.0 %copy-start = (f32[16,8192]{1,0:T(8,128)S(1)}, f32[16,8192]{1,0:T(8,128)}, u32[]{:S(2)}) copy-start(f32[16,8192]{1,0:T(8,128)} %charges.9) | copy-start | bytes 1572868
  6.5 86.0 %all-gather.3.cloned.1.call-start = ((), (), s32[]{:S(2)}) async-start(), calls=%async_computation | async-start | bytes 1056768 | tf_op jit(solution)/shard_map/all_gather | solution.py:570
  13.2 15.5 %collective-permute-start = (f32[16,7680]{1,0:T(8,128)}, f32[16,7680]{1,0:T(8,128)S(1)}, u32[]{:S(2)}, u32[]{:S(2)}) collective-permute-start(f32[16,7680]{1,0:T(8,128)} %get-tuple-element.24), channel_id=1, source_target_pairs={{0,1},{1,2},{2,3},{3,4},{4,5},{5,6},{6,7},{7,8},{8,9},{9,10},{10,1... | collective-permute-start | bytes 1474568 | tf_op jit(solution)/shard_map/ppermute | solution.py:555
  15.1 16.1 %collective-permute-start.1 = (f32[16,7680]{1,0:T(8,128)}, f32[16,7680]{1,0:T(8,128)S(1)}, u32[]{:S(2)}, u32[]{:S(2)}) collective-permute-start(f32[16,7680]{1,0:T(8,128)} %get-tuple-element.25), channel_id=1, source_target_pairs={{1,0},{2,1},{3,2},{4,3},{5,4},{6,5},{7,6},{8,7},{9,8},{10,9},{11,1... | collective-permute-start | bytes 1474568 | tf_op jit(solution)/shard_map/ppermute | solution.py:555
  18.5 0.7 copy-start.6
  19.2 0.7 copy-start.8
  19.9 8.1 %copy-start.11 = (s32[4,1]{0,1:T(1,128)S(1)}, s32[4,1]{0,1:T(1,128)}, u32[]{:S(2)}) copy-start(s32[4,1]{0,1:T(1,128)} %param.18) | copy-start | bytes 52
  19.9 11.2 %copy-start.3 = (f32[3,8192]{1,0:T(4,128)S(1)}, f32[3,8192]{1,0:T(4,128)}, u32[]{:S(2)}) copy-start(f32[3,8192]{1,0:T(4,128)} %skeleton.5) | copy-start | bytes 294916
  19.9 11.2 %copy-start.5 = (f32[16,8192]{1,0:T(8,128)S(1)}, f32[16,8192]{1,0:T(8,128)}, u32[]{:S(2)}) copy-start(f32[16,8192]{1,0:T(8,128)} %get-tuple-element.26.coef) | copy-start | bytes 1572868
  28.0 10.2 %copy-start.7 = (s32[32,128]{1,0:T(8,128)S(1)}, s32[32,128]{1,0:T(8,128)}, u32[]{:S(2)}) copy-start(s32[32,128]{1,0:T(8,128)} %get-tuple-element.21.near_ids) | copy-start | bytes 49156
  28.0 10.2 %copy-start.9 = (s32[8,512]{1,0:T(8,128)S(1)}, s32[8,512]{1,0:T(8,128)}, u32[]{:S(2)}) copy-start(s32[8,512]{1,0:T(8,128)} %get-tuple-element.22.work) | copy-start | bytes 49156
  31.3 19.0 %collective-permute-start.2 = (f32[16,14336]{1,0:T(8,128)S(1)}, f32[16,14336]{1,0:T(8,128)S(1)}, u32[]{:S(2)}, u32[]{:S(2)}) collective-permute-start(f32[16,14336]{1,0:T(8,128)S(1)} %get-tuple-element.27), channel_id=1, source_target_pairs={{0,16},{16,32},{32,48},{48,64},{64,80},{80,96},{96,112},{1,17},{17... | collective-permute-start | bytes 2752520 | tf_op jit(solution)/shard_map/ppermute | solution.py:555
  36.1 15.1 %copy-start.10 = (s32[16,128]{1,0:T(8,128)S(1)}, s32[16,128]{1,0:T(8,128)}, u32[]{:S(2)}) copy-start(s32[16,128]{1,0:T(8,128)} %get-tuple-element.23.far_ids) | copy-start | bytes 24580
  36.1 15.1 %collective-permute-start.3 = (f32[16,14336]{1,0:T(8,128)S(1)}, f32[16,14336]{1,0:T(8,128)S(1)}, u32[]{:S(2)}, u32[]{:S(2)}) collective-permute-start(f32[16,14336]{1,0:T(8,128)S(1)} %get-tuple-element.28), channel_id=1, source_target_pairs={{16,0},{32,16},{48,32},{64,48},{80,64},{96,80},{112,96},{17,1},{33... | collective-permute-start | bytes 2752520 | tf_op jit(solution)/shard_map/ppermute | solution.py:555
  90.9 0.9 copy-start.1
  91.8 0.8 copy-start.2
Sparse Core Ops, SparseCore 0:
  18.6 62.2 all-gather.2

commit v5 on v4

--- a/solution.py
+++ b/solution.py
@@ -16,6 +16,7 @@
 HERE = COLS * BZ
 NEAR = 27
 FAR = 16
+FAR_ROW, WORK_ROW, COUNT_ROW = 32, 48, 60
 NX = BX + 2
 FX = BX + 4
 NEAR_NULL = NX * NX * BZ
@@ -27,7 +28,7 @@
 YLANES = (YCOLS + (YCOLS + 3) // 4) * COL
 XLANES = (XCOLS + (XCOLS + 3) // 4) * COL
 UNITS = 32
-BLOCK = 2048
+BLOCK = 4096
 INNER = ((1, 1), (1, 2), (2, 1), (2, 2))
 STRIP = ((1, 0), (1, 3), (2, 0), (2, 3))
 RIM = tuple((x, y) for x in (0, 3) for y in range(4))
@@ -84,7 +85,7 @@
     return jnp.where(ids >= 0, place, null)
 
 
-def work_lists(used, work):
+def work_lists(used, table):
     lane = lax.broadcasted_iota(jnp.int32, (1, HERE), 1)
     inner_x = (((lane >> 5) + 1) & 2) != 0
     inner_y = ((((lane >> 3) & 3) + 1) & 2) != 0
@@ -101,13 +102,17 @@
         leaf = jnp.sum(jnp.where(passed, 1, 0), axis=0, keepdims=True)
         start = jnp.sum(jnp.where(passed, count, 0), axis=0, keepdims=True)
         code = leaf * 8 + (place[:1] - start)
-        work[phase : phase + 1] = jnp.where(leaf < HERE, code, 7)
-        work[4 + phase : 5 + phase] = jnp.zeros((1, 512), jnp.int32) + jnp.sum(kept, axis=1, keepdims=True)
+        code = jnp.where(leaf < HERE, code, 7)
+        for part in range(4):
+            row = WORK_ROW + 4 * phase + part
+            table[row : row + 1] = code[:, part * 128 : part * 128 + 128]
+        row = COUNT_ROW + phase
+        table[row : row + 1] = jnp.zeros((1, 128), jnp.int32) + jnp.sum(kept, axis=1, keepdims=True)
 
 
 def first_kernel(
     points, charges, near_list, far_list, basis, transfer, skeleton, branch_transfer,
-    coef, device_row, near_ids, far_ids, work, send_down, send_up, total,
+    coef, device_row, table, send_down, send_up, total,
 ):
     lane = lax.broadcasted_iota(jnp.int32, (2 * RHS, 4 * LEAF), 1) // LEAF
     half = low_lanes(RHS)
@@ -149,10 +154,11 @@
     def finish():
         top, leaf = lax.axis_index("top"), lax.axis_index("leaf")
         listed = near_list[...]
-        near_ids[0:NEAR] = window_ids(listed, 1, NX, top, leaf, NEAR_NULL)
-        near_ids[NEAR:32] = jnp.full((5, HERE), NEAR_NULL, jnp.int32)
-        work_lists(jnp.sum((listed >= 0).astype(jnp.int32), axis=0, keepdims=True), work)
-        far_ids[...] = window_ids(far_list[...], 2, FX, top, leaf, 0)
+        table[0:NEAR] = window_ids(listed, 1, NX, top, leaf, NEAR_NULL)
+        table[NEAR:32] = jnp.full((5, HERE), NEAR_NULL, jnp.int32)
+        table[COUNT_ROW:64] = jnp.zeros((64 - COUNT_ROW, HERE), jnp.int32)
+        work_lists(jnp.sum((listed >= 0).astype(jnp.int32), axis=0, keepdims=True), table)
+        table[FAR_ROW : FAR_ROW + FAR] = window_ids(far_list[...], 2, FX, top, leaf, 0)
 
         own = total[0:RHS] + total[RHS : 2 * RHS]
         raised = lax.dot_general(own, branch_transfer[...], NT, precision=EXACT, preferred_element_type=F32)
@@ -319,7 +325,7 @@
     lax.fori_loop(0, steps, run, 0)
 
 
-def near_pass(phase, cells, near_ids, work, points, centre, sources, charge, targets, squares, sums):
+def near_pass(phase, cells, table, points, centre, sources, charge, targets, squares, sums):
     for x, y in cells:
         col = x * BY + y
         build_targets(points[:, col * COL : col * COL + COL], centre, targets, col * BZ)
@@ -333,14 +339,15 @@
     charge[NEAR_NULL] = jnp.zeros((32, 128), BF16)
 
     def choose(step, unit):
-        code = work[phase, step * UNITS + unit]
+        place = step * UNITS + unit
+        code = table[WORK_ROW + 4 * phase + (place >> 7), place & 127]
         return code >> 3, (code & 7) * 4
 
     def add(step, unit, target, value):
         sums[target] = sums[target] + value
 
-    steps = jnp.maximum((work[4 + phase, 0] + UNITS - 1) // UNITS, 1)
-    list_steps(steps, UNITS, choose, near_ids, sources, charge, targets, squares, add)
+    steps = jnp.maximum((table[COUNT_ROW + phase, 0] + UNITS - 1) // UNITS, 1)
+    list_steps(steps, UNITS, choose, table, sources, charge, targets, squares, add)
 
 
 def folded(sums, pair):
@@ -367,22 +374,22 @@
     region(from_up, YCOLS, YFAR, YNEAR, lambda i: (i + 1) * NX + NX - 1, centre, sources, charge)
 
 
-def inner_kernel(near_ids, work, points, charges, out, sources, charge, targets, squares, sums):
+def inner_kernel(table, points, charges, out, sources, charge, targets, squares, sums):
     centre = centre_of()
     near_own(points, charges, centre, sources, charge)
-    near_pass(0, INNER, near_ids, work, points, centre, sources, charge, targets, squares, sums)
+    near_pass(0, INNER, table, points, centre, sources, charge, targets, squares, sums)
     near_store(INNER, out, range(4), sums, charges)
 
 
 def strip_kernel(
-    near_ids, work, points, charges, skeleton, coef, from_down, from_up,
-    out, far_sources, far_charge, far_targets,
-    sources, charge, targets, squares, sums,
+    table, points, charges, skeleton, coef, from_down, from_up,
+    out, far_sources, far_charge, far_targets, sources, charge,
+    targets, squares, sums,
 ):
     centre = centre_of()
     near_own(points, charges, centre, sources, charge)
     near_sides(from_down, from_up, centre, sources, charge)
-    near_pass(1, STRIP, near_ids, work, points, centre, sources, charge, targets, squares, sums)
+    near_pass(1, STRIP, table, points, centre, sources, charge, targets, squares, sums)
     near_store(STRIP, out, range(4), sums, charges)
     own_columns(skeleton, coef, lambda i: i, centre, far_sources, far_charge)
     region(from_down, YCOLS, 0, YFAR, lambda i: COLS + i, centre, far_sources, far_charge)
@@ -398,16 +405,22 @@
 
 
 def rest_kernel(
-    near_ids, work, far_ids, points, charges, from_down, from_up, from_left, from_right,
-    inner, strip, early_sources, early_charge, far_targets, near_out, far_out,
+    table, points, charges, from_down, from_up, from_left, from_right,
+    inner, strip, early_sources, early_charge, far_targets, near_sources, near_charge, near_out, far_out,
     sources, charge, targets, far_sources, far_charge, squares, sums,
 ):
     centre = centre_of()
-    near_own(points, charges, centre, sources, charge)
-    near_sides(from_down, from_up, centre, sources, charge)
+    def keep(i, carry):
+        for leaf in range(BZ):
+            at = NX * BZ + i * BZ + leaf
+            sources[at] = near_sources[at]
+            charge[at] = near_charge[at]
+        return carry
+
+    lax.fori_loop(0, BX * NX, keep, 0)
     region(from_left, XCOLS, XFAR, XNEAR, lambda i: i, centre, sources, charge)
     region(from_right, XCOLS, XFAR, XNEAR, lambda i: (NX - 1) * NX + i, centre, sources, charge)
-    near_pass(2, RIM, near_ids, work, points, centre, sources, charge, targets, squares, sums)
+    near_pass(2, RIM, table, points, centre, sources, charge, targets, squares, sums)
     near_store(RIM, near_out, [x * BY + y for x, y in RIM], sums, charges)
     for cells, done in ((INNER, inner), (STRIP, strip)):
         for i, (x, y) in enumerate(cells):
@@ -430,12 +443,12 @@
     region(from_right, XCOLS, 0, XFAR, lambda i: (BX + 2) * FX + i, centre, far_sources, far_charge)
 
     def choose(step, unit):
-        return step * 16 + unit // 4, unit % 4 * 4
+        return step * 16 + unit // 4, FAR_ROW + unit % 4 * 4
 
     def add(step, unit, target, value):
         sums[target] = value if unit % 4 == 0 else sums[target] + value
 
-    list_steps(HERE * 4 // 64, 64, choose, far_ids, far_sources, far_charge, far_targets, squares, add)
+    list_steps(HERE * 4 // 64, 64, choose, table, far_sources, far_charge, far_targets, squares, add)
 
     def far_store(i, carry):
         far_out[:, pl.ds(pl.multiple_of(i * 128, 128), 128)] = folded(sums, i)
@@ -554,15 +567,14 @@
         pairs = [(i, i + 1) for i in range(size - 1)]
         return lax.ppermute(array, axis, pairs if up else [(j, i) for i, j in pairs])
 
-    coef, device_row, near_ids, far_ids, work, send_down, send_up = pl.pallas_call(
+    coef, device_row, table, send_down, send_up = pl.pallas_call(
         first_kernel,
         grid=(here // BLOCK,),
         in_specs=[VMEM] * 4 + [block(RANK)] * 2 + [VMEM] * 2,
-        out_specs=[VMEM] * 7,
+        out_specs=[VMEM] * 5,
         scratch_shapes=[pltpu.VMEM((2 * RHS, LEAF), F32)],
         out_shape=[
-            shape(RHS, here), shape(RHS, 128), shape(32, HERE, dtype=jnp.int32), shape(FAR, HERE, dtype=jnp.int32),
-            shape(8, 512, dtype=jnp.int32), shape(RHS, YLANES), shape(RHS, YLANES),
+            shape(RHS, here), shape(RHS, 128), shape(64, HERE, dtype=jnp.int32), shape(RHS, YLANES), shape(RHS, YLANES),
         ],
         compiler_params=room(60),
         name="coefficients",
@@ -585,14 +597,14 @@
 
     inner = pl.pallas_call(
         inner_kernel,
-        in_specs=[SMEM] * 2 + [VMEM] * 2,
+        in_specs=[SMEM] + [VMEM] * 2,
         out_specs=VMEM,
         out_shape=shape(RHS, 4 * COL),
         scratch_shapes=scratch(NEAR_NULL + 1) + common,
         compiler_params=room(16),
         cost_estimate=cost(13),
         name="inner",
-    )(near_ids, work, points, charges)
+    )(table, points, charges)
     send_left, send_right = pl.pallas_call(
         side_kernel,
         in_specs=[VMEM] * 6,
@@ -604,31 +616,32 @@
     from_left = moved(send_right, "top", True)
     from_right = moved(send_left, "top", False)
     early = (COLS + 2 * YFAR) * BZ
-    strip, early_sources, early_charge, far_targets = pl.pallas_call(
+    strip, early_sources, early_charge, far_targets, near_sources, near_charge = pl.pallas_call(
         strip_kernel,
-        in_specs=[SMEM] * 2 + [VMEM] * 6,
-        out_specs=[VMEM] * 4,
+        in_specs=[SMEM] + [VMEM] * 6,
+        out_specs=[VMEM] * 6,
         out_shape=[
             shape(RHS, 4 * COL), shape(early, 32, 128, dtype=BF16), shape(early, 32, 128, dtype=BF16),
-            shape(HERE, LEAF, 32, dtype=BF16),
+            shape(HERE, LEAF, 32, dtype=BF16), shape(NEAR_NULL + 1, 32, 128, dtype=BF16),
+            shape(NEAR_NULL + 1, 32, 128, dtype=BF16),
         ],
-        scratch_shapes=scratch(NEAR_NULL + 1) + common,
-        compiler_params=room(26),
+        scratch_shapes=scratch(NEAR_NULL + 1)[2:] + common,
+        compiler_params=room(28),
         cost_estimate=cost(15),
         name="strip",
-    )(near_ids, work, points, charges, leaf_skeleton, coef, from_down, from_up)
+    )(table, points, charges, leaf_skeleton, coef, from_down, from_up)
     near, far = pl.pallas_call(
         rest_kernel,
-        in_specs=[SMEM] * 3 + [VMEM] * 11,
+        in_specs=[SMEM] + [VMEM] * 13,
         out_specs=[VMEM] * 2,
         out_shape=[shape(RHS, here), shape(RHS, here)],
         scratch_shapes=scratch(NEAR_NULL + 1) + scratch(FAR_ALL)[:2] + common,
-        compiler_params=room(34),
+        compiler_params=room(38),
         cost_estimate=cost(55),
         name="rest",
     )(
-        near_ids, work, far_ids, points, charges, from_down, from_up, from_left, from_right,
-        inner, strip, early_sources, early_charge, far_targets,
+        table, points, charges, from_down, from_up, from_left, from_right,
+        inner, strip, early_sources, early_charge, far_targets, near_sources, near_charge,
     )
     return pl.pallas_call(
         last_kernel,

time: 107 us -> 105 us (0.981)
  Pallas kernels: 73.8 us -> 72.1 us
    unnamed x25 -> x19, local copies, waits for them, and re-layouts: 3.78 us -> 3.16 us
where the time goes in v5:
time: 105 us
  Pallas kernels  72.1 us (69%)
  between operations  13.5 us (13%)
  starting transfers between devices  12.2 us (12%)
  waiting for transfers between devices  4.07 us (4%)
  local copies, waits for them, and re-layouts  3.16 us (3%)
    pallas_call x1, Pallas kernels, body(): pl.pallas_call(rest_kernel, in_specs=[SMEM] + [VMEM] * 13, out_specs=[VME...  38.8 us
    ppermute x4, starting transfers between devices, moved(): lax.ppermute(array, axis, pairs if up else [(j, i) for i, j in pairs])  12.2 us
    pallas_call x1, Pallas kernels, body(): pl.pallas_call(strip_kernel, in_specs=[SMEM] + [VMEM] * 6, out_specs=[VME...  12 us
    pallas_call x1, Pallas kernels, body(): pl.pallas_call(inner_kernel, in_specs=[SMEM] + [VMEM] * 2, out_specs=VMEM...  8.09 us
    pallas_call x1, Pallas kernels, body(): pl.pallas_call(last_kernel, grid=(here // BLOCK,), in_specs=[SMEM] + [VME...  6.63 us
    pallas_call x1, Pallas kernels, body(): pl.pallas_call(first_kernel, grid=(here // BLOCK,), in_specs=[VMEM] * 4 +...  6.33 us
    ppermute x4, waiting for transfers between devices, moved(): lax.ppermute(array, axis, pairs if up else [(j, i) for i, j in pairs])  4.05 us
    unnamed x19, local copies, waits for them, and re-layouts  3.16 us
  transfers between devices with their start and end apart: 5, of which 2 were waited for; matrix products, arithmetic and copies ran while one was open for 1% of the time, Pallas kernels for 56%

profile of v5, /device:TPU:107, one launch (start us, length us, event | category | flops | bytes accessed | tf_op | source)
XLA Modules:
  0.0 105.0 jit_solution(14308351599418023221)
XLA Ops:
  6.5 0.0 copy-start.4
  6.5 0.0 copy-start
  6.5 0.0 all-gather.3.cloned.1.call-start
  6.5 6.3 %coefficients.1 = (f32[16,8192]{1,0:T(8,128)}, f32[16,128]{1,0:T(8,128)}, s32[64,128]{1,0:T(8,128)}, f32[16,7680]{1,0:T(8,128)}, f32[16,7680]{1,0:T(8,128)}) custom-call(f32[3,8192]{1,0:T(4,128)} %points.9, f32[16,8192]{1,0:T(8,128)} %charges.9, s32[27,128]{1,0:T(8,128)} %near_list.1, s32[16,128]{1,0:T(8,128)} %far_list.1, f32[64,8192]{1,0:T(8,128)} %basis.3, ...), custom_call_target="tpu_custom_call" | custom-call | tf_op jit(solution)/shard_map/coefficients/pallas_call | solution.py:570
  12.9 1.9 %collective-permute-start = (f32[16,7680]{1,0:T(8,128)}, f32[16,7680]{1,0:T(8,128)S(1)}, u32[]{:S(2)}, u32[]{:S(2)}) collective-permute-start(f32[16,7680]{1,0:T(8,128)} %get-tuple-element.22), channel_id=1, source_target_pairs={{0,1},{1,2},{2,3},{3,4},{4,5},{5,6},{6,7},{7,8},{8,9},{9,10},{10,1... | collective-permute-start | bytes 1474568 | tf_op jit(solution)/shard_map/ppermute | solution.py:568
  14.8 3.4 %collective-permute-start.1 = (f32[16,7680]{1,0:T(8,128)}, f32[16,7680]{1,0:T(8,128)S(1)}, u32[]{:S(2)}, u32[]{:S(2)}) collective-permute-start(f32[16,7680]{1,0:T(8,128)} %get-tuple-element.23), channel_id=1, source_target_pairs={{1,0},{2,1},{3,2},{4,3},{5,4},{6,5},{7,6},{8,7},{9,8},{10,9},{11,1... | collective-permute-start | bytes 1474568 | tf_op jit(solution)/shard_map/ppermute | solution.py:568
  18.2 0.0 all-gather.3.cloned.1.call-update
  18.2 0.0 copy-done.4
  18.2 0.0 copy-done
  18.2 0.0 copy-start.6
  18.2 0.7 copy-done.6
  19.0 0.0 copy-start.8
  19.0 8.1 %inner.1 = f32[16,2048]{1,0:T(8,128)S(1)} custom-call(s32[64,128]{1,0:T(8,128)S(1)} %copy-done.6, f32[3,8192]{1,0:T(4,128)S(1)} %copy-done.4, f32[16,8192]{1,0:T(8,128)S(1)} %copy-done), custom_call_target="tpu_custom_call" | custom-call | flops 12999999488 | bytes 1000000 | tf_op jit(solution)/shard_map/inner/pallas_call | solution.py:598
  27.1 0.0 copy-done.8
  27.1 0.0 copy-start.7
  27.1 0.7 copy.12.device_far
  27.8 0.0 collective-permute-done.from_down
  27.8 3.1 %collective-permute-done.1.from_up = f32[16,7680]{1,0:T(8,128)S(1)} collective-permute-done((f32[16,7680]{1,0:T(8,128)}, f32[16,7680]{1,0:T(8,128)S(1)}, u32[]{:S(2)}, u32[]{:S(2)}) %collective-permute-start.1) | collective-permute-done | bytes 491552 | tf_op jit(solution)/shard_map/ppermute | solution.py:568
  30.9 0.0 copy-done.3
  30.9 0.0 copy-done.5
  30.9 0.2 sides.1
  31.0 4.8 %collective-permute-start.2 = (f32[16,14336]{1,0:T(8,128)S(1)}, f32[16,14336]{1,0:T(8,128)S(1)}, u32[]{:S(2)}, u32[]{:S(2)}) collective-permute-start(f32[16,14336]{1,0:T(8,128)S(1)} %get-tuple-element.25), channel_id=1, source_target_pairs={{0,16},{16,32},{32,48},{48,64},{64,80},{80,96},{96,112},{1,17},{17... | collective-permute-start | bytes 2752520 | tf_op jit(solution)/shard_map/ppermute | solution.py:568
  35.8 2.1 %collective-permute-start.3 = (f32[16,14336]{1,0:T(8,128)S(1)}, f32[16,14336]{1,0:T(8,128)S(1)}, u32[]{:S(2)}, u32[]{:S(2)}) collective-permute-start(f32[16,14336]{1,0:T(8,128)S(1)} %get-tuple-element.26), channel_id=1, source_target_pairs={{16,0},{32,16},{48,32},{64,48},{80,64},{96,80},{112,96},{17,1},{33... | collective-permute-start | bytes 2752520 | tf_op jit(solution)/shard_map/ppermute | solution.py:568
  37.9 0.0 copy-done.7
  37.9 12.0 %strip.1 = (f32[16,2048]{1,0:T(8,128)S(1)}, bf16[256,32,128]{2,1,0:T(8,128)(2,1)S(1)}, bf16[256,32,128]{2,1,0:T(8,128)(2,1)S(1)}, bf16[128,64,32]{2,1,0:T(8,128)...) custom-call(s32[64,128]{1,0:T(8,128)S(1)} %copy-done.7, f32[3,8192]{1,0:T(4,128)S(1)} %copy-done.4, ...), custom_call_target="tpu_custom_call" | custom-call | flops 15000000512 | bytes 1000000 | tf_op jit(solution)/shard_map/strip/pallas_call | solution.py:619
  50.0 0.0 collective-permute-done.2.from_left
  50.0 1.0 collective-permute-done.3.from_right
  50.9 38.8 %rest.1 = (f32[16,8192]{1,0:T(8,128)S(1)}, f32[16,8192]{1,0:T(8,128)S(1)}) custom-call(s32[64,128]{1,0:T(8,128)S(1)} %copy-done.7, f32[3,8192]{1,0:T(4,128)S(1)} %copy-done.4, f32[16,8192]{1,0:T(8,128)S(1)} %copy-done, f32[16,7680]{1,0:T(8,128)S(1)} %collective-permute-done.from_down, f32[16,7680]{1,0:T(8,128)S(1)} %collective-permute-done.1.from_up, ...), custom_call_target="tpu_custom_call" | custom-call | flops 54999998464 | bytes 1000000 | tf_op jit(solution)/shard_map/rest/pallas_call | solution.py:633
  89.8 0.0 copy-start.1
  89.8 0.9 copy-done.1
  90.7 0.8 copy-done.2
  91.5 6.6 %fields.1 = f32[16,8192]{1,0:T(8,128)} custom-call(s32[4,1]{1,0:T(4,128)} %copy.12.device_far, f32[128,16,128]{2,1,0:T(8,128)} %bitcast.1, f32[3,8192]{1,0:T(4,128)} %device_skeleton.1, f32[3,512]{1,0:T(4,128)} %branch_skeleton.1, f32[64,64]{1,0:T(8,128)} %branch_transfer.3, f32[64,8192]{1,0:T(8,128)} %transfer.3, f32[64,8192]{1,0:T(8,128)} %basis.3, ...), custom_call_target="tpu_custom_call" | custom-call | tf_op jit(solution)/shard_map/fields/pallas_call | solution.py:646
  (4 shorter events, 0.0 us)
Async XLA Ops:
  6.5 11.6 %copy-start.4 = (f32[3,8192]{1,0:T(4,128)S(1)}, f32[3,8192]{1,0:T(4,128)}, u32[]{:S(2)}) copy-start(f32[3,8192]{1,0:T(4,128)} %points.9) | copy-start | bytes 294916
  6.5 11.7 %copy-start = (f32[16,8192]{1,0:T(8,128)S(1)}, f32[16,8192]{1,0:T(8,128)}, u32[]{:S(2)}) copy-start(f32[16,8192]{1,0:T(8,128)} %charges.9) | copy-start | bytes 1572868
  6.5 85.0 %all-gather.3.cloned.1.call-start = ((), (), s32[]{:S(2)}) async-start(), calls=%async_computation | async-start | bytes 1056768 | tf_op jit(solution)/shard_map/all_gather | solution.py:582
  12.9 14.9 %collective-permute-start = (f32[16,7680]{1,0:T(8,128)}, f32[16,7680]{1,0:T(8,128)S(1)}, u32[]{:S(2)}, u32[]{:S(2)}) collective-permute-start(f32[16,7680]{1,0:T(8,128)} %get-tuple-element.22), channel_id=1, source_target_pairs={{0,1},{1,2},{2,3},{3,4},{4,5},{5,6},{6,7},{7,8},{8,9},{9,10},{10,1... | collective-permute-start | bytes 1474568 | tf_op jit(solution)/shard_map/ppermute | solution.py:568
  14.8 16.1 %collective-permute-start.1 = (f32[16,7680]{1,0:T(8,128)}, f32[16,7680]{1,0:T(8,128)S(1)}, u32[]{:S(2)}, u32[]{:S(2)}) collective-permute-start(f32[16,7680]{1,0:T(8,128)} %get-tuple-element.23), channel_id=1, source_target_pairs={{1,0},{2,1},{3,2},{4,3},{5,4},{6,5},{7,6},{8,7},{9,8},{10,9},{11,1... | collective-permute-start | bytes 1474568 | tf_op jit(solution)/shard_map/ppermute | solution.py:568
  18.2 0.8 copy-start.6
  19.0 8.1 %copy-start.8 = (s32[4,1]{0,1:T(1,128)S(1)}, s32[4,1]{0,1:T(1,128)}, u32[]{:S(2)}) copy-start(s32[4,1]{0,1:T(1,128)} %param.18) | copy-start | bytes 52
  19.0 11.9 %copy-start.3 = (f32[3,8192]{1,0:T(4,128)S(1)}, f32[3,8192]{1,0:T(4,128)}, u32[]{:S(2)}) copy-start(f32[3,8192]{1,0:T(4,128)} %skeleton.5) | copy-start | bytes 294916
  19.0 11.9 %copy-start.5 = (f32[16,8192]{1,0:T(8,128)S(1)}, f32[16,8192]{1,0:T(8,128)}, u32[]{:S(2)}) copy-start(f32[16,8192]{1,0:T(8,128)} %get-tuple-element.24.coef) | copy-start | bytes 1572868
  27.1 10.9 %copy-start.7 = (s32[64,128]{1,0:T(8,128)S(1)}, s32[64,128]{1,0:T(8,128)}, u32[]{:S(2)}) copy-start(s32[64,128]{1,0:T(8,128)} %get-tuple-element.21.table) | copy-start | bytes 98308
  31.0 18.9 %collective-permute-start.2 = (f32[16,14336]{1,0:T(8,128)S(1)}, f32[16,14336]{1,0:T(8,128)S(1)}, u32[]{:S(2)}, u32[]{:S(2)}) collective-permute-start(f32[16,14336]{1,0:T(8,128)S(1)} %get-tuple-element.25), channel_id=1, source_target_pairs={{0,16},{16,32},{32,48},{48,64},{64,80},{80,96},{96,112},{1,17},{17... | collective-permute-start | bytes 2752520 | tf_op jit(solution)/shard_map/ppermute | solution.py:568
  35.8 15.1 %collective-permute-start.3 = (f32[16,14336]{1,0:T(8,128)S(1)}, f32[16,14336]{1,0:T(8,128)S(1)}, u32[]{:S(2)}, u32[]{:S(2)}) collective-permute-start(f32[16,14336]{1,0:T(8,128)S(1)} %get-tuple-element.26), channel_id=1, source_target_pairs={{16,0},{32,16},{48,32},{64,48},{80,64},{96,80},{112,96},{17,1},{33... | collective-permute-start | bytes 2752520 | tf_op jit(solution)/shard_map/ppermute | solution.py:568
  89.8 0.9 copy-start.1
  90.7 0.8 copy-start.2
Sparse Core Ops, SparseCore 0:
  18.3 62.1 all-gather.2

commit v6 on v5

--- a/solution.py
+++ b/solution.py
@@ -362,7 +362,7 @@
         for pair in range(BZ // 2):
             at = (x * BY + y) * COL + pair * 128
             value = folded(sums, (x * BY + y) * (BZ // 2) + pair)
-            out[:, to * COL + pair * 128 : to * COL + pair * 128 + 128] = value + NUGGET * charges[:, at : at + 128]
+            out[0:RHS, to * COL + pair * 128 : to * COL + pair * 128 + 128] = value + NUGGET * charges[:, at : at + 128]
 
 
 def near_own(points, charges, centre, sources, charge):
@@ -406,7 +406,7 @@
 
 def rest_kernel(
     table, points, charges, from_down, from_up, from_left, from_right,
-    inner, strip, early_sources, early_charge, far_targets, near_sources, near_charge, near_out, far_out,
+    inner, strip, early_sources, early_charge, far_targets, near_sources, near_charge, out,
     sources, charge, targets, far_sources, far_charge, squares, sums,
 ):
     centre = centre_of()
@@ -421,10 +421,10 @@
     region(from_left, XCOLS, XFAR, XNEAR, lambda i: i, centre, sources, charge)
     region(from_right, XCOLS, XFAR, XNEAR, lambda i: (NX - 1) * NX + i, centre, sources, charge)
     near_pass(2, RIM, table, points, centre, sources, charge, targets, squares, sums)
-    near_store(RIM, near_out, [x * BY + y for x, y in RIM], sums, charges)
+    near_store(RIM, out, [x * BY + y for x, y in RIM], sums, charges)
     for cells, done in ((INNER, inner), (STRIP, strip)):
         for i, (x, y) in enumerate(cells):
-            near_out[:, column(x * BY + y)] = done[:, i * COL : i * COL + COL]
+            out[0:RHS, column(x * BY + y)] = done[:, i * COL : i * COL + COL]
 
     def place(first, count, to):
         def step(i, carry):
@@ -451,14 +451,14 @@
     list_steps(HERE * 4 // 64, 64, choose, table, far_sources, far_charge, far_targets, squares, add)
 
     def far_store(i, carry):
-        far_out[:, pl.ds(pl.multiple_of(i * 128, 128), 128)] = folded(sums, i)
+        out[RHS : 2 * RHS, pl.ds(pl.multiple_of(i * 128, 128), 128)] = folded(sums, i)
         return carry
 
     lax.fori_loop(0, HERE // 2, far_store, 0)
 
 
 def last_kernel(
-    device_far, rows, device_skeleton, branch_skeleton, branch_transfer, transfer, basis, near, far, out, coupling
+    device_far, rows, device_skeleton, branch_skeleton, branch_transfer, transfer, basis, near_far, out, coupling
 ):
     @pl.when(pl.program_id(0) == 0)
     def start():
@@ -513,7 +513,7 @@
         t_high, t_low = halves(transfer[:, place])
         up = dot(lifted, t_high) + dot(lifted, t_low)
         places.append(place)
-        fields.append(far[:, place] + (up[:RHS] + up[RHS:]))
+        fields.append(near_far[RHS : 2 * RHS, place] + (up[:RHS] + up[RHS:]))
     products = []
     for place, value in zip(places, fields):
         pieces = []
@@ -536,7 +536,7 @@
             ],
             axis=1,
         )
-        out[:, place] = near[:, place] + result
+        out[:, place] = near_far[0:RHS, place] + result
 
 
 def block(rows):
@@ -630,11 +630,11 @@
         cost_estimate=cost(15),
         name="strip",
     )(table, points, charges, leaf_skeleton, coef, from_down, from_up)
-    near, far = pl.pallas_call(
+    near_far = pl.pallas_call(
         rest_kernel,
         in_specs=[SMEM] + [VMEM] * 13,
-        out_specs=[VMEM] * 2,
-        out_shape=[shape(RHS, here), shape(RHS, here)],
+        out_specs=VMEM,
+        out_shape=shape(2 * RHS, here),
         scratch_shapes=scratch(NEAR_NULL + 1) + scratch(FAR_ALL)[:2] + common,
         compiler_params=room(38),
         cost_estimate=cost(55),
@@ -646,7 +646,7 @@
     return pl.pallas_call(
         last_kernel,
         grid=(here // BLOCK,),
-        in_specs=[SMEM] + [VMEM] * 4 + [block(RANK)] * 2 + [block(RHS)] * 2,
+        in_specs=[SMEM] + [VMEM] * 4 + [block(RANK)] * 2 + [block(2 * RHS)],
         out_specs=block(RHS),
         scratch_shapes=[pltpu.VMEM((RHS, LEAF), F32)],
         out_shape=shape(RHS, here),
@@ -660,8 +660,7 @@
         branch_transfer,
         transfer,
         leaf_basis,
-        near,
-        far,
+        near_far,
     )
 
 

time: 105 us -> 105 us (level)
    unnamed x19 -> x17, local copies, waits for them, and re-layouts: 3.16 us -> 2.5 us
  transfers between devices with their start and end apart: 5 -> 5, of which waited for: 2 -> 2; matrix products, arithmetic and copies ran while one was open for 1% -> 1% of each run, Pallas kernels for 56% -> 57%
where the time goes in v6:
time: 105 us; the launch traced here: 104 us
  Pallas kernels  72 us (69%)
  between operations  13.5 us (13%)
  starting transfers between devices  12.2 us (12%)
  waiting for transfers between devices  4.1 us (4%)
  local copies, waits for them, and re-layouts  2.5 us (2%)
    pallas_call x1, Pallas kernels, body(): pl.pallas_call(rest_kernel, in_specs=[SMEM] + [VMEM] * 13, out_specs=VMEM...  38.8 us
    ppermute x4, starting transfers between devices, moved(): lax.ppermute(array, axis, pairs if up else [(j, i) for i, j in pairs])  12.2 us
    pallas_call x1, Pallas kernels, body(): pl.pallas_call(strip_kernel, in_specs=[SMEM] + [VMEM] * 6, out_specs=[VME...  12 us
    pallas_call x1, Pallas kernels, body(): pl.pallas_call(inner_kernel, in_specs=[SMEM] + [VMEM] * 2, out_specs=VMEM...  8.08 us
    pallas_call x1, Pallas kernels, body(): pl.pallas_call(last_kernel, grid=(here // BLOCK,), in_specs=[SMEM] + [VME...  6.61 us
    pallas_call x1, Pallas kernels, body(): pl.pallas_call(first_kernel, grid=(here // BLOCK,), in_specs=[VMEM] * 4 +...  6.32 us
    ppermute x4, waiting for transfers between devices, moved(): lax.ppermute(array, axis, pairs if up else [(j, i) for i, j in pairs])  4.08 us
    unnamed x17, local copies, waits for them, and re-layouts  2.5 us
  transfers between devices with their start and end apart: 5, of which 2 were waited for; matrix products, arithmetic and copies ran while one was open for 1% of the time, Pallas kernels for 57%

profile of v6, /device:TPU:107, one launch (start us, length us, event | category | flops | bytes accessed | tf_op | source)
XLA Modules:
  0.0 104.3 jit_solution(12785800688086717289)
XLA Ops:
  6.5 0.0 copy-start.3
  6.5 0.0 copy-start
  6.5 0.0 all-gather.3.cloned.1.call-start
  6.5 6.3 %coefficients.1 = (f32[16,8192]{1,0:T(8,128)}, f32[16,128]{1,0:T(8,128)}, s32[64,128]{1,0:T(8,128)}, f32[16,7680]{1,0:T(8,128)}, f32[16,7680]{1,0:T(8,128)}) custom-call(f32[3,8192]{1,0:T(4,128)} %points.9, f32[16,8192]{1,0:T(8,128)} %charges.9, s32[27,128]{1,0:T(8,128)} %near_list.1, s32[16,128]{1,0:T(8,128)} %far_list.1, f32[64,8192]{1,0:T(8,128)} %basis.3, ...), custom_call_target="tpu_custom_call" | custom-call | tf_op jit(solution)/shard_map/coefficients/pallas_call | solution.py:570
  12.9 1.9 %collective-permute-start = (f32[16,7680]{1,0:T(8,128)}, f32[16,7680]{1,0:T(8,128)S(1)}, u32[]{:S(2)}, u32[]{:S(2)}) collective-permute-start(f32[16,7680]{1,0:T(8,128)} %get-tuple-element.20), channel_id=1, source_target_pairs={{0,1},{1,2},{2,3},{3,4},{4,5},{5,6},{6,7},{7,8},{8,9},{9,10},{10,1... | collective-permute-start | bytes 1474568 | tf_op jit(solution)/shard_map/ppermute | solution.py:568
  14.8 3.4 %collective-permute-start.1 = (f32[16,7680]{1,0:T(8,128)}, f32[16,7680]{1,0:T(8,128)S(1)}, u32[]{:S(2)}, u32[]{:S(2)}) collective-permute-start(f32[16,7680]{1,0:T(8,128)} %get-tuple-element.21), channel_id=1, source_target_pairs={{1,0},{2,1},{3,2},{4,3},{5,4},{6,5},{7,6},{8,7},{9,8},{10,9},{11,1... | collective-permute-start | bytes 1474568 | tf_op jit(solution)/shard_map/ppermute | solution.py:568
  18.1 0.0 all-gather.3.cloned.1.call-update
  18.2 0.0 copy-done.3
  18.2 0.0 copy-done
  18.2 0.0 copy-start.5
  18.2 0.7 copy-done.5
  19.0 0.0 copy-start.7
  19.0 0.0 copy-start.2
  19.0 8.1 %inner.1 = f32[16,2048]{1,0:T(8,128)S(1)} custom-call(s32[64,128]{1,0:T(8,128)S(1)} %copy-done.5, f32[3,8192]{1,0:T(4,128)S(1)} %copy-done.3, f32[16,8192]{1,0:T(8,128)S(1)} %copy-done), custom_call_target="tpu_custom_call" | custom-call | flops 12999999488 | bytes 1000000 | tf_op jit(solution)/shard_map/inner/pallas_call | solution.py:598
  27.0 0.0 copy-done.7
  27.1 0.0 copy-start.6
  27.1 0.7 copy.12.device_far
  27.7 0.0 collective-permute-done.from_down
  27.7 3.1 %collective-permute-done.1.from_up = f32[16,7680]{1,0:T(8,128)S(1)} collective-permute-done((f32[16,7680]{1,0:T(8,128)}, f32[16,7680]{1,0:T(8,128)S(1)}, u32[]{:S(2)}, u32[]{:S(2)}) %collective-permute-start.1) | collective-permute-done | bytes 491552 | tf_op jit(solution)/shard_map/ppermute | solution.py:568
  30.9 0.0 copy-done.2
  30.9 0.0 copy-done.4
  30.9 0.2 sides.1
  31.0 4.8 %collective-permute-start.2 = (f32[16,14336]{1,0:T(8,128)S(1)}, f32[16,14336]{1,0:T(8,128)S(1)}, u32[]{:S(2)}, u32[]{:S(2)}) collective-permute-start(f32[16,14336]{1,0:T(8,128)S(1)} %get-tuple-element.23), channel_id=1, source_target_pairs={{0,16},{16,32},{32,48},{48,64},{64,80},{80,96},{96,112},{1,17},{17... | collective-permute-start | bytes 2752520 | tf_op jit(solution)/shard_map/ppermute | solution.py:568
  35.8 2.1 %collective-permute-start.3 = (f32[16,14336]{1,0:T(8,128)S(1)}, f32[16,14336]{1,0:T(8,128)S(1)}, u32[]{:S(2)}, u32[]{:S(2)}) collective-permute-start(f32[16,14336]{1,0:T(8,128)S(1)} %get-tuple-element.24), channel_id=1, source_target_pairs={{16,0},{32,16},{48,32},{64,48},{80,64},{96,80},{112,96},{17,1},{33... | collective-permute-start | bytes 2752520 | tf_op jit(solution)/shard_map/ppermute | solution.py:568
  37.9 0.0 copy-done.6
  37.9 12.0 %strip.1 = (f32[16,2048]{1,0:T(8,128)S(1)}, bf16[256,32,128]{2,1,0:T(8,128)(2,1)S(1)}, bf16[256,32,128]{2,1,0:T(8,128)(2,1)S(1)}, bf16[128,64,32]{2,1,0:T(8,128)...) custom-call(s32[64,128]{1,0:T(8,128)S(1)} %copy-done.6, f32[3,8192]{1,0:T(4,128)S(1)} %copy-done.3, ...), custom_call_target="tpu_custom_call" | custom-call | flops 15000000512 | bytes 1000000 | tf_op jit(solution)/shard_map/strip/pallas_call | solution.py:619
  50.0 0.0 collective-permute-done.2.from_left
  50.0 0.9 collective-permute-done.3.from_right
  50.9 38.8 %rest.1.near_far = f32[32,8192]{1,0:T(8,128)S(1)} custom-call(s32[64,128]{1,0:T(8,128)S(1)} %copy-done.6, f32[3,8192]{1,0:T(4,128)S(1)} %copy-done.3, f32[16,8192]{1,0:T(8,128)S(1)} %copy-done, f32[16,7680]{1,0:T(8,128)S(1)} %collective-permute-done.from_down, f32[16,7680]{1,0:T(8,128)S(1)} %collective-permute-done.1.from_up, ...), custom_call_target="tpu_custom_call" | custom-call | flops 54999998464 | bytes 1000000 | tf_op jit(solution)/shard_map/rest/pallas_call | solution.py:633
  89.8 0.0 copy-start.1
  89.8 1.1 %copy-done.1 = f32[32,8192]{1,0:T(8,128)} copy-done((f32[32,8192]{1,0:T(8,128)}, f32[32,8192]{1,0:T(8,128)S(1)}, u32[]{:S(2)}) %copy-start.1) | copy-done | bytes 1048600
  90.8 6.6 %fields.1 = f32[16,8192]{1,0:T(8,128)} custom-call(s32[4,1]{1,0:T(4,128)} %copy.12.device_far, f32[128,16,128]{2,1,0:T(8,128)} %bitcast.1, f32[3,8192]{1,0:T(4,128)} %device_skeleton.1, f32[3,512]{1,0:T(4,128)} %branch_skeleton.1, f32[64,64]{1,0:T(8,128)} %branch_transfer.3, f32[64,8192]{1,0:T(8,128)} %transfer.3, f32[64,8192]{1,0:T(8,128)} %basis.3, ...), custom_call_target="tpu_custom_call" | custom-call | tf_op jit(solution)/shard_map/fields/pallas_call | solution.py:646
  (2 shorter events, 0.0 us)
Async XLA Ops:
  6.5 11.6 %copy-start.3 = (f32[3,8192]{1,0:T(4,128)S(1)}, f32[3,8192]{1,0:T(4,128)}, u32[]{:S(2)}) copy-start(f32[3,8192]{1,0:T(4,128)} %points.9) | copy-start | bytes 294916
  6.5 11.6 %copy-start = (f32[16,8192]{1,0:T(8,128)S(1)}, f32[16,8192]{1,0:T(8,128)}, u32[]{:S(2)}) copy-start(f32[16,8192]{1,0:T(8,128)} %charges.9) | copy-start | bytes 1572868
  6.5 84.3 %all-gather.3.cloned.1.call-start = ((), (), s32[]{:S(2)}) async-start(), calls=%async_computation | async-start | bytes 1056768 | tf_op jit(solution)/shard_map/all_gather | solution.py:582
  12.9 14.9 %collective-permute-start = (f32[16,7680]{1,0:T(8,128)}, f32[16,7680]{1,0:T(8,128)S(1)}, u32[]{:S(2)}, u32[]{:S(2)}) collective-permute-start(f32[16,7680]{1,0:T(8,128)} %get-tuple-element.20), channel_id=1, source_target_pairs={{0,1},{1,2},{2,3},{3,4},{4,5},{5,6},{6,7},{7,8},{8,9},{9,10},{10,1... | collective-permute-start | bytes 1474568 | tf_op jit(solution)/shard_map/ppermute | solution.py:568
  14.8 16.1 %collective-permute-start.1 = (f32[16,7680]{1,0:T(8,128)}, f32[16,7680]{1,0:T(8,128)S(1)}, u32[]{:S(2)}, u32[]{:S(2)}) collective-permute-start(f32[16,7680]{1,0:T(8,128)} %get-tuple-element.21), channel_id=1, source_target_pairs={{1,0},{2,1},{3,2},{4,3},{5,4},{6,5},{7,6},{8,7},{9,8},{10,9},{11,1... | collective-permute-start | bytes 1474568 | tf_op jit(solution)/shard_map/ppermute | solution.py:568
  18.2 0.8 copy-start.5
  19.0 8.1 %copy-start.7 = (s32[4,1]{0,1:T(1,128)S(1)}, s32[4,1]{0,1:T(1,128)}, u32[]{:S(2)}) copy-start(s32[4,1]{0,1:T(1,128)} %param.18) | copy-start | bytes 52
  19.0 11.9 %copy-start.2 = (f32[3,8192]{1,0:T(4,128)S(1)}, f32[3,8192]{1,0:T(4,128)}, u32[]{:S(2)}) copy-start(f32[3,8192]{1,0:T(4,128)} %skeleton.5) | copy-start | bytes 294916
  19.0 11.9 %copy-start.4 = (f32[16,8192]{1,0:T(8,128)S(1)}, f32[16,8192]{1,0:T(8,128)}, u32[]{:S(2)}) copy-start(f32[16,8192]{1,0:T(8,128)} %get-tuple-element.22.coef) | copy-start | bytes 1572868
  27.1 10.9 %copy-start.6 = (s32[64,128]{1,0:T(8,128)S(1)}, s32[64,128]{1,0:T(8,128)}, u32[]{:S(2)}) copy-start(s32[64,128]{1,0:T(8,128)} %get-tuple-element.19.table) | copy-start | bytes 98308
  31.0 18.9 %collective-permute-start.2 = (f32[16,14336]{1,0:T(8,128)S(1)}, f32[16,14336]{1,0:T(8,128)S(1)}, u32[]{:S(2)}, u32[]{:S(2)}) collective-permute-start(f32[16,14336]{1,0:T(8,128)S(1)} %get-tuple-element.23), channel_id=1, source_target_pairs={{0,16},{16,32},{32,48},{48,64},{64,80},{80,96},{96,112},{1,17},{17... | collective-permute-start | bytes 2752520 | tf_op jit(solution)/shard_map/ppermute | solution.py:568
  35.8 15.1 %collective-permute-start.3 = (f32[16,14336]{1,0:T(8,128)S(1)}, f32[16,14336]{1,0:T(8,128)S(1)}, u32[]{:S(2)}, u32[]{:S(2)}) collective-permute-start(f32[16,14336]{1,0:T(8,128)S(1)} %get-tuple-element.24), channel_id=1, source_target_pairs={{16,0},{32,16},{48,32},{64,48},{80,64},{96,80},{112,96},{17,1},{33... | collective-permute-start | bytes 2752520 | tf_op jit(solution)/shard_map/ppermute | solution.py:568
  89.8 1.1 %copy-start.1 = (f32[32,8192]{1,0:T(8,128)}, f32[32,8192]{1,0:T(8,128)S(1)}, u32[]{:S(2)}) copy-start(f32[32,8192]{1,0:T(8,128)S(1)} %rest.1.near_far) | copy-start | bytes 3145732
Sparse Core Ops, SparseCore 0:
  18.3 62.1 all-gather.2
